TPU v7x, 32 devices: a whole 2x2x4 slice. The times are simulated.
32 devices in a mesh: tm: 2 (over core), lon: 4 (over y, x), head: 4 (over z).
Axes of the slice: x: 2, y: 2, z: 4, core: 2. Of those that a mesh axis runs over, the one named last changes fastest.
Arguments:
- query_rows: bfloat16 [8, 8, 32, 5120], P('tm', None, 'lon', 'head'), may hold values from -16 to 16
- key_rows: bfloat16 [8, 8, 32, 5120], P('tm', None, 'lon', 'head'), may hold values from -16 to 16
- value_rows: bfloat16 [8, 8, 32, 5120], P('tm', None, 'lon', 'head'), may hold values from -6 to 6
- out_grad: bfloat16 [8, 8, 32, 5120], P('tm', None, 'lon', 'head'), may hold values from -6 to 6
- window_offsets: int32 [2, 2, 8], P('tm', None, 'lon'), may hold values from -1 to 1
Outputs:
- attended: bfloat16 [8, 8, 32, 5120], P('tm', None, 'lon', 'head')
- query_grad: bfloat16 [8, 8, 32, 5120], P('tm', None, 'lon', 'head')
- key_grad: bfloat16 [8, 8, 32, 5120], P('tm', None, 'lon', 'head')
- value_grad: bfloat16 [8, 8, 32, 5120], P('tm', None, 'lon', 'head')
All inputs are finite; a program needn't handle non-finite values.
Results may differ from a plain program's by a relative error of at most 0.013.
The roundings to bfloat16 on the way count: a program that leaves them out, or rounds other values in their place, can miss the bound.
Values may be sent and summed in bfloat16 or wider, within the bound.
No kernel may reach another device: no remote copies, remote signals or barrier semaphores. Data moves between devices by JAX's collectives and lax.ppermute only.
A program may use at most 128 MiB of HBM per device.

v0:
```python
import math

import jax
import jax.numpy as jnp
from jax import lax
from jax.sharding import PartitionSpec as P

HD = 128
TILE = 4


def partner(block, axis, distance):
    count = lax.axis_size(axis)
    route = []
    for low in range(count):
        high = low | 1 << distance
        if high != low and high < count:
            route += [(low, high), (high, low)]
    return lax.ppermute(block, axis, route)


def extended(array, sides, width):
    for axis, dim in sides:
        count, length = (lax.axis_size(axis), array.shape[dim])
        up = [(i, (i + 1) % count) for i in range(count)]
        down = [(j, i) for i, j in up]
        last = lax.slice_in_dim(array, length - width, length, axis=dim)
        leading = lax.slice_in_dim(array, 0, width, axis=dim)
        before = lax.ppermute(last, axis, up)
        after = lax.ppermute(leading, axis, down)
        array = jnp.concatenate([before, array, after], axis=dim)
    return array


def passed_along(block, axis, distance):
    devices = range(lax.axis_size(axis))
    route = [((i - distance) % len(devices), i) for i in devices]
    return lax.ppermute(block, axis, route)


def widen_frames(stacked, frame_index):
    depth = stacked.shape[1]
    inward = partner(stacked, "tm", 0)
    joined = jnp.concatenate([inward, stacked, inward], axis=1)
    return lax.dynamic_slice_in_dim(joined, (1 - frame_index) * TILE, depth + TILE, 1)


def widen_lon(stacked):
    return extended(stacked, (("lon", 3),), 2 * TILE)


def return_lon(key_part, value_part):
    rim_cells = 2 * TILE
    low_rim = jnp.stack([key_part[:, :, :rim_cells], value_part[:, :, :rim_cells]])
    high_rim = jnp.stack([key_part[:, :, -rim_cells:], value_part[:, :, -rim_cells:]])
    from_next = passed_along(low_rim.astype(jnp.bfloat16), "lon", -1).astype(low_rim.dtype)
    from_prior = passed_along(high_rim.astype(jnp.bfloat16), "lon", 1).astype(high_rim.dtype)
    inner_key = key_part[:, :, rim_cells:-rim_cells]
    inner_value = value_part[:, :, rim_cells:-rim_cells]
    inner_key = (
        inner_key.at[:, :, -rim_cells:].add(from_next[0]).at[:, :, :rim_cells].add(from_prior[0])
    )
    inner_value = (
        inner_value.at[:, :, -rim_cells:].add(from_next[1]).at[:, :, :rim_cells].add(from_prior[1])
    )
    return (inner_key, inner_value)


def return_frames(key_part, value_part, frame_index):
    depth = key_part.shape[0] - TILE
    send_start = (1 - frame_index) * depth
    outward = jnp.stack(
        [
            lax.dynamic_slice_in_dim(key_part, send_start, TILE, 0),
            lax.dynamic_slice_in_dim(value_part, send_start, TILE, 0),
        ]
    )
    inward = partner(outward.astype(jnp.bfloat16), "tm", 0).astype(outward.dtype)
    own_start = frame_index * TILE
    own_key = lax.dynamic_slice_in_dim(key_part, own_start, depth, 0)
    own_value = lax.dynamic_slice_in_dim(value_part, own_start, depth, 0)
    own_key = own_key + inward[0]
    own_value = own_value + inward[1]
    return (own_key, own_value)


def window_rows(
    window_offsets, frame_index, frame_tiles, lat_tiles, lon_tiles, key_frames, lat_cells, key_lon
):
    group_shape = (frame_tiles, lat_tiles, lon_tiles)
    group_frame = jnp.broadcast_to(jnp.arange(frame_tiles)[:, None, None], group_shape).reshape(-1)
    group_lat = jnp.broadcast_to(jnp.arange(lat_tiles)[None, :, None], group_shape).reshape(-1)
    group_lon = jnp.broadcast_to(jnp.arange(lon_tiles)[None, None, :], group_shape).reshape(-1)
    group_shift = window_offsets.reshape(-1)
    frame_span = jnp.arange(key_frames)
    cell_span = jnp.arange(3 * TILE)
    lat_pos = jnp.clip(group_lat[:, None] * TILE - TILE + cell_span[None, :], 0, lat_cells - 1)
    lon_pos = (group_lon + group_shift + 1)[:, None] * TILE + cell_span[None, :]
    flat_index = (
        frame_span[None, :, None, None] * lat_cells + lat_pos[:, None, :, None]
    ) * key_lon + lon_pos[:, None, None, :]
    group_count = group_frame.shape[0]
    flat_index = flat_index.reshape(group_count, -1)
    key_tile = frame_span // TILE
    query_tile = frame_index * frame_tiles + group_frame
    frame_ok = jnp.abs(key_tile[None, :] - query_tile[:, None]) <= 1
    lat_step = group_lat[:, None] - 1 + cell_span[None, :] // TILE
    lat_ok = (lat_step >= 0) & (lat_step < lat_tiles)
    allowed = frame_ok[:, :, None, None] & lat_ok[:, None, :, None]
    allowed = jnp.broadcast_to(allowed, (group_count, key_frames, 3 * TILE, 3 * TILE)).reshape(
        group_count, -1
    )
    return (flat_index, allowed)


def on_device(query_rows, key_rows, value_rows, out_grad, window_offsets):
    frame_depth, lat_cells, lon_cells, width = query_rows.shape
    head_count = width // HD
    scale = 1.0 / math.sqrt(HD)
    frame_tiles = frame_depth // TILE
    lat_tiles = lat_cells // TILE
    lon_tiles = lon_cells // TILE
    group_count = frame_tiles * lat_tiles * lon_tiles
    frame_index = lax.axis_index("tm")
    stacked = jnp.stack([key_rows, value_rows])
    widened = widen_frames(widen_lon(stacked), frame_index)
    key_frames = widened.shape[1]
    key_lon = widened.shape[3]
    key_flat = widened[0].reshape(-1, width)
    value_flat = widened[1].reshape(-1, width)
    key_count = key_flat.shape[0]
    flat_index, allowed = window_rows(
        window_offsets,
        frame_index,
        frame_tiles,
        lat_tiles,
        lon_tiles,
        key_frames,
        lat_cells,
        key_lon,
    )
    allowed = allowed[:, None, :]
    tile_rows = TILE * TILE * TILE

    def to_groups(array):
        shaped = array.reshape(frame_tiles, TILE, lat_tiles, TILE, lon_tiles, TILE, width)
        return shaped.transpose(0, 2, 4, 1, 3, 5, 6).reshape(group_count, tile_rows, width)

    def from_groups(array):
        shaped = array.reshape(frame_tiles, lat_tiles, lon_tiles, TILE, TILE, TILE, width)
        return shaped.transpose(0, 3, 1, 4, 2, 5, 6).reshape(
            frame_depth, lat_cells, lon_cells, width
        )

    query_groups = to_groups(query_rows)
    grad_groups = to_groups(out_grad)
    index_rows = flat_index.reshape(-1)

    def one_head(head_index, carry):
        attended, query_grad, key_grad, value_grad = carry
        start = head_index * HD
        query_head = lax.dynamic_slice_in_dim(query_groups, start, HD, 2)
        grad_head = lax.dynamic_slice_in_dim(grad_groups, start, HD, 2)
        key_block = jnp.take(lax.dynamic_slice_in_dim(key_flat, start, HD, 1), flat_index, axis=0)
        value_block = jnp.take(
            lax.dynamic_slice_in_dim(value_flat, start, HD, 1), flat_index, axis=0
        )
        scores = (
            jnp.einsum("gqd,gkd->gqk", query_head, key_block, preferred_element_type=jnp.float32)
            * scale
        )
        peak = jnp.max(jnp.where(allowed, scores, -jnp.inf), axis=2, keepdims=True)
        expo = jnp.exp(jnp.where(allowed, scores - peak, -jnp.inf))
        probs = (expo / jnp.sum(expo, axis=2, keepdims=True)).astype(jnp.bfloat16)
        out_head = jnp.einsum(
            "gqk,gkd->gqd", probs, value_block, preferred_element_type=jnp.float32
        ).astype(jnp.bfloat16)
        delta = jnp.sum(
            grad_head.astype(jnp.float32) * out_head.astype(jnp.float32), axis=2, keepdims=True
        )
        dprobs = jnp.einsum(
            "gqd,gkd->gqk", grad_head, value_block, preferred_element_type=jnp.float32
        )
        dscores = (probs.astype(jnp.float32) * (dprobs - delta)).astype(jnp.bfloat16)
        query_head_grad = (
            jnp.einsum("gqk,gkd->gqd", dscores, key_block, preferred_element_type=jnp.float32)
            * scale
        ).astype(jnp.bfloat16)
        key_block_grad = (
            jnp.einsum("gqk,gqd->gkd", dscores, query_head, preferred_element_type=jnp.float32)
            * scale
        )
        value_block_grad = jnp.einsum(
            "gqk,gqd->gkd", probs, grad_head, preferred_element_type=jnp.float32
        )
        empty = jnp.zeros((key_count, HD), jnp.float32)
        key_head_grad = empty.at[index_rows].add(key_block_grad.reshape(-1, HD))
        value_head_grad = empty.at[index_rows].add(value_block_grad.reshape(-1, HD))
        attended = lax.dynamic_update_slice_in_dim(attended, out_head, start, 2)
        query_grad = lax.dynamic_update_slice_in_dim(query_grad, query_head_grad, start, 2)
        key_grad = lax.dynamic_update_slice_in_dim(key_grad, key_head_grad, start, 1)
        value_grad = lax.dynamic_update_slice_in_dim(value_grad, value_head_grad, start, 1)
        return (attended, query_grad, key_grad, value_grad)

    initial = (
        jnp.zeros((group_count, tile_rows, width), jnp.bfloat16),
        jnp.zeros((group_count, tile_rows, width), jnp.bfloat16),
        jnp.zeros((key_count, width), jnp.float32),
        jnp.zeros((key_count, width), jnp.float32),
    )
    attended, query_grad, key_grad, value_grad = lax.fori_loop(0, head_count, one_head, initial)
    grown_shape = (key_frames, lat_cells, key_lon, width)
    key_grad = key_grad.reshape(grown_shape)
    value_grad = value_grad.reshape(grown_shape)
    key_grad, value_grad = return_frames(key_grad, value_grad, frame_index)
    key_grad, value_grad = return_lon(key_grad, value_grad)
    return (
        from_groups(attended),
        from_groups(query_grad),
        key_grad.astype(jnp.bfloat16),
        value_grad.astype(jnp.bfloat16),
    )


def solution(mesh):
    in_specs = (
        P("tm", None, "lon", "head"),
        P("tm", None, "lon", "head"),
        P("tm", None, "lon", "head"),
        P("tm", None, "lon", "head"),
        P("tm", None, "lon"),
    )
    out_specs = (
        P("tm", None, "lon", "head"),
        P("tm", None, "lon", "head"),
        P("tm", None, "lon", "head"),
        P("tm", None, "lon", "head"),
    )
    return jax.shard_map(
        on_device, mesh=mesh, in_specs=in_specs, out_specs=out_specs, check_vma=False
    )
```

profile of v0, /device:TPU:0, one launch (start us, length us, event | category | flops | bytes accessed | tf_op | source)
XLA Modules:
  0.0 1066.1 jit_solution(9203609239147295008)
XLA Ops:
  6.1 29.2 %collective-permute-done.1 = bf16[2,4,8,8,1280]{4,3,2,1,0:T(8,128)(2,1)S(1)} collective-permute-done((bf16[2,4,8,8,1280]{4,3,2,1,0:T(8,128)(2,1)S(1)}, bf16[2,4,8,8,1280]{4,3,2,1,0:T(8,128)(2,1)S(1)}, u32[]{:S(2)}, u32[]{:S(2)}) %collective-permute-start.1) | collective-permute-done | bytes 1310752 | tf_op jit(solution)/shard_map/ppermute | solution.py:30
  35.3 27.9 %collective-permute-done = bf16[2,4,8,8,1280]{4,3,2,1,0:T(8,128)(2,1)S(1)} collective-permute-done((bf16[2,4,8,8,1280]{4,3,2,1,0:T(8,128)(2,1)S(1)}, bf16[2,4,8,8,1280]{4,3,2,1,0:T(8,128)(2,1)S(1)}, u32[]{:S(2)}, u32[]{:S(2)}) %collective-permute-start) | collective-permute-done | bytes 1310752 | tf_op jit(solution)/shard_map/ppermute | solution.py:29
  77.1 6.6 fusion.41
  96.1 875.3 %while.29 = (s32[]{:T(128)}, bf16[4,64,1280]{2,1,0:T(8,128)(2,1)}, bf16[4,64,1280]{2,1,0:T(8,128)(2,1)}, f32[1536,1280]{1,0:T(8,128)}, f32[1536,1280]{1,0:T(8,12...) while((s32[]{:T(128)}, bf16[4,64,1280]{2,1,0:T(8,128)(2,1)}, ...), condition=%wide.region_6.8_spmd.clone.clone, body=%wide.region_0.7_spmd.clone.clone.sunk | while | flops 460652928 | bytes 37832076 | solution.py:211
  99.1 8.8 gather_fusion
  107.9 8.8 gather_fusion.1
  128.3 25.3 %scatter_custom_fusion.15 = f32[1536,128]{1,0:T(8,128)S(1)} fusion(s32[4608]{0:T(1024)S(1)} %fusion.97, f32[4608,128]{1,0:T(8,128)S(1)} %bitcast.95, f32[]{:T(128)} %constant.241.clone.1..sunk), kind=kCustom, calls=%fused_computation.33.clone.1 | custom fusion | flops 589824 | bytes 786436 | tf_op jit(solution)/shard_map/while/body/eval_jaxpr/scatter-add | solution.py:197
  156.7 25.6 %scatter_custom_fusion.14 = f32[1536,128]{1,0:T(8,128)S(1)} fusion(s32[4608]{0:T(1024)S(1)} %fusion.97, f32[4608,128]{1,0:T(8,128)} %bitcast.94, f32[]{:T(128)} %constant.241.clone.1..sunk), kind=kCustom, calls=%fused_computation.31.clone.1 | custom fusion | flops 589824 | bytes 786944 | tf_op jit(solution)/shard_map/while/body/eval_jaxpr/scatter-add | solution.py:198
  186.6 8.8 gather_fusion
  195.4 8.8 gather_fusion.1
  215.8 25.3 %scatter_custom_fusion.15 = f32[1536,128]{1,0:T(8,128)S(1)} fusion(s32[4608]{0:T(1024)S(1)} %fusion.97, f32[4608,128]{1,0:T(8,128)S(1)} %bitcast.95, f32[]{:T(128)} %constant.241.clone.1..sunk), kind=kCustom, calls=%fused_computation.33.clone.1 | custom fusion | flops 589824 | bytes 786436 | tf_op jit(solution)/shard_map/while/body/eval_jaxpr/scatter-add | solution.py:197
  244.2 25.6 %scatter_custom_fusion.14 = f32[1536,128]{1,0:T(8,128)S(1)} fusion(s32[4608]{0:T(1024)S(1)} %fusion.97, f32[4608,128]{1,0:T(8,128)} %bitcast.94, f32[]{:T(128)} %constant.241.clone.1..sunk), kind=kCustom, calls=%fused_computation.31.clone.1 | custom fusion | flops 589824 | bytes 786944 | tf_op jit(solution)/shard_map/while/body/eval_jaxpr/scatter-add | solution.py:198
  274.1 8.8 gather_fusion
  282.9 8.8 gather_fusion.1
  303.3 25.3 %scatter_custom_fusion.15 = f32[1536,128]{1,0:T(8,128)S(1)} fusion(s32[4608]{0:T(1024)S(1)} %fusion.97, f32[4608,128]{1,0:T(8,128)S(1)} %bitcast.95, f32[]{:T(128)} %constant.241.clone.1..sunk), kind=kCustom, calls=%fused_computation.33.clone.1 | custom fusion | flops 589824 | bytes 786436 | tf_op jit(solution)/shard_map/while/body/eval_jaxpr/scatter-add | solution.py:197
  331.7 25.6 %scatter_custom_fusion.14 = f32[1536,128]{1,0:T(8,128)S(1)} fusion(s32[4608]{0:T(1024)S(1)} %fusion.97, f32[4608,128]{1,0:T(8,128)} %bitcast.94, f32[]{:T(128)} %constant.241.clone.1..sunk), kind=kCustom, calls=%fused_computation.31.clone.1 | custom fusion | flops 589824 | bytes 786944 | tf_op jit(solution)/shard_map/while/body/eval_jaxpr/scatter-add | solution.py:198
  361.6 8.8 gather_fusion
  370.4 8.8 gather_fusion.1
  390.8 25.3 %scatter_custom_fusion.15 = f32[1536,128]{1,0:T(8,128)S(1)} fusion(s32[4608]{0:T(1024)S(1)} %fusion.97, f32[4608,128]{1,0:T(8,128)S(1)} %bitcast.95, f32[]{:T(128)} %constant.241.clone.1..sunk), kind=kCustom, calls=%fused_computation.33.clone.1 | custom fusion | flops 589824 | bytes 786436 | tf_op jit(solution)/shard_map/while/body/eval_jaxpr/scatter-add | solution.py:197
  419.2 25.6 %scatter_custom_fusion.14 = f32[1536,128]{1,0:T(8,128)S(1)} fusion(s32[4608]{0:T(1024)S(1)} %fusion.97, f32[4608,128]{1,0:T(8,128)} %bitcast.94, f32[]{:T(128)} %constant.241.clone.1..sunk), kind=kCustom, calls=%fused_computation.31.clone.1 | custom fusion | flops 589824 | bytes 786944 | tf_op jit(solution)/shard_map/while/body/eval_jaxpr/scatter-add | solution.py:198
  449.1 8.8 gather_fusion
  457.9 8.8 gather_fusion.1
  478.3 25.3 %scatter_custom_fusion.15 = f32[1536,128]{1,0:T(8,128)S(1)} fusion(s32[4608]{0:T(1024)S(1)} %fusion.97, f32[4608,128]{1,0:T(8,128)S(1)} %bitcast.95, f32[]{:T(128)} %constant.241.clone.1..sunk), kind=kCustom, calls=%fused_computation.33.clone.1 | custom fusion | flops 589824 | bytes 786436 | tf_op jit(solution)/shard_map/while/body/eval_jaxpr/scatter-add | solution.py:197
  506.7 25.6 %scatter_custom_fusion.14 = f32[1536,128]{1,0:T(8,128)S(1)} fusion(s32[4608]{0:T(1024)S(1)} %fusion.97, f32[4608,128]{1,0:T(8,128)} %bitcast.94, f32[]{:T(128)} %constant.241.clone.1..sunk), kind=kCustom, calls=%fused_computation.31.clone.1 | custom fusion | flops 589824 | bytes 786944 | tf_op jit(solution)/shard_map/while/body/eval_jaxpr/scatter-add | solution.py:198
  536.7 8.8 gather_fusion
  545.5 8.8 gather_fusion.1
  565.9 25.3 %scatter_custom_fusion.15 = f32[1536,128]{1,0:T(8,128)S(1)} fusion(s32[4608]{0:T(1024)S(1)} %fusion.97, f32[4608,128]{1,0:T(8,128)S(1)} %bitcast.95, f32[]{:T(128)} %constant.241.clone.1..sunk), kind=kCustom, calls=%fused_computation.33.clone.1 | custom fusion | flops 589824 | bytes 786436 | tf_op jit(solution)/shard_map/while/body/eval_jaxpr/scatter-add | solution.py:197
  594.3 25.6 %scatter_custom_fusion.14 = f32[1536,128]{1,0:T(8,128)S(1)} fusion(s32[4608]{0:T(1024)S(1)} %fusion.97, f32[4608,128]{1,0:T(8,128)} %bitcast.94, f32[]{:T(128)} %constant.241.clone.1..sunk), kind=kCustom, calls=%fused_computation.31.clone.1 | custom fusion | flops 589824 | bytes 786944 | tf_op jit(solution)/shard_map/while/body/eval_jaxpr/scatter-add | solution.py:198
  624.3 8.8 gather_fusion
  633.1 8.8 gather_fusion.1
  653.5 25.3 %scatter_custom_fusion.15 = f32[1536,128]{1,0:T(8,128)S(1)} fusion(s32[4608]{0:T(1024)S(1)} %fusion.97, f32[4608,128]{1,0:T(8,128)S(1)} %bitcast.95, f32[]{:T(128)} %constant.241.clone.1..sunk), kind=kCustom, calls=%fused_computation.33.clone.1 | custom fusion | flops 589824 | bytes 786436 | tf_op jit(solution)/shard_map/while/body/eval_jaxpr/scatter-add | solution.py:197
  681.9 25.6 %scatter_custom_fusion.14 = f32[1536,128]{1,0:T(8,128)S(1)} fusion(s32[4608]{0:T(1024)S(1)} %fusion.97, f32[4608,128]{1,0:T(8,128)} %bitcast.94, f32[]{:T(128)} %constant.241.clone.1..sunk), kind=kCustom, calls=%fused_computation.31.clone.1 | custom fusion | flops 589824 | bytes 786944 | tf_op jit(solution)/shard_map/while/body/eval_jaxpr/scatter-add | solution.py:198
  711.8 8.8 gather_fusion
  720.6 8.8 gather_fusion.1
  741.0 25.3 %scatter_custom_fusion.15 = f32[1536,128]{1,0:T(8,128)S(1)} fusion(s32[4608]{0:T(1024)S(1)} %fusion.97, f32[4608,128]{1,0:T(8,128)S(1)} %bitcast.95, f32[]{:T(128)} %constant.241.clone.1..sunk), kind=kCustom, calls=%fused_computation.33.clone.1 | custom fusion | flops 589824 | bytes 786436 | tf_op jit(solution)/shard_map/while/body/eval_jaxpr/scatter-add | solution.py:197
  769.4 25.6 %scatter_custom_fusion.14 = f32[1536,128]{1,0:T(8,128)S(1)} fusion(s32[4608]{0:T(1024)S(1)} %fusion.97, f32[4608,128]{1,0:T(8,128)} %bitcast.94, f32[]{:T(128)} %constant.241.clone.1..sunk), kind=kCustom, calls=%fused_computation.31.clone.1 | custom fusion | flops 589824 | bytes 786944 | tf_op jit(solution)/shard_map/while/body/eval_jaxpr/scatter-add | solution.py:198
  799.3 8.8 gather_fusion
  808.1 8.8 gather_fusion.1
  828.5 25.3 %scatter_custom_fusion.15 = f32[1536,128]{1,0:T(8,128)S(1)} fusion(s32[4608]{0:T(1024)S(1)} %fusion.97, f32[4608,128]{1,0:T(8,128)S(1)} %bitcast.95, f32[]{:T(128)} %constant.241.clone.1..sunk), kind=kCustom, calls=%fused_computation.33.clone.1 | custom fusion | flops 589824 | bytes 786436 | tf_op jit(solution)/shard_map/while/body/eval_jaxpr/scatter-add | solution.py:197
  856.9 25.6 %scatter_custom_fusion.14 = f32[1536,128]{1,0:T(8,128)S(1)} fusion(s32[4608]{0:T(1024)S(1)} %fusion.97, f32[4608,128]{1,0:T(8,128)} %bitcast.94, f32[]{:T(128)} %constant.241.clone.1..sunk), kind=kCustom, calls=%fused_computation.31.clone.1 | custom fusion | flops 589824 | bytes 786944 | tf_op jit(solution)/shard_map/while/body/eval_jaxpr/scatter-add | solution.py:198
  886.9 8.8 gather_fusion
  895.7 8.8 gather_fusion.1
  916.2 25.3 %scatter_custom_fusion.15 = f32[1536,128]{1,0:T(8,128)S(1)} fusion(s32[4608]{0:T(1024)S(1)} %fusion.97, f32[4608,128]{1,0:T(8,128)S(1)} %bitcast.95, f32[]{:T(128)} %constant.241.clone.1..sunk), kind=kCustom, calls=%fused_computation.33.clone.1 | custom fusion | flops 589824 | bytes 786436 | tf_op jit(solution)/shard_map/while/body/eval_jaxpr/scatter-add | solution.py:197
  944.5 25.6 %scatter_custom_fusion.14 = f32[1536,128]{1,0:T(8,128)S(1)} fusion(s32[4608]{0:T(1024)S(1)} %fusion.97, f32[4608,128]{1,0:T(8,128)} %bitcast.94, f32[]{:T(128)} %constant.241.clone.1..sunk), kind=kCustom, calls=%fused_computation.31.clone.1 | custom fusion | flops 589824 | bytes 786944 | tf_op jit(solution)/shard_map/while/body/eval_jaxpr/scatter-add | solution.py:198
  978.0 6.8 collective-permute-done.3
  990.7 10.0 fusion.59
  1009.2 25.7 %collective-permute-done.5 = bf16[2,4,8,8,1280]{4,3,2,1,0:T(8,128)(2,1)} collective-permute-done((bf16[2,4,8,8,1280]{4,3,2,1,0:T(8,128)(2,1)S(1)}, bf16[2,4,8,8,1280]{4,3,2,1,0:T(8,128)(2,1)}, u32[]{:S(2)}, u32[]{:S(2)}) %collective-permute-start.5) | collective-permute-done | bytes 1310752 | tf_op jit(solution)/shard_map/ppermute | solution.py:38
  1036.5 24.8 %collective-permute-done.4 = bf16[2,4,8,8,1280]{4,3,2,1,0:T(8,128)(2,1)} collective-permute-done((bf16[2,4,8,8,1280]{4,3,2,1,0:T(8,128)(2,1)}, bf16[2,4,8,8,1280]{4,3,2,1,0:T(8,128)(2,1)}, u32[]{:S(2)}, u32[]{:S(2)}) %collective-permute-start.4) | collective-permute-done | bytes 1310752 | tf_op jit(solution)/shard_map/ppermute | solution.py:38
  (344 shorter events, 248.2 us)
Async XLA Ops:
  0.6 62.6 %copy-start.1 = (bf16[4,8,8,1280]{3,2,1,0:T(8,128)(2,1)S(1)}, bf16[4,8,8,1280]{3,2,1,0:T(8,128)(2,1)}, u32[]{:S(2)}) copy-start(bf16[4,8,8,1280]{3,2,1,0:T(8,128)(2,1)} %param.27) | copy-start | bytes 1966084
  0.6 62.6 %copy-start.2 = (bf16[4,8,8,1280]{3,2,1,0:T(8,128)(2,1)S(1)}, bf16[4,8,8,1280]{3,2,1,0:T(8,128)(2,1)}, u32[]{:S(2)}) copy-start(bf16[4,8,8,1280]{3,2,1,0:T(8,128)(2,1)} %param.26) | copy-start | bytes 1966084
  2.2 63.4 %copy-start.8 = (s32[1,2,2]{2,1,0:T(2,128)S(1)}, s32[1,2,2]{2,1,0:T(2,128)}, u32[]{:S(2)}) copy-start(s32[1,2,2]{2,1,0:T(2,128)} %param.29) | copy-start | bytes 52
  2.2 33.1 %collective-permute-start.1 = (bf16[2,4,8,8,1280]{4,3,2,1,0:T(8,128)(2,1)S(1)}, bf16[2,4,8,8,1280]{4,3,2,1,0:T(8,128)(2,1)S(1)}, u32[]{:S(2)}, u32[]{:S(2)}) collective-permute-start(bf16[2,4,8,8,1280]{4,3,2,1,0:T(8,128)(2,1)S(1)} %pad_maximum_fusion.2), channel_id=1, source_target_pairs={{4,0},{8,4},{12,8},{0,12},{5,1},{9,5},{13,9},{1,13},{6,2},{10,6},{... | collective-permute-start | bytes 3932168 | tf_op jit(solution)/shard_map/ppermute | solution.py:30
  6.1 57.1 %collective-permute-start = (bf16[2,4,8,8,1280]{4,3,2,1,0:T(8,128)(2,1)S(1)}, bf16[2,4,8,8,1280]{4,3,2,1,0:T(8,128)(2,1)S(1)}, u32[]{:S(2)}, u32[]{:S(2)}) collective-permute-start(bf16[2,4,8,8,1280]{4,3,2,1,0:T(8,128)(2,1)S(1)} %pad_maximum_fusion.2), channel_id=1, source_target_pairs={{0,4},{4,8},{8,12},{12,0},{1,5},{5,9},{9,13},{13,1},{2,6},{6,10},{... | collective-permute-start | bytes 3932168 | tf_op jit(solution)/shard_map/ppermute | solution.py:29
  63.2 2.3 copy-start.3
  65.6 11.6 %collective-permute-start.2 = (bf16[2,4,8,24,1280]{4,3,2,1,0:T(8,128)(2,1)}, bf16[2,4,8,24,1280]{4,3,2,1,0:T(8,128)(2,1)}, u32[]{:S(2)}, u32[]{:S(2)}) collective-permute-start(bf16[2,4,8,24,1280]{4,3,2,1,0:T(8,128)(2,1)} %pad_maximum_fusion), channel_id=1, source_target_pairs={{0,16},{16,0},{1,17},{17,1},{2,18},{18,2},{3,19},{19,3},{4,20},{20... | collective-permute-start | bytes 11796488 | tf_op jit(solution)/shard_map/ppermute | solution.py:19
  96.1 20.6 %copy-start.4 = (bf16[4,64,1280]{2,1,0:T(8,128)(2,1)}, bf16[4,64,1280]{2,1,0:T(8,128)(2,1)S(1)}, u32[]{:S(2)}) copy-start(bf16[4,64,1280]{2,1,0:T(8,128)(2,1)S(1)} %get-tuple-element.530) | copy-start | bytes 1966084 | tf_op jit(solution)/shard_map/while
  119.3 5.2 copy-start
  156.7 26.9 %copy-start.5 = (bf16[4,64,1280]{2,1,0:T(8,128)(2,1)S(1)}, bf16[4,64,1280]{2,1,0:T(8,128)(2,1)}, u32[]{:S(2)}) copy-start(bf16[4,64,1280]{2,1,0:T(8,128)(2,1)} %copy-done.4) | copy-start | bytes 1966084 | tf_op jit(solution)/shard_map/while
  183.6 20.6 %copy-start.4 = (bf16[4,64,1280]{2,1,0:T(8,128)(2,1)}, bf16[4,64,1280]{2,1,0:T(8,128)(2,1)S(1)}, u32[]{:S(2)}) copy-start(bf16[4,64,1280]{2,1,0:T(8,128)(2,1)S(1)} %get-tuple-element.530) | copy-start | bytes 1966084 | tf_op jit(solution)/shard_map/while
  206.8 5.2 copy-start
  244.2 27.0 %copy-start.5 = (bf16[4,64,1280]{2,1,0:T(8,128)(2,1)S(1)}, bf16[4,64,1280]{2,1,0:T(8,128)(2,1)}, u32[]{:S(2)}) copy-start(bf16[4,64,1280]{2,1,0:T(8,128)(2,1)} %copy-done.4) | copy-start | bytes 1966084 | tf_op jit(solution)/shard_map/while
  271.1 20.6 %copy-start.4 = (bf16[4,64,1280]{2,1,0:T(8,128)(2,1)}, bf16[4,64,1280]{2,1,0:T(8,128)(2,1)S(1)}, u32[]{:S(2)}) copy-start(bf16[4,64,1280]{2,1,0:T(8,128)(2,1)S(1)} %get-tuple-element.530) | copy-start | bytes 1966084 | tf_op jit(solution)/shard_map/while
  294.3 5.2 copy-start
  331.7 26.9 %copy-start.5 = (bf16[4,64,1280]{2,1,0:T(8,128)(2,1)S(1)}, bf16[4,64,1280]{2,1,0:T(8,128)(2,1)}, u32[]{:S(2)}) copy-start(bf16[4,64,1280]{2,1,0:T(8,128)(2,1)} %copy-done.4) | copy-start | bytes 1966084 | tf_op jit(solution)/shard_map/while
  358.6 20.6 %copy-start.4 = (bf16[4,64,1280]{2,1,0:T(8,128)(2,1)}, bf16[4,64,1280]{2,1,0:T(8,128)(2,1)S(1)}, u32[]{:S(2)}) copy-start(bf16[4,64,1280]{2,1,0:T(8,128)(2,1)S(1)} %get-tuple-element.530) | copy-start | bytes 1966084 | tf_op jit(solution)/shard_map/while
  381.8 5.2 copy-start
  419.2 26.9 %copy-start.5 = (bf16[4,64,1280]{2,1,0:T(8,128)(2,1)S(1)}, bf16[4,64,1280]{2,1,0:T(8,128)(2,1)}, u32[]{:S(2)}) copy-start(bf16[4,64,1280]{2,1,0:T(8,128)(2,1)} %copy-done.4) | copy-start | bytes 1966084 | tf_op jit(solution)/shard_map/while
  446.1 20.6 %copy-start.4 = (bf16[4,64,1280]{2,1,0:T(8,128)(2,1)}, bf16[4,64,1280]{2,1,0:T(8,128)(2,1)S(1)}, u32[]{:S(2)}) copy-start(bf16[4,64,1280]{2,1,0:T(8,128)(2,1)S(1)} %get-tuple-element.530) | copy-start | bytes 1966084 | tf_op jit(solution)/shard_map/while
  469.3 5.2 copy-start
  506.7 27.0 %copy-start.5 = (bf16[4,64,1280]{2,1,0:T(8,128)(2,1)S(1)}, bf16[4,64,1280]{2,1,0:T(8,128)(2,1)}, u32[]{:S(2)}) copy-start(bf16[4,64,1280]{2,1,0:T(8,128)(2,1)} %copy-done.4) | copy-start | bytes 1966084 | tf_op jit(solution)/shard_map/while
  533.7 20.6 %copy-start.4 = (bf16[4,64,1280]{2,1,0:T(8,128)(2,1)}, bf16[4,64,1280]{2,1,0:T(8,128)(2,1)S(1)}, u32[]{:S(2)}) copy-start(bf16[4,64,1280]{2,1,0:T(8,128)(2,1)S(1)} %get-tuple-element.530) | copy-start | bytes 1966084 | tf_op jit(solution)/shard_map/while
  556.9 5.2 copy-start
  594.3 27.0 %copy-start.5 = (bf16[4,64,1280]{2,1,0:T(8,128)(2,1)S(1)}, bf16[4,64,1280]{2,1,0:T(8,128)(2,1)}, u32[]{:S(2)}) copy-start(bf16[4,64,1280]{2,1,0:T(8,128)(2,1)} %copy-done.4) | copy-start | bytes 1966084 | tf_op jit(solution)/shard_map/while
  621.3 20.6 %copy-start.4 = (bf16[4,64,1280]{2,1,0:T(8,128)(2,1)}, bf16[4,64,1280]{2,1,0:T(8,128)(2,1)S(1)}, u32[]{:S(2)}) copy-start(bf16[4,64,1280]{2,1,0:T(8,128)(2,1)S(1)} %get-tuple-element.530) | copy-start | bytes 1966084 | tf_op jit(solution)/shard_map/while
  644.5 5.2 copy-start
  681.9 27.0 %copy-start.5 = (bf16[4,64,1280]{2,1,0:T(8,128)(2,1)S(1)}, bf16[4,64,1280]{2,1,0:T(8,128)(2,1)}, u32[]{:S(2)}) copy-start(bf16[4,64,1280]{2,1,0:T(8,128)(2,1)} %copy-done.4) | copy-start | bytes 1966084 | tf_op jit(solution)/shard_map/while
  708.8 20.6 %copy-start.4 = (bf16[4,64,1280]{2,1,0:T(8,128)(2,1)}, bf16[4,64,1280]{2,1,0:T(8,128)(2,1)S(1)}, u32[]{:S(2)}) copy-start(bf16[4,64,1280]{2,1,0:T(8,128)(2,1)S(1)} %get-tuple-element.530) | copy-start | bytes 1966084 | tf_op jit(solution)/shard_map/while
  732.0 5.2 copy-start
  769.4 27.0 %copy-start.5 = (bf16[4,64,1280]{2,1,0:T(8,128)(2,1)S(1)}, bf16[4,64,1280]{2,1,0:T(8,128)(2,1)}, u32[]{:S(2)}) copy-start(bf16[4,64,1280]{2,1,0:T(8,128)(2,1)} %copy-done.4) | copy-start | bytes 1966084 | tf_op jit(solution)/shard_map/while
  796.3 20.6 %copy-start.4 = (bf16[4,64,1280]{2,1,0:T(8,128)(2,1)}, bf16[4,64,1280]{2,1,0:T(8,128)(2,1)S(1)}, u32[]{:S(2)}) copy-start(bf16[4,64,1280]{2,1,0:T(8,128)(2,1)S(1)} %get-tuple-element.530) | copy-start | bytes 1966084 | tf_op jit(solution)/shard_map/while
  819.5 5.2 copy-start
  856.9 27.1 %copy-start.5 = (bf16[4,64,1280]{2,1,0:T(8,128)(2,1)S(1)}, bf16[4,64,1280]{2,1,0:T(8,128)(2,1)}, u32[]{:S(2)}) copy-start(bf16[4,64,1280]{2,1,0:T(8,128)(2,1)} %copy-done.4) | copy-start | bytes 1966084 | tf_op jit(solution)/shard_map/while
  884.0 20.6 %copy-start.4 = (bf16[4,64,1280]{2,1,0:T(8,128)(2,1)}, bf16[4,64,1280]{2,1,0:T(8,128)(2,1)S(1)}, u32[]{:S(2)}) copy-start(bf16[4,64,1280]{2,1,0:T(8,128)(2,1)S(1)} %get-tuple-element.530) | copy-start | bytes 1966084 | tf_op jit(solution)/shard_map/while
  907.2 5.2 copy-start
  944.5 26.9 %copy-start.5 = (bf16[4,64,1280]{2,1,0:T(8,128)(2,1)S(1)}, bf16[4,64,1280]{2,1,0:T(8,128)(2,1)}, u32[]{:S(2)}) copy-start(bf16[4,64,1280]{2,1,0:T(8,128)(2,1)} %copy-done.4) | copy-start | bytes 1966084 | tf_op jit(solution)/shard_map/while
  977.4 7.3 collective-permute-start.3
  1002.1 4.3 copy-start.7
  1002.2 32.7 %collective-permute-start.5 = (bf16[2,4,8,8,1280]{4,3,2,1,0:T(8,128)(2,1)S(1)}, bf16[2,4,8,8,1280]{4,3,2,1,0:T(8,128)(2,1)}, u32[]{:S(2)}, u32[]{:S(2)}) collective-permute-start(bf16[2,4,8,8,1280]{4,3,2,1,0:T(8,128)(2,1)S(1)} %pad_maximum_fusion.4), channel_id=1, source_target_pairs={{12,0},{0,4},{4,8},{8,12},{13,1},{1,5},{5,9},{9,13},{14,2},{2,6},{... | collective-permute-start | bytes 3932168 | tf_op jit(solution)/shard_map/ppermute | solution.py:38
  1005.0 2.8 copy-start.6
  1005.0 56.3 %collective-permute-start.4 = (bf16[2,4,8,8,1280]{4,3,2,1,0:T(8,128)(2,1)}, bf16[2,4,8,8,1280]{4,3,2,1,0:T(8,128)(2,1)}, u32[]{:S(2)}, u32[]{:S(2)}) collective-permute-start(bf16[2,4,8,8,1280]{4,3,2,1,0:T(8,128)(2,1)} %pad_maximum_fusion.3), channel_id=1, source_target_pairs={{4,0},{8,4},{12,8},{0,12},{5,1},{9,5},{13,9},{1,13},{6,2},{10,6},{... | collective-permute-start | bytes 3932168 | tf_op jit(solution)/shard_map/ppermute | solution.py:38
where the time goes:
time: 1070 us
  other arithmetic  567 us (53%)
  local copies, waits for them, and re-layouts  248 us (23%)
  matrix products  127 us (12%)
  waiting for transfers between devices  114 us (11%)
    scatter-add x10, other arithmetic, one_head(): value_head_grad = empty.at[index_rows].add(value_block_grad.reshape(-1, HD))  256 us
    scatter-add x10, other arithmetic, one_head(): key_head_grad = empty.at[index_rows].add(key_block_grad.reshape(-1, HD))  253 us
    gather x10, local copies, waits for them, and re-layouts, one_head(): jnp.take(lax.dynamic_slice_in_dim(value_flat, start, HD, 1), flat_index,...  87.9 us
    gather x10, local copies, waits for them, and re-layouts, one_head(): jnp.take(lax.dynamic_slice_in_dim(key_flat, start, HD, 1), flat_index, ax...  87.9 us
    ppermute x2, waiting for transfers between devices, passed_along(): return lax.ppermute(block, axis, route)  50.6 us
    dot_general x10, matrix products, one_head(): jnp.einsum('gqk,gqd->gkd', probs, grad_head, preferred_element_type=jnp.f...  31.1 us
    ppermute x1, waiting for transfers between devices, extended(): after = lax.ppermute(leading, axis, down)  29.2 us
    ppermute x1, waiting for transfers between devices, extended(): before = lax.ppermute(last, axis, up)  27.9 us
  transfers between devices with their start and end apart: 6, of which 5 were waited for; matrix products, arithmetic and copies ran while one was open for 2% of the time, Pallas kernels for 0%

commit v1 on v0

v1 whole, which is shorter than its diff:
```python
import functools
import math

import jax
import jax.numpy as jnp
from jax import lax
from jax.experimental import pallas as pl
from jax.experimental.pallas import tpu as pltpu
from jax.sharding import PartitionSpec as P

HD = 128
TILE = 4
MASKED = -1e30
CHUNKS = 2

LAST = (((1,), (1,)), ((), ()))
FIRST = (((0,), (0,)), ((), ()))
PLAIN = (((1,), (0,)), ((), ()))


def dot(a, b, dims):
    return lax.dot_general(a, b, dims, preferred_element_type=jnp.float32)


def to_partner(block):
    count = lax.axis_size("lon")
    return lax.ppermute(block, "lon", [(i, i ^ 1) for i in range(count)])


def to_far(block, outward):
    count = lax.axis_size("lon")
    route = []
    for i in range(count):
        step = 2 if (i % 2 == 0) == outward else -2
        route.append((i, (i + step) % count))
    return lax.ppermute(block, "lon", route)


def to_twin(block):
    return lax.ppermute(block, "tm", [(0, 1), (1, 0)])


def attention_kernel(
    bias_ref,
    own_q,
    par_q,
    own_a,
    own_b,
    par_a,
    par_b,
    yown_a,
    yown_b,
    rel_a,
    rel_b,
    own_out,
    par_out,
    near_ref,
    twin_ref,
    scores_ref,
    probs_ref,
    grad_ref,
):
    rows = own_q.shape[2]
    factor = math.log2(math.e) / math.sqrt(HD)
    scale = 1.0 / math.sqrt(HD)
    blocks = ((own_a, own_b), (par_a, par_b), (yown_a, yown_b), (rel_a, rel_b))
    lon = bias_ref.shape[2]
    for which, (q_ref, out_ref) in enumerate(((own_q, own_out), (par_q, par_out))):
        query = q_ref[0, 0]
        grad = q_ref[0, 1]
        used = (0, 1, 3) if which == 0 else (1, 0, 2)
        parts = [(b, f) for b in used for f in range(2)]
        peak = None
        for at, (b, f) in enumerate(parts):
            key = blocks[b][f][0, 0]
            score = dot(key, query, LAST) * factor
            score = score.reshape(rows // lon, lon, rows) + bias_ref[which, at // 2][None]
            scores_ref[at] = score.reshape(rows, rows)
            top = jnp.max(score, axis=0)
            peak = top if peak is None else jnp.maximum(peak, top)
        peak = jnp.max(peak, axis=0, keepdims=True)
        total = jnp.zeros((lon, rows), jnp.float32)
        for at in range(len(parts)):
            expo = jnp.exp2(scores_ref[at] - peak)
            scores_ref[at] = expo
            total += jnp.sum(expo.reshape(rows // lon, lon, rows), axis=0)
        inverse = 1.0 / jnp.sum(total, axis=0, keepdims=True)
        attended = jnp.zeros((HD, rows), jnp.float32)
        for at, (b, f) in enumerate(parts):
            probs = (scores_ref[at] * inverse).astype(jnp.bfloat16)
            probs_ref[at] = probs
            attended += dot(blocks[b][f][0, 1], probs, FIRST)
        attended = attended.T.astype(jnp.bfloat16)
        out_ref[0, 0] = attended
        product = grad.astype(jnp.float32) * attended.astype(jnp.float32)
        delta = jnp.sum(product.T, axis=0, keepdims=True)
        query_grad = jnp.zeros((HD, rows), jnp.float32)
        for at, (b, f) in enumerate(parts):
            key = blocks[b][f][0, 0]
            value = blocks[b][f][0, 1]
            probs = probs_ref[at]
            dprobs = dot(value, grad, LAST)
            dscores = (probs.astype(jnp.float32) * (dprobs - delta)).astype(jnp.bfloat16)
            query_grad += dot(key, dscores, FIRST)
            key_part = dot(dscores, query, PLAIN) * scale
            value_part = dot(probs, grad, PLAIN)
            if which == 0 and b != 2 or b == 2:
                grad_ref[b, f, 0] = key_part
                grad_ref[b, f, 1] = value_part
            else:
                grad_ref[b, f, 0] += key_part
                grad_ref[b, f, 1] += value_part
        out_ref[0, 1] = (query_grad * scale).T.astype(jnp.bfloat16)
    for b in range(4):
        near_ref[0, b] = grad_ref[b, 0]
        twin_ref[0, b] = grad_ref[b, 1].astype(jnp.bfloat16)


def attention(bias, own_q, par_q, blocks):
    heads, _, rows, _ = own_q.shape
    one = pl.BlockSpec((1, 2, rows, HD), lambda h: (h, 0, 0, 0))
    whole = pl.BlockSpec(bias.shape, lambda h: (0, 0, 0, 0))
    flat = [part for pair in blocks for part in pair]
    pairs = (heads, 2, rows, HD)
    spread = (heads, 4, 2, rows, HD)
    per_head = pl.BlockSpec((1, 4, 2, rows, HD), lambda h: (h, 0, 0, 0, 0))
    work = heads * 2 * 6 * 6 * 2 * rows * rows * HD
    return pl.pallas_call(
        attention_kernel,
        grid=(heads,),
        in_specs=[whole] + [one] * (2 + len(flat)),
        out_specs=[one, one, per_head, per_head],
        out_shape=[
            jax.ShapeDtypeStruct(pairs, jnp.bfloat16),
            jax.ShapeDtypeStruct(pairs, jnp.bfloat16),
            jax.ShapeDtypeStruct(spread, jnp.float32),
            jax.ShapeDtypeStruct(spread, jnp.bfloat16),
        ],
        scratch_shapes=[
            pltpu.VMEM((6, rows, rows), jnp.float32),
            pltpu.VMEM((6, rows, rows), jnp.bfloat16),
            pltpu.VMEM((4, 2, 2, rows, HD), jnp.float32),
        ],
        compiler_params=pltpu.CompilerParams(vmem_limit_bytes=40 * 1024 * 1024),
        cost_estimate=pl.CostEstimate(
            flops=work, bytes_accessed=heads * 28 * rows * HD * 2, transcendentals=heads * 12 * rows * rows
        ),
        name="attention",
    )(bias, own_q, par_q, *flat)


def window_bias(offsets, side, frames, lats, lons):
    lat_tiles, lon_tiles = offsets.shape[1:]
    per_row = jnp.repeat(jnp.repeat(offsets, TILE, axis=1), TILE, axis=2)
    centre = per_row + (jnp.arange(lons) // TILE)[None, None, :]
    centre = jnp.broadcast_to(centre[:, None], (2, frames, lats, lons)).reshape(2, -1)
    sign = 1 - 2 * side
    place = jnp.arange(lons) // TILE
    shift = jnp.array([[0, 1, -1], [0, -1, 1]], jnp.int32) * sign * lon_tiles
    column = shift[:, :, None] + place[None, None, :]
    near = jnp.abs(column[:, :, :, None] - centre[:, None, None, :]) <= 1
    return jnp.where(near, 0.0, MASKED).astype(jnp.float32)


def on_device(query_rows, key_rows, value_rows, out_grad, window_offsets):
    frames, lats, lons, width = query_rows.shape
    heads = width // HD
    half = heads // 2
    rows = frames * lats * lons
    frame_tiles = frames // TILE * lax.axis_size("tm")
    if frame_tiles > 2 or lats // TILE > 2 or lons != 2 * TILE or heads % 2:
        raise ValueError("unsupported block")
    side = lax.axis_index("lon") % 2

    def by_head(first, second):
        pair = jnp.stack([first, second]).reshape(2, frames, lats, lons, heads, HD)
        return pair.transpose(4, 0, 1, 2, 3, 5).reshape(heads, 2, rows, HD)

    key_value = by_head(key_rows, value_rows)
    query_grad = by_head(query_rows, out_grad)

    def halves(array):
        mine = lax.dynamic_slice_in_dim(array, side * half, half, 0)
        theirs = lax.dynamic_slice_in_dim(array, (1 - side) * half, half, 0)
        return mine, theirs

    mine_kv, theirs_kv = halves(key_value)
    mine_qg, theirs_qg = halves(query_grad)
    offsets = window_offsets.reshape(lats // TILE, lons // TILE)
    bias = window_bias(jnp.stack([offsets, to_partner(offsets)]), side, frames, lats, lons)

    bounds = [half * c // CHUNKS for c in range(CHUNKS + 1)]
    spans = list(zip(bounds[:-1], bounds[1:]))
    results = []
    for low, high in spans:
        own = mine_kv[low:high]
        partner = to_partner(theirs_kv[low:high])
        far = to_far(own, False)
        partner_q = to_partner(theirs_qg[low:high])
        relayed = to_far(partner, True)
        blocks = [(part, to_twin(part)) for part in (own, partner, far, relayed)]
        own_out, partner_out, near, twin = attention(bias, mine_qg[low:high], partner_q, blocks)
        summed = near + to_twin(twin).astype(jnp.float32)
        back_out = to_partner(partner_out)
        back_relay = to_far(summed[:, 3].astype(jnp.bfloat16), False)
        back_far = to_far(summed[:, 2].astype(jnp.bfloat16), True)
        theirs_grad = to_partner((summed[:, 1] + back_relay.astype(jnp.float32)).astype(jnp.bfloat16))
        mine_grad = (summed[:, 0] + back_far.astype(jnp.float32)).astype(jnp.bfloat16)
        results.append((own_out, mine_grad, back_out, theirs_grad))

    own_out, mine_grad, back_out, theirs_grad = (jnp.concatenate(r) for r in zip(*results))

    def assembled(mine, theirs):
        low = jnp.where(side == 0, mine, theirs)
        high = jnp.where(side == 0, theirs, mine)
        array = jnp.concatenate([low, high])
        shaped = array.reshape(heads, 2, frames, lats, lons, HD).transpose(1, 2, 3, 4, 0, 5)
        shaped = shaped.reshape(2, frames, lats, lons, width)
        return shaped[0], shaped[1]

    attended, query_out = assembled(own_out, back_out)
    key_out, value_out = assembled(mine_grad, theirs_grad)
    return attended, query_out, key_out, value_out


def solution(mesh):
    rows = P("tm", None, "lon", "head")
    return jax.shard_map(
        on_device,
        mesh=mesh,
        in_specs=(rows, rows, rows, rows, P("tm", None, "lon")),
        out_specs=(rows, rows, rows, rows),
        check_vma=False,
    )
```

time: 1070 us -> 114 us (0.11)
  other arithmetic: 567 us -> 9.42 us
  local copies, waits for them, and re-layouts: 248 us -> 16 us
  matrix products: 127 us -> 0 us
  waiting for transfers between devices: 114 us -> 41.3 us
  Pallas kernels: 0 us -> 24.5 us
  starting transfers between devices: 7.49 us -> 21.7 us
    scatter-add x20 -> x0, other arithmetic: 509 us -> none  [the longest x10 256 us: one_head(): value_head_grad = empty.at[index_rows].add(value_block_grad.reshape(-1, HD))]
    gather x20 -> x0, local copies, waits for them, and re-layouts: 176 us -> none  [the longest x10 87.9 us: one_head(): jnp.take(lax.dynamic_slice_in_dim(value_flat, start, HD, 1), flat_index,...]
    dot_general x60 -> x0, matrix products: 127 us -> none  [the longest x10 31.1 us: one_head(): jnp.einsum('gqk,gqd->gkd', probs, grad_head, preferred_element_type=jnp.f...]
    ppermute x6 -> x27, waiting for transfers between devices: 114 us -> 41.3 us  [the longest x8 22.2 us: to_far(): return lax.ppermute(block, 'lon', route)]
    pallas_call x0 -> x2, Pallas kernels: none -> 24.5 us  [attention(): pl.pallas_call(attention_kernel, grid=(heads,), in_specs=[whole] + [one]...]
    dynamic_slice x20 -> x0, local copies, waits for them, and re-layouts: 20.6 us -> none  [the longest x10 10.3 us: one_head(): lax.dynamic_slice_in_dim(key_flat, start, HD, 1)]
    another operation x17 -> x3, local copies, waits for them, and re-layouts: 15.8 us -> 0.83 us  [the longest x2 0.73 us: by_head(): pair = jnp.stack([first, second]).reshape(2, frames, lats, lons, heads, HD)]
    ppermute x6 -> x27, starting transfers between devices: 7.49 us -> 21.7 us  [the longest x8 10.5 us: to_far(): return lax.ppermute(block, 'lon', route)]
  transfers between devices with their start and end apart: 6 -> 27, of which waited for: 5 -> 9; matrix products, arithmetic and copies ran while one was open for 2% -> 13% of each run, Pallas kernels for 0% -> 21%
where the time goes in v1:
time: 114 us
  waiting for transfers between devices  41.3 us (36%)
  Pallas kernels  24.5 us (21%)
  starting transfers between devices  21.7 us (19%)
  local copies, waits for them, and re-layouts  16 us (14%)
  other arithmetic  9.42 us (8%)
    pallas_call x2, Pallas kernels, attention(): pl.pallas_call(attention_kernel, grid=(heads,), in_specs=[whole] + [one]...  24.5 us
    ppermute x8, waiting for transfers between devices, to_far(): return lax.ppermute(block, 'lon', route)  22.2 us
    ppermute x9, waiting for transfers between devices, to_partner(): return lax.ppermute(block, 'lon', [(i, i ^ 1) for i in range(count)])  17.6 us
    ppermute x8, starting transfers between devices, to_far(): return lax.ppermute(block, 'lon', route)  10.5 us
    ppermute x9, starting transfers between devices, to_partner(): return lax.ppermute(block, 'lon', [(i, i ^ 1) for i in range(count)])  9.4 us
    unnamed x30, local copies, waits for them, and re-layouts  5.98 us
    slice x6, local copies, waits for them, and re-layouts, assembled(): return (shaped[0], shaped[1])  4.06 us
    convert_element_type x2, other arithmetic, on_device(): (summed[:, 1] + back_relay.astype(jnp.float32)).astype(jnp.bfloat16)  2.31 us
  transfers between devices with their start and end apart: 27, of which 9 were waited for; matrix products, arithmetic and copies ran while one was open for 13% of the time, Pallas kernels for 21%

profile of v1, /device:TPU:0, one launch (start us, length us, event | category | flops | bytes accessed | tf_op | source)
XLA Modules:
  0.0 113.8 jit_solution(9636971081738171677)
XLA Ops:
  0.6 3.0 %collective-permute-start = (s32[2,2]{1,0:T(2,128)}, s32[2,2]{1,0:T(2,128)S(1)}, u32[]{:S(2)}, u32[]{:S(2)}) collective-permute-start(s32[2,2]{1,0:T(2,128)} %bitcast.94), channel_id=1, source_target_pairs={{0,4},{4,0},{8,12},{12,8},{1,5},{5,1},{9,13},{13,9},{2,6},{6,2},{1... | collective-permute-start | bytes 56 | tf_op jit(solution)/shard_map/ppermute | solution.py:27
  3.6 1.4 %pad_maximum_fusion = bf16[2,4,8,8,10,128]{5,3,4,2,1,0:T(8,128)(2,1)S(1)} fusion(bf16[1,4,8,8,10,128]{5,3,4,2,1,0:T(8,128)(2,1)} %bitcast.81, bf16[1,4,8,8,10,128]{5,3,4,2,1,0:T(8,128)(2,1)} %bitcast.82), kind=kLoop, calls=%fused_computation.2 | loop fusion | flops 655360 | bytes 2621440 | tf_op jit(solution)/shard_map/stack | solution.py:176
  5.5 1.0 copy-done.8
  7.2 2.1 %collective-permute-start.3 = (bf16[2,2,256,128]{3,2,1,0:T(8,128)(2,1)S(1)}, bf16[2,2,256,128]{3,2,1,0:T(8,128)(2,1)S(1)}, u32[]{:S(2)}, u32[]{:S(2)}) collective-permute-start(bf16[2,2,256,128]{3,2,1,0:T(8,128)(2,1)S(1)} %get-tuple-element.30), channel_id=1, source_target_pairs={{0,4},{4,0},{8,12},{12,8},{1,5},{5,1},{9,13},{13,9},{2,6},{6,2},{1... | collective-permute-start | bytes 786440 | tf_op jit(solution)/shard_map/ppermute | solution.py:27
  9.2 1.5 %collective-permute-start.5 = (bf16[2,2,256,128]{3,2,1,0:T(8,128)(2,1)S(1)}, bf16[2,2,256,128]{3,2,1,0:T(8,128)(2,1)S(1)}, u32[]{:S(2)}, u32[]{:S(2)}) collective-permute-start(bf16[2,2,256,128]{3,2,1,0:T(8,128)(2,1)S(1)} %get-tuple-element.31.own_a), channel_id=1, source_target_pairs={{0,8},{4,12},{8,0},{12,4},{1,9},{5,13},{9,1},{13,5},{2,10},{6,14},... | collective-permute-start | bytes 786440 | tf_op jit(solution)/shard_map/ppermute | solution.py:36
  10.7 1.2 %constant_dynamic-slice_fusion.4 = (bf16[3,2,256,128]{3,2,1,0:T(8,128)(2,1)S(1)}, bf16[3,2,256,128]{3,2,1,0:T(8,128)(2,1)S(1)}) fusion(bf16[10,2,256,128]{3,2,1,0:T(8,128)(2,1)} %bitcast.78, s32[]{:T(128)S(6)} %add.80, s32[]{:T(128)S(6)} %add.79), kind=kLoop, calls=%fused_computation.43 | loop fusion | bytes 1572872 | tf_op jit(solution)/shard_map/slice | solution.py:197
  11.9 1.0 collective-permute-start.11
  13.0 8.4 %collective-permute-done.3.par_a = bf16[2,2,256,128]{3,2,1,0:T(8,128)(2,1)S(1)} collective-permute-done((bf16[2,2,256,128]{3,2,1,0:T(8,128)(2,1)S(1)}, bf16[2,2,256,128]{3,2,1,0:T(8,128)(2,1)S(1)}, u32[]{:S(2)}, u32[]{:S(2)}) %collective-permute-start.3) | collective-permute-done | bytes 262176 | tf_op jit(solution)/shard_map/ppermute | solution.py:27
  21.4 1.5 %collective-permute-start.7 = (bf16[2,2,256,128]{3,2,1,0:T(8,128)(2,1)S(1)}, bf16[2,2,256,128]{3,2,1,0:T(8,128)(2,1)}, u32[]{:S(2)}, u32[]{:S(2)}) collective-permute-start(bf16[2,2,256,128]{3,2,1,0:T(8,128)(2,1)S(1)} %collective-permute-done.3.par_a), channel_id=1, source_target_pairs={{0,8},{4,12},{8,0},{12,4},{1,9},{5,13},{9,1},{13,5},{2,10},{6,14},... | collective-permute-start | bytes 786440 | tf_op jit(solution)/shard_map/ppermute | solution.py:36
  22.9 0.7 broadcast_add_fusion.1
  24.1 4.3 %collective-permute-done.11.par_a = bf16[3,2,256,128]{3,2,1,0:T(8,128)(2,1)S(1)} collective-permute-done((bf16[3,2,256,128]{3,2,1,0:T(8,128)(2,1)S(1)}, bf16[3,2,256,128]{3,2,1,0:T(8,128)(2,1)S(1)}, u32[]{:S(2)}, u32[]{:S(2)}) %collective-permute-start.11) | collective-permute-done | bytes 393248 | tf_op jit(solution)/shard_map/ppermute | solution.py:27
  28.4 1.5 %collective-permute-start.15 = (bf16[3,2,256,128]{3,2,1,0:T(8,128)(2,1)S(1)}, bf16[3,2,256,128]{3,2,1,0:T(8,128)(2,1)S(1)}, u32[]{:S(2)}, u32[]{:S(2)}) collective-permute-start(bf16[3,2,256,128]{3,2,1,0:T(8,128)(2,1)S(1)} %collective-permute-done.11.par_a), channel_id=1, source_target_pairs={{0,8},{4,12},{8,0},{12,4},{1,9},{5,13},{9,1},{13,5},{2,10},{6,14},... | collective-permute-start | bytes 1179656 | tf_op jit(solution)/shard_map/ppermute | solution.py:36
  29.9 1.9 %constant_dynamic-slice_fusion.6 = (bf16[3,2,256,128]{3,2,1,0:T(8,128)(2,1)}, bf16[3,2,256,128]{3,2,1,0:T(8,128)(2,1)S(1)}) fusion(bf16[10,2,256,128]{3,2,1,0:T(8,128)(2,1)} %bitcast.76, s32[]{:T(128)S(6)} %add.80, s32[]{:T(128)S(6)} %add.79), kind=kLoop, calls=%fused_computation.45 | loop fusion | bytes 1572872 | tf_op jit(solution)/shard_map/slice | solution.py:199
  31.8 0.7 copy-done.2
  33.3 0.7 broadcast_add_fusion
  34.1 0.6 broadcast_in_dim.26
  34.7 0.8 sub.32
  35.6 3.5 %collective-permute-done.13.yown_a = bf16[3,2,256,128]{3,2,1,0:T(8,128)(2,1)S(1)} collective-permute-done((bf16[3,2,256,128]{3,2,1,0:T(8,128)(2,1)S(1)}, bf16[3,2,256,128]{3,2,1,0:T(8,128)(2,1)S(1)}, u32[]{:S(2)}, u32[]{:S(2)}) %collective-permute-start.13) | collective-permute-done | bytes 393248 | tf_op jit(solution)/shard_map/ppermute | solution.py:36
  39.1 0.7 copy-done.4
  40.3 3.3 %collective-permute-done.15.rel_a = bf16[3,2,256,128]{3,2,1,0:T(8,128)(2,1)S(1)} collective-permute-done((bf16[3,2,256,128]{3,2,1,0:T(8,128)(2,1)S(1)}, bf16[3,2,256,128]{3,2,1,0:T(8,128)(2,1)S(1)}, u32[]{:S(2)}, u32[]{:S(2)}) %collective-permute-start.15) | collective-permute-done | bytes 393248 | tf_op jit(solution)/shard_map/ppermute | solution.py:36
  43.6 0.8 fusion.8.bias_ref
  44.4 0.9 copy-done.3
  45.4 0.9 copy-done.5
  46.3 10.4 %attention.2 = (bf16[2,2,256,128]{3,2,1,0:T(8,128)(2,1)S(1)}, bf16[2,2,256,128]{3,2,1,0:T(8,128)(2,1)S(1)}, f32[2,4,2,256,128]{4,3,2,1,0:T(8,128)S(1)}, bf16[2,4,2,256,128]{4,3,2,1,0:T(8,128)(2,1)S(1)}) custom-call(f32[2,3,8,256]{3,2,1,0:T(8,128)S(1)} %fusion.8.bias_ref, bf16[2,2,256,128]{3,2,1,0:T(8,128)(2,1)S(1)} %get-tuple-element.33.own_q, ...), custom_call_target="tpu_custom_call" | custom-call | flops 2415919104 | bytes 3670016 | tf_op jit(solution)/shard_map/attention/pallas_call | solution.py:128
  56.8 0.6 collective-permute-start.19
  57.3 14.0 %attention.3 = (bf16[3,2,256,128]{3,2,1,0:T(8,128)(2,1)S(1)}, bf16[3,2,256,128]{3,2,1,0:T(8,128)(2,1)S(1)}, f32[3,4,2,256,128]{4,3,2,1,0:T(8,128)S(1)}, bf16[3,4,2,256,128]{4,3,2,1,0:T(8,128)(2,1)S(1)}) custom-call(f32[2,3,8,256]{3,2,1,0:T(8,128)S(1)} %fusion.8.bias_ref, bf16[3,2,256,128]{3,2,1,0:T(8,128)(2,1)S(1)} %get-tuple-element.37.own_q, ...), custom_call_target="tpu_custom_call" | custom-call | flops 3623878656 | bytes 5505024 | tf_op jit(solution)/shard_map/attention/pallas_call | solution.py:128
  71.8 1.6 %collective-permute-start.23 = (bf16[2,2,256,128]{3,2,1,0:T(8,128)(2,1)S(1)}, bf16[2,2,256,128]{3,2,1,0:T(8,128)(2,1)S(1)}, u32[]{:S(2)}, u32[]{:S(2)}) collective-permute-start(bf16[2,2,256,128]{3,2,1,0:T(8,128)(2,1)S(1)} %get-tuple-element.39), channel_id=1, source_target_pairs={{0,8},{4,12},{8,0},{12,4},{1,9},{5,13},{9,1},{13,5},{2,10},{6,14},... | collective-permute-start | bytes 786440 | tf_op jit(solution)/shard_map/ppermute | solution.py:36
  73.4 1.5 %collective-permute-done.21 = bf16[3,4,2,256,128]{4,3,2,1,0:T(8,128)(2,1)S(1)} collective-permute-done((bf16[3,4,2,256,128]{4,3,2,1,0:T(8,128)(2,1)S(1)}, bf16[3,4,2,256,128]{4,3,2,1,0:T(8,128)(2,1)S(1)}, u32[]{:S(2)}, u32[]{:S(2)}) %collective-permute-start.21) | collective-permute-done | bytes 1572896 | tf_op jit(solution)/shard_map/ppermute | solution.py:40
  75.3 1.6 %copy-done.6 = f32[3,4,2,256,128]{4,3,2,1,0:T(8,128)} copy-done((f32[3,4,2,256,128]{4,3,2,1,0:T(8,128)}, f32[3,4,2,256,128]{4,3,2,1,0:T(8,128)S(1)}, u32[]{:S(2)}) %copy-start.6) | copy-done | bytes 3145752
  77.1 1.6 %collective-permute-start.25 = (bf16[3,2,256,128]{3,2,1,0:T(8,128)(2,1)S(1)}, bf16[3,2,256,128]{3,2,1,0:T(8,128)(2,1)S(1)}, u32[]{:S(2)}, u32[]{:S(2)}) collective-permute-start(bf16[3,2,256,128]{3,2,1,0:T(8,128)(2,1)S(1)} %get-tuple-element.21), channel_id=1, source_target_pairs={{0,8},{4,12},{8,0},{12,4},{1,9},{5,13},{9,1},{13,5},{2,10},{6,14},... | collective-permute-start | bytes 1179656 | tf_op jit(solution)/shard_map/ppermute | solution.py:36
  78.6 0.5 collective-permute-start.17
  79.2 1.5 %collective-permute-start.18 = (bf16[3,2,256,128]{3,2,1,0:T(8,128)(2,1)S(1)}, bf16[3,2,256,128]{3,2,1,0:T(8,128)(2,1)S(1)}, u32[]{:S(2)}, u32[]{:S(2)}) collective-permute-start(bf16[3,2,256,128]{3,2,1,0:T(8,128)(2,1)S(1)} %get-tuple-element.15), channel_id=1, source_target_pairs={{0,4},{4,0},{8,12},{12,8},{1,5},{5,1},{9,13},{13,9},{2,6},{6,2},{1... | collective-permute-start | bytes 1179656 | tf_op jit(solution)/shard_map/ppermute | solution.py:27
  80.7 0.8 collective-permute-start.20
  81.4 1.1 fusion.5
  82.5 0.6 collective-permute-start.24
  83.1 6.3 %collective-permute-done.25 = bf16[3,2,256,128]{3,2,1,0:T(8,128)(2,1)S(1)} collective-permute-done((bf16[3,2,256,128]{3,2,1,0:T(8,128)(2,1)S(1)}, bf16[3,2,256,128]{3,2,1,0:T(8,128)(2,1)S(1)}, u32[]{:S(2)}, u32[]{:S(2)}) %collective-permute-start.25) | collective-permute-done | bytes 393248 | tf_op jit(solution)/shard_map/ppermute | solution.py:36
  89.4 1.5 %collective-permute-start.22 = (bf16[3,2,256,128]{3,2,1,0:T(8,128)(2,1)S(1)}, bf16[3,2,256,128]{3,2,1,0:T(8,128)(2,1)S(1)}, u32[]{:S(2)}, u32[]{:S(2)}) collective-permute-start(bf16[3,2,256,128]{3,2,1,0:T(8,128)(2,1)S(1)} %get-tuple-element.20), channel_id=1, source_target_pairs={{0,8},{4,12},{8,0},{12,4},{1,9},{5,13},{9,1},{13,5},{2,10},{6,14},... | collective-permute-start | bytes 1179656 | tf_op jit(solution)/shard_map/ppermute | solution.py:36
  90.9 1.2 %fusion.1 = bf16[3,2,256,128]{3,2,1,0:T(8,128)(2,1)S(1)} fusion(f32[3,4,2,256,128]{4,3,2,1,0:T(8,128)} %copy-done.6, bf16[3,2,256,128]{3,2,1,0:T(8,128)(2,1)S(1)} %collective-permute-done.25), kind=kLoop, calls=%fused_computation.8 | loop fusion | flops 589824 | bytes 1572864 | tf_op jit(solution)/shard_map/convert_element_type | solution.py:207
  92.2 2.9 %collective-permute-done.20 = bf16[2,2,256,128]{3,2,1,0:T(8,128)(2,1)S(1)} collective-permute-done((bf16[2,2,256,128]{3,2,1,0:T(8,128)(2,1)S(1)}, bf16[2,2,256,128]{3,2,1,0:T(8,128)(2,1)S(1)}, u32[]{:S(2)}, u32[]{:S(2)}) %collective-permute-start.20) | collective-permute-done | bytes 262176 | tf_op jit(solution)/shard_map/ppermute | solution.py:36
  95.0 0.6 collective-permute-start.26
  95.7 1.1 fusion.7
  96.8 6.3 %collective-permute-done.22 = bf16[3,2,256,128]{3,2,1,0:T(8,128)(2,1)S(1)} collective-permute-done((bf16[3,2,256,128]{3,2,1,0:T(8,128)(2,1)S(1)}, bf16[3,2,256,128]{3,2,1,0:T(8,128)(2,1)S(1)}, u32[]{:S(2)}, u32[]{:S(2)}) %collective-permute-start.22) | collective-permute-done | bytes 393248 | tf_op jit(solution)/shard_map/ppermute | solution.py:36
  103.0 1.2 %fusion.3 = bf16[3,2,256,128]{3,2,1,0:T(8,128)(2,1)S(1)} fusion(bf16[3,2,256,128]{3,2,1,0:T(8,128)(2,1)S(1)} %collective-permute-done.22, f32[3,4,2,256,128]{4,3,2,1,0:T(8,128)} %copy-done.6), kind=kLoop, calls=%fused_computation.11 | loop fusion | flops 589824 | bytes 1572864 | tf_op jit(solution)/shard_map/convert_element_type | solution.py:208
  104.3 4.9 %collective-permute-done.26 = bf16[3,2,256,128]{3,2,1,0:T(8,128)(2,1)S(1)} collective-permute-done((bf16[3,2,256,128]{3,2,1,0:T(8,128)(2,1)S(1)}, bf16[3,2,256,128]{3,2,1,0:T(8,128)(2,1)S(1)}, u32[]{:S(2)}, u32[]{:S(2)}) %collective-permute-start.26) | collective-permute-done | bytes 393248 | tf_op jit(solution)/shard_map/ppermute | solution.py:27
  109.7 0.9 copy.42
  110.7 0.9 copy.43
  111.9 0.9 copy.44
  112.8 0.9 copy.45
  (76 shorter events, 4.8 us)
Async XLA Ops:
  0.6 12.3 %collective-permute-start = (s32[2,2]{1,0:T(2,128)}, s32[2,2]{1,0:T(2,128)S(1)}, u32[]{:S(2)}, u32[]{:S(2)}) collective-permute-start(s32[2,2]{1,0:T(2,128)} %bitcast.94), channel_id=1, source_target_pairs={{0,4},{4,0},{8,12},{12,8},{1,5},{5,1},{9,13},{13,9},{2,6},{6,2},{1... | collective-permute-start | bytes 56 | tf_op jit(solution)/shard_map/ppermute | solution.py:27
  5.0 1.5 %copy-start.10 = (bf16[4,8,8,1280]{3,2,1,0:T(8,128)(2,1)S(1)}, bf16[4,8,8,1280]{3,2,1,0:T(8,128)(2,1)}, u32[]{:S(2)}) copy-start(bf16[4,8,8,1280]{3,2,1,0:T(8,128)(2,1)} %param.8) | copy-start | bytes 1966084
  5.1 1.5 %copy-start.11 = (bf16[4,8,8,1280]{3,2,1,0:T(8,128)(2,1)S(1)}, bf16[4,8,8,1280]{3,2,1,0:T(8,128)(2,1)}, u32[]{:S(2)}) copy-start(bf16[4,8,8,1280]{3,2,1,0:T(8,128)(2,1)} %param.7) | copy-start | bytes 1966084
  5.4 1.1 copy-start.8
  6.5 17.0 %collective-permute-start.1 = (bf16[2,2,256,128]{3,2,1,0:T(8,128)(2,1)S(1)}, bf16[2,2,256,128]{3,2,1,0:T(8,128)(2,1)S(1)}, u32[]{:S(2)}, u32[]{:S(2)}) collective-permute-start(bf16[2,2,256,128]{3,2,1,0:T(8,128)(2,1)S(1)} %get-tuple-element.32), channel_id=1, source_target_pairs={{0,4},{4,0},{8,12},{12,8},{1,5},{5,1},{9,13},{13,9},{2,6},{6,2},{1... | collective-permute-start | bytes 786440 | tf_op jit(solution)/shard_map/ppermute | solution.py:27
  7.1 2.1 %copy-start.9 = (bf16[2,4,8,8,10,128]{5,3,2,1,0,4:T(8,128)(2,1)}, bf16[2,4,8,8,10,128]{5,3,2,1,0,4:T(8,128)(2,1)S(1)}, u32[]{:S(2)}) copy-start(bf16[2,4,8,8,10,128]{5,3,2,1,0,4:T(8,128)(2,1)S(1)} %copy.25) | copy-start | bytes 3932164
  7.1 5.8 %copy-start.13 = (s32[2,3]{1,0:T(2,128)S(1)}, s32[2,3]{1,0:T(2,128)}, u32[]{:S(2)}) copy-start(s32[2,3]{1,0:T(2,128)} %constant.49.clone) | copy-start | bytes 76
  7.2 14.2 %collective-permute-start.3 = (bf16[2,2,256,128]{3,2,1,0:T(8,128)(2,1)S(1)}, bf16[2,2,256,128]{3,2,1,0:T(8,128)(2,1)S(1)}, u32[]{:S(2)}, u32[]{:S(2)}) collective-permute-start(bf16[2,2,256,128]{3,2,1,0:T(8,128)(2,1)S(1)} %get-tuple-element.30), channel_id=1, source_target_pairs={{0,4},{4,0},{8,12},{12,8},{1,5},{5,1},{9,13},{13,9},{2,6},{6,2},{1... | collective-permute-start | bytes 786440 | tf_op jit(solution)/shard_map/ppermute | solution.py:27
  9.2 22.6 %collective-permute-start.5 = (bf16[2,2,256,128]{3,2,1,0:T(8,128)(2,1)S(1)}, bf16[2,2,256,128]{3,2,1,0:T(8,128)(2,1)S(1)}, u32[]{:S(2)}, u32[]{:S(2)}) collective-permute-start(bf16[2,2,256,128]{3,2,1,0:T(8,128)(2,1)S(1)} %get-tuple-element.31.own_a), channel_id=1, source_target_pairs={{0,8},{4,12},{8,0},{12,4},{1,9},{5,13},{9,1},{13,5},{2,10},{6,14},... | collective-permute-start | bytes 786440 | tf_op jit(solution)/shard_map/ppermute | solution.py:36
  10.7 22.3 %copy-start.14 = (s32[1,2,2]{2,1,0:T(2,128)S(1)}, s32[1,2,2]{2,1,0:T(2,128)}, u32[]{:S(2)}) copy-start(s32[1,2,2]{2,1,0:T(2,128)} %param.10) | copy-start | bytes 52
  11.9 16.4 %collective-permute-start.11 = (bf16[3,2,256,128]{3,2,1,0:T(8,128)(2,1)S(1)}, bf16[3,2,256,128]{3,2,1,0:T(8,128)(2,1)S(1)}, u32[]{:S(2)}, u32[]{:S(2)}) collective-permute-start(bf16[3,2,256,128]{3,2,1,0:T(8,128)(2,1)S(1)} %get-tuple-element.34), channel_id=1, source_target_pairs={{0,4},{4,0},{8,12},{12,8},{1,5},{5,1},{9,13},{13,9},{2,6},{6,2},{1... | collective-permute-start | bytes 1179656 | tf_op jit(solution)/shard_map/ppermute | solution.py:27
  12.9 10.7 %copy-start.12 = (s32[8]{0:T(128)}, s32[8]{0:T(128)S(1)}, u32[]{:S(2)}) copy-start(s32[8]{0:T(128)S(1)} %and_select_fusion) | copy-start | bytes 100
  12.9 18.9 %collective-permute-start.2 = (bf16[2,2,256,128]{3,2,1,0:T(8,128)(2,1)S(1)}, bf16[2,2,256,128]{3,2,1,0:T(8,128)(2,1)S(1)}, u32[]{:S(2)}, u32[]{:S(2)}) collective-permute-start(bf16[2,2,256,128]{3,2,1,0:T(8,128)(2,1)S(1)} %get-tuple-element.31.own_a), channel_id=1, source_target_pairs={{0,16},{16,0},{1,17},{17,1},{2,18},{18,2},{3,19},{19,3},{4,20},{20... | collective-permute-start | bytes 786440 | tf_op jit(solution)/shard_map/ppermute | solution.py:40
  21.4 11.6 %collective-permute-start.7 = (bf16[2,2,256,128]{3,2,1,0:T(8,128)(2,1)S(1)}, bf16[2,2,256,128]{3,2,1,0:T(8,128)(2,1)}, u32[]{:S(2)}, u32[]{:S(2)}) collective-permute-start(bf16[2,2,256,128]{3,2,1,0:T(8,128)(2,1)S(1)} %collective-permute-done.3.par_a), channel_id=1, source_target_pairs={{0,8},{4,12},{8,0},{12,4},{1,9},{5,13},{9,1},{13,5},{2,10},{6,14},... | collective-permute-start | bytes 786440 | tf_op jit(solution)/shard_map/ppermute | solution.py:36
  23.6 15.5 %collective-permute-start.13 = (bf16[3,2,256,128]{3,2,1,0:T(8,128)(2,1)S(1)}, bf16[3,2,256,128]{3,2,1,0:T(8,128)(2,1)S(1)}, u32[]{:S(2)}, u32[]{:S(2)}) collective-permute-start(bf16[3,2,256,128]{3,2,1,0:T(8,128)(2,1)S(1)} %get-tuple-element.35.own_a), channel_id=1, source_target_pairs={{0,8},{4,12},{8,0},{12,4},{1,9},{5,13},{9,1},{13,5},{2,10},{6,14},... | collective-permute-start | bytes 1179656 | tf_op jit(solution)/shard_map/ppermute | solution.py:36
  28.4 15.3 %collective-permute-start.15 = (bf16[3,2,256,128]{3,2,1,0:T(8,128)(2,1)S(1)}, bf16[3,2,256,128]{3,2,1,0:T(8,128)(2,1)S(1)}, u32[]{:S(2)}, u32[]{:S(2)}) collective-permute-start(bf16[3,2,256,128]{3,2,1,0:T(8,128)(2,1)S(1)} %collective-permute-done.11.par_a), channel_id=1, source_target_pairs={{0,8},{4,12},{8,0},{12,4},{1,9},{5,13},{9,1},{13,5},{2,10},{6,14},... | collective-permute-start | bytes 1179656 | tf_op jit(solution)/shard_map/ppermute | solution.py:36
  31.8 7.3 %collective-permute-start.4 = (bf16[2,2,256,128]{3,2,1,0:T(8,128)(2,1)S(1)}, bf16[2,2,256,128]{3,2,1,0:T(8,128)(2,1)}, u32[]{:S(2)}, u32[]{:S(2)}) collective-permute-start(bf16[2,2,256,128]{3,2,1,0:T(8,128)(2,1)S(1)} %collective-permute-done.3.par_a), channel_id=1, source_target_pairs={{0,16},{16,0},{1,17},{17,1},{2,18},{18,2},{3,19},{19,3},{4,20},{20... | collective-permute-start | bytes 786440 | tf_op jit(solution)/shard_map/ppermute | solution.py:40
  31.8 0.7 copy-start.2
  32.5 6.6 %collective-permute-start.6 = (bf16[2,2,256,128]{3,2,1,0:T(8,128)(2,1)S(1)}, bf16[2,2,256,128]{3,2,1,0:T(8,128)(2,1)S(1)}, u32[]{:S(2)}, u32[]{:S(2)}) collective-permute-start(bf16[2,2,256,128]{3,2,1,0:T(8,128)(2,1)S(1)} %collective-permute-done.5.yown_a), channel_id=1, source_target_pairs={{0,16},{16,0},{1,17},{17,1},{2,18},{18,2},{3,19},{19,3},{4,20},{20... | collective-permute-start | bytes 786440 | tf_op jit(solution)/shard_map/ppermute | solution.py:40
  33.0 7.3 %collective-permute-start.8 = (bf16[2,2,256,128]{3,2,1,0:T(8,128)(2,1)}, bf16[2,2,256,128]{3,2,1,0:T(8,128)(2,1)}, u32[]{:S(2)}, u32[]{:S(2)}) collective-permute-start(bf16[2,2,256,128]{3,2,1,0:T(8,128)(2,1)} %collective-permute-done.7.rel_a), channel_id=1, source_target_pairs={{0,16},{16,0},{1,17},{17,1},{2,18},{18,2},{3,19},{19,3},{4,20},{20... | collective-permute-start | bytes 786440 | tf_op jit(solution)/shard_map/ppermute | solution.py:40
  39.1 18.3 %collective-permute-start.10 = (bf16[3,2,256,128]{3,2,1,0:T(8,128)(2,1)S(1)}, bf16[3,2,256,128]{3,2,1,0:T(8,128)(2,1)S(1)}, u32[]{:S(2)}, u32[]{:S(2)}) collective-permute-start(bf16[3,2,256,128]{3,2,1,0:T(8,128)(2,1)S(1)} %get-tuple-element.35.own_a), channel_id=1, source_target_pairs={{0,16},{16,0},{1,17},{17,1},{2,18},{18,2},{3,19},{19,3},{4,20},{20... | collective-permute-start | bytes 1179656 | tf_op jit(solution)/shard_map/ppermute | solution.py:40
  39.1 17.7 %collective-permute-start.9 = (bf16[3,2,256,128]{3,2,1,0:T(8,128)(2,1)}, bf16[3,2,256,128]{3,2,1,0:T(8,128)(2,1)S(1)}, u32[]{:S(2)}, u32[]{:S(2)}) collective-permute-start(bf16[3,2,256,128]{3,2,1,0:T(8,128)(2,1)} %get-tuple-element.36), channel_id=1, source_target_pairs={{0,4},{4,0},{8,12},{12,8},{1,5},{5,1},{9,13},{13,9},{2,6},{6,2},{1... | collective-permute-start | bytes 1179656 | tf_op jit(solution)/shard_map/ppermute | solution.py:27
  39.1 0.7 copy-start.4
  39.8 17.5 %collective-permute-start.12 = (bf16[3,2,256,128]{3,2,1,0:T(8,128)(2,1)S(1)}, bf16[3,2,256,128]{3,2,1,0:T(8,128)(2,1)S(1)}, u32[]{:S(2)}, u32[]{:S(2)}) collective-permute-start(bf16[3,2,256,128]{3,2,1,0:T(8,128)(2,1)S(1)} %collective-permute-done.11.par_a), channel_id=1, source_target_pairs={{0,16},{16,0},{1,17},{17,1},{2,18},{18,2},{3,19},{19,3},{4,20},{20... | collective-permute-start | bytes 1179656 | tf_op jit(solution)/shard_map/ppermute | solution.py:40
  40.3 17.0 %collective-permute-start.14 = (bf16[3,2,256,128]{3,2,1,0:T(8,128)(2,1)S(1)}, bf16[3,2,256,128]{3,2,1,0:T(8,128)(2,1)S(1)}, u32[]{:S(2)}, u32[]{:S(2)}) collective-permute-start(bf16[3,2,256,128]{3,2,1,0:T(8,128)(2,1)S(1)} %collective-permute-done.13.yown_a), channel_id=1, source_target_pairs={{0,16},{16,0},{1,17},{17,1},{2,18},{18,2},{3,19},{19,3},{4,20},{20... | collective-permute-start | bytes 1179656 | tf_op jit(solution)/shard_map/ppermute | solution.py:40
  43.6 13.7 %collective-permute-start.16 = (bf16[3,2,256,128]{3,2,1,0:T(8,128)(2,1)S(1)}, bf16[3,2,256,128]{3,2,1,0:T(8,128)(2,1)S(1)}, u32[]{:S(2)}, u32[]{:S(2)}) collective-permute-start(bf16[3,2,256,128]{3,2,1,0:T(8,128)(2,1)S(1)} %collective-permute-done.15.rel_a), channel_id=1, source_target_pairs={{0,16},{16,0},{1,17},{17,1},{2,18},{18,2},{3,19},{19,3},{4,20},{20... | collective-permute-start | bytes 1179656 | tf_op jit(solution)/shard_map/ppermute | solution.py:40
  44.4 1.0 copy-start.3
  45.4 0.9 copy-start.5
  56.7 14.7 %copy-start = (bf16[2,2,256,128]{3,2,1,0:T(8,128)(2,1)}, bf16[2,2,256,128]{3,2,1,0:T(8,128)(2,1)S(1)}, u32[]{:S(2)}) copy-start(bf16[2,2,256,128]{3,2,1,0:T(8,128)(2,1)S(1)} %get-tuple-element.14) | copy-start | bytes 786436
  56.8 14.7 %collective-permute-start.19 = (bf16[2,4,2,256,128]{4,3,2,1,0:T(8,128)(2,1)S(1)}, bf16[2,4,2,256,128]{4,3,2,1,0:T(8,128)(2,1)S(1)}, u32[]{:S(2)}, u32[]{:S(2)}) collective-permute-start(bf16[2,4,2,256,128]{4,3,2,1,0:T(8,128)(2,1)S(1)} %get-tuple-element.17), channel_id=1, source_target_pairs={{0,16},{16,0},{1,17},{17,1},{2,18},{18,2},{3,19},{19,3},{4,20},{20... | collective-permute-start | bytes 3145736 | tf_op jit(solution)/shard_map/ppermute | solution.py:40
  71.4 3.5 %collective-permute-start.21 = (bf16[3,4,2,256,128]{4,3,2,1,0:T(8,128)(2,1)S(1)}, bf16[3,4,2,256,128]{4,3,2,1,0:T(8,128)(2,1)S(1)}, u32[]{:S(2)}, u32[]{:S(2)}) collective-permute-start(bf16[3,4,2,256,128]{4,3,2,1,0:T(8,128)(2,1)S(1)} %get-tuple-element.19), channel_id=1, source_target_pairs={{0,16},{16,0},{1,17},{17,1},{2,18},{18,2},{3,19},{19,3},{4,20},{20... | collective-permute-start | bytes 4718600 | tf_op jit(solution)/shard_map/ppermute | solution.py:40
  71.7 3.2 %copy-start.7 = (f32[2,4,2,256,128]{4,3,2,1,0:T(8,128)}, f32[2,4,2,256,128]{4,3,2,1,0:T(8,128)S(1)}, u32[]{:S(2)}) copy-start(f32[2,4,2,256,128]{4,3,2,1,0:T(8,128)S(1)} %convert_add_fusion.1) | copy-start | bytes 6291460
  71.8 9.6 %collective-permute-start.23 = (bf16[2,2,256,128]{3,2,1,0:T(8,128)(2,1)S(1)}, bf16[2,2,256,128]{3,2,1,0:T(8,128)(2,1)S(1)}, u32[]{:S(2)}, u32[]{:S(2)}) collective-permute-start(bf16[2,2,256,128]{3,2,1,0:T(8,128)(2,1)S(1)} %get-tuple-element.39), channel_id=1, source_target_pairs={{0,8},{4,12},{8,0},{12,4},{1,9},{5,13},{9,1},{13,5},{2,10},{6,14},... | collective-permute-start | bytes 786440 | tf_op jit(solution)/shard_map/ppermute | solution.py:36
  75.3 1.6 %copy-start.6 = (f32[3,4,2,256,128]{4,3,2,1,0:T(8,128)}, f32[3,4,2,256,128]{4,3,2,1,0:T(8,128)S(1)}, u32[]{:S(2)}) copy-start(f32[3,4,2,256,128]{4,3,2,1,0:T(8,128)S(1)} %convert_add_fusion) | copy-start | bytes 9437188
  76.9 1.7 %copy-start.1 = (bf16[2,2,256,128]{3,2,1,0:T(8,128)(2,1)S(1)}, bf16[2,2,256,128]{3,2,1,0:T(8,128)(2,1)}, u32[]{:S(2)}) copy-start(bf16[2,2,256,128]{3,2,1,0:T(8,128)(2,1)} %copy-done) | copy-start | bytes 786436
  77.1 12.3 %collective-permute-start.25 = (bf16[3,2,256,128]{3,2,1,0:T(8,128)(2,1)S(1)}, bf16[3,2,256,128]{3,2,1,0:T(8,128)(2,1)S(1)}, u32[]{:S(2)}, u32[]{:S(2)}) collective-permute-start(bf16[3,2,256,128]{3,2,1,0:T(8,128)(2,1)S(1)} %get-tuple-element.21), channel_id=1, source_target_pairs={{0,8},{4,12},{8,0},{12,4},{1,9},{5,13},{9,1},{13,5},{2,10},{6,14},... | collective-permute-start | bytes 1179656 | tf_op jit(solution)/shard_map/ppermute | solution.py:36
  78.6 25.6 %collective-permute-start.17 = (bf16[2,2,256,128]{3,2,1,0:T(8,128)(2,1)S(1)}, bf16[2,2,256,128]{3,2,1,0:T(8,128)(2,1)S(1)}, u32[]{:S(2)}, u32[]{:S(2)}) collective-permute-start(bf16[2,2,256,128]{3,2,1,0:T(8,128)(2,1)S(1)} %copy-done.1), channel_id=1, source_target_pairs={{0,4},{4,0},{8,12},{12,8},{1,5},{5,1},{9,13},{13,9},{2,6},{6,2},{1... | collective-permute-start | bytes 786440 | tf_op jit(solution)/shard_map/ppermute | solution.py:27
  79.2 25.1 %collective-permute-start.18 = (bf16[3,2,256,128]{3,2,1,0:T(8,128)(2,1)S(1)}, bf16[3,2,256,128]{3,2,1,0:T(8,128)(2,1)S(1)}, u32[]{:S(2)}, u32[]{:S(2)}) collective-permute-start(bf16[3,2,256,128]{3,2,1,0:T(8,128)(2,1)S(1)} %get-tuple-element.15), channel_id=1, source_target_pairs={{0,4},{4,0},{8,12},{12,8},{1,5},{5,1},{9,13},{13,9},{2,6},{6,2},{1... | collective-permute-start | bytes 1179656 | tf_op jit(solution)/shard_map/ppermute | solution.py:27
  80.7 14.3 %collective-permute-start.20 = (bf16[2,2,256,128]{3,2,1,0:T(8,128)(2,1)S(1)}, bf16[2,2,256,128]{3,2,1,0:T(8,128)(2,1)S(1)}, u32[]{:S(2)}, u32[]{:S(2)}) collective-permute-start(bf16[2,2,256,128]{3,2,1,0:T(8,128)(2,1)S(1)} %get-tuple-element.38), channel_id=1, source_target_pairs={{0,8},{4,12},{8,0},{12,4},{1,9},{5,13},{9,1},{13,5},{2,10},{6,14},... | collective-permute-start | bytes 786440 | tf_op jit(solution)/shard_map/ppermute | solution.py:36
  82.5 21.7 %collective-permute-start.24 = (bf16[2,2,256,128]{3,2,1,0:T(8,128)(2,1)S(1)}, bf16[2,2,256,128]{3,2,1,0:T(8,128)(2,1)S(1)}, u32[]{:S(2)}, u32[]{:S(2)}) collective-permute-start(bf16[2,2,256,128]{3,2,1,0:T(8,128)(2,1)S(1)} %fusion.5), channel_id=1, source_target_pairs={{0,4},{4,0},{8,12},{12,8},{1,5},{5,1},{9,13},{13,9},{2,6},{6,2},{1... | collective-permute-start | bytes 786440 | tf_op jit(solution)/shard_map/ppermute | solution.py:27
  89.4 13.6 %collective-permute-start.22 = (bf16[3,2,256,128]{3,2,1,0:T(8,128)(2,1)S(1)}, bf16[3,2,256,128]{3,2,1,0:T(8,128)(2,1)S(1)}, u32[]{:S(2)}, u32[]{:S(2)}) collective-permute-start(bf16[3,2,256,128]{3,2,1,0:T(8,128)(2,1)S(1)} %get-tuple-element.20), channel_id=1, source_target_pairs={{0,8},{4,12},{8,0},{12,4},{1,9},{5,13},{9,1},{13,5},{2,10},{6,14},... | collective-permute-start | bytes 1179656 | tf_op jit(solution)/shard_map/ppermute | solution.py:36
  95.0 14.2 %collective-permute-start.26 = (bf16[3,2,256,128]{3,2,1,0:T(8,128)(2,1)S(1)}, bf16[3,2,256,128]{3,2,1,0:T(8,128)(2,1)S(1)}, u32[]{:S(2)}, u32[]{:S(2)}) collective-permute-start(bf16[3,2,256,128]{3,2,1,0:T(8,128)(2,1)S(1)} %fusion.1), channel_id=1, source_target_pairs={{0,4},{4,0},{8,12},{12,8},{1,5},{5,1},{9,13},{13,9},{2,6},{6,2},{1... | collective-permute-start | bytes 1179656 | tf_op jit(solution)/shard_map/ppermute | solution.py:27

commit v2 on v1

v2 whole, which is shorter than its diff:
```python
import math

import jax
import jax.numpy as jnp
from jax import lax
from jax.experimental import pallas as pl
from jax.experimental.pallas import tpu as pltpu
from jax.sharding import PartitionSpec as P

HD = 128
TILE = 4
MASKED = -1e30
FIRST_HEADS = 2
LAST_HEADS = 1

LAST = (((1,), (1,)), ((), ()))
FIRST = (((0,), (0,)), ((), ()))
PLAIN = (((1,), (0,)), ((), ()))


def dot(a, b, dims):
    return lax.dot_general(a, b, dims, preferred_element_type=jnp.float32)


def to_partner(block):
    count = lax.axis_size("lon")
    return lax.ppermute(block, "lon", [(i, i ^ 1) for i in range(count)])


def to_far(block, outward):
    count = lax.axis_size("lon")
    route = []
    for i in range(count):
        step = 2 if (i % 2 == 0) == outward else -2
        route.append((i, (i + step) % count))
    return lax.ppermute(block, "lon", route)


def to_twin(block):
    return lax.ppermute(block, "tm", [(0, 1), (1, 0)])


class Order:
    def __init__(self):
        self.token = jnp.zeros((), jnp.float32)

    def gate(self, value):
        return lax.optimization_barrier((self.token, value))[1]

    def passed(self, *values):
        self.token, *values = lax.optimization_barrier((self.token, *values))
        return values if len(values) > 1 else values[0]


def attention_kernel(
    bias_ref,
    own_q,
    par_q,
    own_a,
    own_b,
    par_a,
    par_b,
    yown_a,
    yown_b,
    rel_a,
    rel_b,
    own_out,
    par_out,
    near_own,
    near_par,
    near_far,
    near_rel,
    twin_stay,
    twin_send,
    key_ref,
    value_ref,
    scores_ref,
    probs_ref,
    dprobs_ref,
    grad_ref,
):
    rows = own_q.shape[2]
    lon = bias_ref.shape[2]
    scale = 1.0 / math.sqrt(HD)
    factor = math.log2(math.e) * scale
    ring = (rel_a, rel_b, own_a, own_b, par_a, par_b, yown_a, yown_b)
    for at, ref in enumerate(ring):
        key_ref[at] = ref[0, 0]
        value_ref[at] = ref[0, 1]
    span = 6
    for which, (q_ref, out_ref) in enumerate(((own_q, own_out), (par_q, par_out))):
        first = 2 * which
        query = q_ref[0, 0]
        grad = q_ref[0, 1]
        peak = None
        for at in range(span):
            score = dot(key_ref[first + at], query, LAST)
            score = score.reshape(rows // lon, lon, rows) + bias_ref[which, at // 2][None]
            scores_ref[at] = score.reshape(rows, rows)
            top = jnp.max(score, axis=0)
            peak = top if peak is None else jnp.maximum(peak, top)
        peak = jnp.max(peak, axis=0, keepdims=True)
        total = jnp.zeros((lon, rows), jnp.float32)
        attended = jnp.zeros((HD, rows), jnp.float32)
        for at in range(span):
            expo = jnp.exp2((scores_ref[at] - peak) * factor)
            total += jnp.sum(expo.reshape(rows // lon, lon, rows), axis=0)
            probs = expo.astype(jnp.bfloat16)
            probs_ref[at] = probs
            attended += dot(value_ref[first + at], probs, FIRST)
            dprobs_ref[at] = dot(value_ref[first + at], grad, LAST)
        inverse = 1.0 / jnp.sum(total, axis=0, keepdims=True)
        column = jnp.broadcast_to(inverse, (HD, rows)).T
        query_part = (query.astype(jnp.float32) * (column * scale)).astype(jnp.bfloat16)
        grad_part = (grad.astype(jnp.float32) * column).astype(jnp.bfloat16)
        attended = (attended * inverse).astype(jnp.bfloat16)
        out_ref[0, 0] = attended.T
        product = grad.T.astype(jnp.float32) * attended.astype(jnp.float32)
        delta = jnp.sum(product, axis=0, keepdims=True)
        query_grad = jnp.zeros((HD, rows), jnp.float32)
        for at in range(span):
            probs = probs_ref[at]
            dscores = probs.astype(jnp.float32) * (dprobs_ref[at] - delta)
            dscores = dscores.astype(jnp.bfloat16)
            query_grad += dot(key_ref[first + at], dscores, FIRST)
            key_part = dot(dscores, query_part, PLAIN)
            value_part = dot(probs, grad_part, PLAIN)
            if which == 0 or at >= 4:
                grad_ref[first + at, 0] = key_part
                grad_ref[first + at, 1] = value_part
            else:
                grad_ref[first + at, 0] += key_part
                grad_ref[first + at, 1] += value_part
        out_ref[0, 1] = (query_grad * (inverse * scale)).T.astype(jnp.bfloat16)
    for b, (at, near_ref) in enumerate(((2, near_own), (4, near_par), (6, near_far), (0, near_rel))):
        near_ref[0] = grad_ref[at].astype(jnp.bfloat16)
        twin_ref = twin_stay if b < 2 else twin_send
        twin_ref[b % 2, 0] = grad_ref[at + 1].astype(jnp.bfloat16)


def attention(bias, own_q, partner_q, blocks, low, skip, heads):
    rows = own_q.shape[2]
    here = pl.BlockSpec((1, 2, rows, HD), lambda h: (h + low, 0, 0, 0))
    there = pl.BlockSpec((1, 2, rows, HD), lambda h: (h + skip, 0, 0, 0))
    one = pl.BlockSpec((1, 2, rows, HD), lambda h: (h, 0, 0, 0))
    whole = pl.BlockSpec(bias.shape, lambda h: (0, 0, 0, 0))
    flat = [part for pair in blocks for part in pair]
    pairs = (heads, 2, rows, HD)
    spread = (2, heads, 2, rows, HD)
    per_head = pl.BlockSpec((2, 1, 2, rows, HD), lambda h: (0, h, 0, 0, 0))
    operands = [pltpu.with_memory_space_constraint(x, pltpu.HBM) for x in (own_q, partner_q, *flat[:-1])]
    operands.append(pltpu.with_memory_space_constraint(flat[-1], pltpu.VMEM))
    return pl.pallas_call(
        attention_kernel,
        grid=(heads,),
        in_specs=[whole, here, there, here, here, there, there, here, here, there, there],
        out_specs=[one] * 6 + [per_head] * 2,
        out_shape=[
            pltpu.HBM(shape, jnp.bfloat16) for shape in [pairs] * 6 + [spread] * 2
        ],
        scratch_shapes=[
            pltpu.VMEM((8, rows, HD), jnp.bfloat16),
            pltpu.VMEM((8, rows, HD), jnp.bfloat16),
            pltpu.VMEM((6, rows, rows), jnp.float32),
            pltpu.VMEM((6, rows, rows), jnp.bfloat16),
            pltpu.VMEM((6, rows, rows), jnp.float32),
            pltpu.VMEM((8, 2, rows, HD), jnp.float32),
        ],
        compiler_params=pltpu.CompilerParams(vmem_limit_bytes=18 * 1024 * 1024),
        cost_estimate=pl.CostEstimate(
            flops=heads * 2 * 6 * 6 * 2 * rows * rows * HD, bytes_accessed=heads * 28 * rows * HD * 2, transcendentals=0
        ),
        name="attention",
    )(bias, *operands)


def window_bias(offsets, side, frames, lats, lons):
    lat_tiles, lon_tiles = offsets.shape[1:]
    per_row = jnp.repeat(jnp.repeat(offsets, TILE, axis=1), TILE, axis=2)
    centre = per_row + (jnp.arange(lons) // TILE)[None, None, :]
    centre = jnp.broadcast_to(centre[:, None], (2, frames, lats, lons)).reshape(2, -1)
    sign = 1 - 2 * side
    place = jnp.arange(lons) // TILE
    shift = jnp.array([[-1, 0, 1], [-1, 0, 1]], jnp.int32) * sign * lon_tiles
    column = shift[:, :, None] + place[None, None, :]
    near = jnp.abs(column[:, :, :, None] - centre[:, None, None, :]) <= 1
    return jnp.where(near, 0.0, MASKED).astype(jnp.float32)


def on_device(query_rows, key_rows, value_rows, out_grad, window_offsets):
    frames, lats, lons, width = query_rows.shape
    heads = width // HD
    half = heads // 2
    rows = frames * lats * lons
    frame_tiles = frames // TILE * lax.axis_size("tm")
    if lax.axis_size("tm") != 2 or frame_tiles > 2 or lats // TILE > 2 or lons != 2 * TILE or heads % 2:
        raise ValueError("unsupported block")
    side = lax.axis_index("lon") % 2

    def by_head(*arrays):
        pair = jnp.stack(arrays).reshape(len(arrays), frames, lats, lons, heads, HD)
        return pair.transpose(4, 0, 1, 2, 3, 5).reshape(heads, len(arrays), rows, HD)

    def half_of(array, which):
        return lax.dynamic_slice_in_dim(array, which * half, half, 0)

    key_value = by_head(key_rows, value_rows)
    mine_kv, theirs_kv = half_of(key_value, side), half_of(key_value, 1 - side)
    query_grad = by_head(query_rows, out_grad)
    mine_qg, theirs_qg = half_of(query_grad, side), half_of(query_grad, 1 - side)
    offsets = window_offsets.reshape(lats // TILE, lons // TILE)

    first = min(FIRST_HEADS, half - 1)
    last = half - min(LAST_HEADS, half - first)
    order = Order()
    far = to_far(mine_kv, False)
    partner_0 = to_partner(theirs_kv[:first])
    both = to_partner(order.gate(offsets))
    partner_1 = to_partner(theirs_kv[first:])
    own_b = to_twin(mine_kv)
    partner_0 = order.passed(partner_0)
    relay_0 = to_far(order.gate(partner_0), True)
    part_q0 = to_partner(order.gate(theirs_qg[:first]))
    relay_0, part_q0, far, partner_1, both, own_b = order.passed(relay_0, part_q0, far, partner_1, both, own_b)
    bias = window_bias(jnp.stack([offsets, both]), side, frames, lats, lons)
    relay_0b = to_twin(order.gate(relay_0))
    far_b = to_twin(order.gate(far))
    partner_0b = to_twin(order.gate(partner_0))
    relay_1 = to_far(order.gate(partner_1), True)
    part_q1 = to_partner(order.gate(theirs_qg[first:]))
    relay_0b, partner_0b, far_b = order.passed(relay_0b, partner_0b, far_b)
    partner_1b = to_twin(order.gate(partner_1))

    def compute(low, high, partner, relay, part_q):
        skip = low - (first if low else 0)
        blocks = [(mine_kv, own_b), partner, (far, far_b), relay]
        return attention(order.gate(bias), mine_qg, part_q, blocks, low, skip, high - low)

    def total(near, twin, block):
        return near[block] + twin[block % 2].astype(jnp.float32)

    def rounded(near, twin, block):
        return total(near, twin, block).astype(jnp.bfloat16)

    def theirs_total(near, twin, back):
        return (total(near, twin, 1) + back.astype(jnp.float32)).astype(jnp.bfloat16)

    def send_back(near, twin):
        relayed, ahead = rounded(near, twin, 3), rounded(near, twin, 2)
        if lax.axis_size("lon") == 4:
            return to_far(jnp.stack([relayed, ahead]), True)
        return to_far(relayed, False), to_far(ahead, True)

    done_0, out_0, *near_0, stay_0, send_0 = compute(
        0, first, (partner_0, partner_0b), (relay_0, relay_0b), part_q0
    )
    send_0, relay_1, part_q1, partner_1b = order.passed(send_0, relay_1, part_q1, partner_1b)
    send_0 = to_twin(order.gate(send_0))
    relay_1b = to_twin(order.gate(relay_1))
    send_0, relay_1b = order.passed(send_0, relay_1b)
    back_0, ahead_0 = send_back(near_0, send_0)
    back_out_0 = to_partner(order.gate(out_0))
    stay_0 = to_twin(order.gate(stay_0))

    rest = (partner_1, partner_1b), (relay_1, relay_1b), part_q1
    done_1, out_1, *near_1, stay_1, send_1 = compute(first, last, *rest)
    send_1, back_0, ahead_0, back_out_0, stay_0 = order.passed(send_1, back_0, ahead_0, back_out_0, stay_0)
    send_1 = to_twin(order.gate(send_1))
    theirs_0 = theirs_total(near_0, stay_0, order.gate(back_0))
    mixed_1 = to_partner(jnp.concatenate([theirs_0, order.gate(out_1)]))
    send_1 = order.passed(send_1)
    back_1, ahead_1 = send_back(near_1, send_1)
    stay_1 = to_twin(order.gate(stay_1))

    done_2, out_2, *near_2, stay_2, send_2 = compute(last, half, *rest)
    send_2 = order.passed(send_2)
    send_2 = to_twin(order.gate(send_2))
    send_2, back_1, ahead_1, mixed_1, stay_1 = order.passed(send_2, back_1, ahead_1, mixed_1, stay_1)
    back_2 = to_far(rounded(near_2, send_2, 3), False)
    theirs_1 = theirs_total(near_1, stay_1, order.gate(back_1))
    mixed_2 = to_partner(jnp.concatenate([theirs_1, order.gate(out_2)]))
    stay_2 = to_twin(order.gate(stay_2))
    back_2, stay_2 = order.passed(back_2, stay_2)
    theirs_2 = to_partner(theirs_total(near_2, stay_2, order.gate(back_2)))
    ahead_2 = to_far(order.gate(rounded(near_2, send_2, 2)), True)

    theirs_0, back_out_1 = mixed_1[:first], mixed_1[first:]
    theirs_1, back_out_2 = mixed_2[: last - first], mixed_2[last - first :]
    def assembled(mine, theirs):
        mine, theirs = jnp.concatenate(mine), jnp.concatenate(theirs)
        low = jnp.where(side == 0, mine, theirs)
        high = jnp.where(side == 0, theirs, mine)
        array = jnp.concatenate([low, high])
        shaped = array.reshape(heads, 2, frames, lats, lons, HD).transpose(1, 2, 3, 4, 0, 5)
        shaped = shaped.reshape(2, frames, lats, lons, width)
        return shaped[0], shaped[1]

    attended, query_out = assembled((done_0, done_1, done_2), (back_out_0, back_out_1, back_out_2))
    theirs_2, ahead_2, attended, query_out = order.passed(theirs_2, ahead_2, attended, query_out)
    mine = [
        (total(near, twin, 0) + ahead.astype(jnp.float32)).astype(jnp.bfloat16)
        for near, twin, ahead in ((near_0, stay_0, ahead_0), (near_1, stay_1, ahead_1), (near_2, stay_2, ahead_2))
    ]
    key_out, value_out = assembled(mine, (theirs_0, theirs_1, theirs_2))
    return attended, query_out, key_out, value_out


def solution(mesh):
    rows = P("tm", None, "lon", "head")
    return jax.shard_map(
        on_device,
        mesh=mesh,
        in_specs=(rows, rows, rows, rows, P("tm", None, "lon")),
        out_specs=(rows, rows, rows, rows),
        check_vma=False,
    )
```

time: 114 us -> 99.6 us (0.87)
  local copies, waits for them, and re-layouts: 16 us -> 7.16 us
  waiting for transfers between devices: 41.3 us -> 38.4 us
  other arithmetic: 9.42 us -> 6.62 us
  starting transfers between devices: 21.7 us -> 20.1 us
  Pallas kernels: 24.5 us -> 25.8 us
    ppermute x8 -> x7, waiting for transfers between devices: 22.2 us -> 8.79 us  [to_far(): return lax.ppermute(block, 'lon', route)]
    ppermute x9, waiting for transfers between devices: 17.6 us -> 24.6 us  [to_partner(): return lax.ppermute(block, 'lon', [(i, i ^ 1) for i in range(count)])]
    unnamed x30 -> x54, local copies, waits for them, and re-layouts: 5.98 us -> 0.71 us
    ppermute x10 -> x12, waiting for transfers between devices: 1.5 us -> 5.08 us  [to_twin(): return lax.ppermute(block, 'tm', [(0, 1), (1, 0)])]
    ppermute x8 -> x7, starting transfers between devices: 10.5 us -> 7.24 us  [to_far(): return lax.ppermute(block, 'lon', route)]
    convert_element_type x4 -> x5, other arithmetic: 4.62 us -> 1.61 us  [the longest x1 1.08 us: rounded(): return total(near, twin, block).astype(jnp.bfloat16)]
    another operation x3 -> x7, other arithmetic: 1.53 us -> 4.1 us  [the longest x4 2.57 us: send_back(): return to_far(jnp.stack([relayed, ahead]), True)]
    slice x4 -> x7, local copies, waits for them, and re-layouts: 3.17 us -> 0.9 us  [the longest x1 0.77 us: on_device(): partner_1 = to_partner(theirs_kv[first:])]
  transfers between devices with their start and end apart: 27 -> 28, of which waited for: 9 -> 12; matrix products, arithmetic and copies ran while one was open for 13% -> 5% of each run, Pallas kernels for 21% -> 26%
where the time goes in v2:
time: 99.6 us; the launch traced here: 99.3 us
  waiting for transfers between devices  38.4 us (39%)
  Pallas kernels  25.8 us (26%)
  starting transfers between devices  20.1 us (20%)
  local copies, waits for them, and re-layouts  7.16 us (7%)
  other arithmetic  6.62 us (7%)
  between operations  1.21 us (1%)
    pallas_call x3, Pallas kernels, attention(): pl.pallas_call(attention_kernel, grid=(heads,), in_specs=[whole, here, th...  25.8 us
    ppermute x9, waiting for transfers between devices, to_partner(): return lax.ppermute(block, 'lon', [(i, i ^ 1) for i in range(count)])  24.6 us
    ppermute x9, starting transfers between devices, to_partner(): return lax.ppermute(block, 'lon', [(i, i ^ 1) for i in range(count)])  10.3 us
    ppermute x7, waiting for transfers between devices, to_far(): return lax.ppermute(block, 'lon', route)  8.79 us
    ppermute x7, starting transfers between devices, to_far(): return lax.ppermute(block, 'lon', route)  7.24 us
    ppermute x12, waiting for transfers between devices, to_twin(): return lax.ppermute(block, 'tm', [(0, 1), (1, 0)])  5.08 us
    another operation x4, other arithmetic, send_back(): return to_far(jnp.stack([relayed, ahead]), True)  2.57 us
    ppermute x12, starting transfers between devices, to_twin(): return lax.ppermute(block, 'tm', [(0, 1), (1, 0)])  2.56 us
  transfers between devices with their start and end apart: 28, of which 12 were waited for; matrix products, arithmetic and copies ran while one was open for 5% of the time, Pallas kernels for 26%

profile of v2, /device:TPU:0, one launch (start us, length us, event | category | flops | bytes accessed | tf_op | source)
XLA Modules:
  0.0 99.3 jit_solution(11177457189627042664)
XLA Ops:
  0.6 1.4 %pad_maximum_fusion = bf16[2,4,8,8,10,128]{5,3,4,2,1,0:T(8,128)(2,1)S(1)} fusion(bf16[1,4,8,8,10,128]{5,3,4,2,1,0:T(8,128)(2,1)} %bitcast.106, bf16[1,4,8,8,10,128]{5,3,4,2,1,0:T(8,128)(2,1)} %bitcast.107), kind=kLoop, calls=%fused_computation | loop fusion | flops 655360 | bytes 2621440 | tf_op jit(solution)/shard_map/stack | solution.py:201
  2.1 0.4 copy.20
  2.5 0.5 collective-permute-start.6
  3.1 2.6 %collective-permute-start.3 = (bf16[5,2,256,128]{3,2,1,0:T(8,128)(2,1)S(1)}, bf16[5,2,256,128]{3,2,1,0:T(8,128)(2,1)}, u32[]{:S(2)}, u32[]{:S(2)}) collective-permute-start(bf16[5,2,256,128]{3,2,1,0:T(8,128)(2,1)S(1)} %constant_dynamic-slice_fusion.3.own_a), channel_id=1, source_target_pairs={{0,8},{4,12},{8,0},{12,4},{1,9},{5,13},{9,1},{13,5},{2,10},{6,14},... | collective-permute-start | bytes 1966088 | tf_op jit(solution)/shard_map/ppermute | solution.py:36
  5.7 1.5 %collective-permute-start.5 = (s32[2,2]{1,0:T(2,128)S(1)}, s32[2,2]{1,0:T(2,128)S(1)}, u32[]{:S(2)}, u32[]{:S(2)}) collective-permute-start(s32[2,2]{1,0:T(2,128)S(1)} %bitcast.120), channel_id=1, source_target_pairs={{0,4},{4,0},{8,12},{12,8},{1,5},{5,1},{9,13},{13,9},{2,6},{6,2},{1... | collective-permute-start | bytes 56 | tf_op jit(solution)/shard_map/ppermute | solution.py:27
  7.2 0.6 collective-permute-start
  7.8 0.8 constant_dynamic-slice_fusion.5
  8.5 1.5 %collective-permute-start.4 = (bf16[3,2,256,128]{3,2,1,0:T(8,128)(2,1)}, bf16[3,2,256,128]{3,2,1,0:T(8,128)(2,1)S(1)}, u32[]{:S(2)}, u32[]{:S(2)}) collective-permute-start(bf16[3,2,256,128]{3,2,1,0:T(8,128)(2,1)} %constant_dynamic-slice_fusion.5), channel_id=1, source_target_pairs={{0,4},{4,0},{8,12},{12,8},{1,5},{5,1},{9,13},{13,9},{2,6},{6,2},{1... | collective-permute-start | bytes 1179656 | tf_op jit(solution)/shard_map/ppermute | solution.py:27
  10.2 0.4 copy.21
  10.6 0.9 constant_dynamic-slice_fusion.2.own_q
  11.5 5.0 %collective-permute-done.par_a = bf16[2,2,256,128]{3,2,1,0:T(8,128)(2,1)} collective-permute-done((bf16[2,2,256,128]{3,2,1,0:T(8,128)(2,1)S(1)}, bf16[2,2,256,128]{3,2,1,0:T(8,128)(2,1)}, u32[]{:S(2)}, u32[]{:S(2)}) %collective-permute-start) | collective-permute-done | bytes 262176 | tf_op jit(solution)/shard_map/ppermute | solution.py:27
  16.5 0.5 collective-permute-start.2
  17.1 0.5 collective-permute-start.1
  17.6 7.3 %collective-permute-done.4.par_a = bf16[3,2,256,128]{3,2,1,0:T(8,128)(2,1)S(1)} collective-permute-done((bf16[3,2,256,128]{3,2,1,0:T(8,128)(2,1)}, bf16[3,2,256,128]{3,2,1,0:T(8,128)(2,1)S(1)}, u32[]{:S(2)}, u32[]{:S(2)}) %collective-permute-start.4) | collective-permute-done | bytes 393248 | tf_op jit(solution)/shard_map/ppermute | solution.py:27
  24.9 4.5 %collective-permute-done.2.par_q = bf16[2,2,256,128]{3,2,1,0:T(8,128)(2,1)S(1)} collective-permute-done((bf16[2,2,256,128]{3,2,1,0:T(8,128)(2,1)S(1)}, bf16[2,2,256,128]{3,2,1,0:T(8,128)(2,1)S(1)}, u32[]{:S(2)}, u32[]{:S(2)}) %collective-permute-start.2) | collective-permute-done | bytes 262176 | tf_op jit(solution)/shard_map/ppermute | solution.py:27
  29.6 0.5 collective-permute-start.8
  30.7 0.6 collective-permute-start.11
  31.3 0.3 collective-permute-start.10
  31.5 1.0 collective-permute-done.8.par_b
  32.8 0.4 copy-done.26
  33.4 9.9 %attention.3 = (bf16[2,2,256,128]{3,2,1,0:T(8,128)(2,1)}, bf16[2,2,256,128]{3,2,1,0:T(8,128)(2,1)}, bf16[2,2,256,128]{3,2,1,0:T(8,128)(2,1)}, bf16[2,2,256,128]{...) custom-call(f32[2,3,8,256]{3,2,1,0:T(8,128)S(1)} %fusion.22.bias_ref, ...), custom_call_target="tpu_custom_call" | custom-call | flops 2415919104 | bytes 3670016 | tf_op jit(solution)/shard_map/attention/pallas_call | solution.py:153
  43.6 0.4 collective-permute-start.14
  44.0 2.0 %collective-permute-done.14.rel_b = bf16[3,2,256,128]{3,2,1,0:T(8,128)(2,1)S(1)} collective-permute-done((bf16[3,2,256,128]{3,2,1,0:T(8,128)(2,1)S(1)}, bf16[3,2,256,128]{3,2,1,0:T(8,128)(2,1)S(1)}, u32[]{:S(2)}, u32[]{:S(2)}) %collective-permute-start.14) | collective-permute-done | bytes 393248 | tf_op jit(solution)/shard_map/ppermute | solution.py:40
  46.0 1.2 %fusion.12 = (bf16[1,2,2,256,128]{4,3,2,1,0:T(8,128)(2,1)S(1)}, bf16[1,2,2,256,128]{4,3,2,1,0:T(8,128)(2,1)S(1)}) fusion(bf16[2,2,256,128]{3,2,1,0:T(8,128)(2,1)} %get-tuple-element.132, bf16[2,2,2,256,128]{4,3,2,1,0:T(8,128)(2,1)S(1)} %collective-permute-done.13, bf16[2,2,256,128]{3,2,1,0:T(8,128)(2,1)} %get-tuple-element.134), kind=kLoop, calls=%fused_computation.40 | loop fusion | flops 1048576 | bytes 1572864 | tf_op jit(solution)/shard_map/stack | solution.py:251
  47.3 0.8 collective-permute-start.15
  48.2 1.6 %collective-permute-start.16 = (bf16[2,2,256,128]{3,2,1,0:T(8,128)(2,1)S(1)}, bf16[2,2,256,128]{3,2,1,0:T(8,128)(2,1)S(1)}, u32[]{:S(2)}, u32[]{:S(2)}) collective-permute-start(bf16[2,2,256,128]{3,2,1,0:T(8,128)(2,1)S(1)} %copy-done.25), channel_id=1, source_target_pairs={{0,4},{4,0},{8,12},{12,8},{1,5},{5,1},{9,13},{13,9},{2,6},{6,2},{1... | collective-permute-start | bytes 786440 | tf_op jit(solution)/shard_map/ppermute | solution.py:27
  49.7 9.9 %attention.4 = (bf16[2,2,256,128]{3,2,1,0:T(8,128)(2,1)}, bf16[2,2,256,128]{3,2,1,0:T(8,128)(2,1)}, bf16[2,2,256,128]{3,2,1,0:T(8,128)(2,1)}, bf16[2,2,256,128]{...) custom-call(f32[2,3,8,256]{3,2,1,0:T(8,128)S(1)} %fusion.22.bias_ref, ...), custom_call_target="tpu_custom_call" | custom-call | flops 2415919104 | bytes 3670016 | tf_op jit(solution)/shard_map/attention/pallas_call | solution.py:153
  59.6 1.7 %collective-permute-done.15 = bf16[2,2,2,256,128]{4,3,2,1,0:T(8,128)(2,1)S(1)} collective-permute-done((bf16[2,2,2,256,128]{4,3,2,1,0:T(8,128)(2,1)S(1)}, bf16[2,2,2,256,128]{4,3,2,1,0:T(8,128)(2,1)S(1)}, u32[]{:S(2)}, u32[]{:S(2)}) %collective-permute-start.15) | collective-permute-done | bytes 524320 | tf_op jit(solution)/shard_map/ppermute | solution.py:36
  61.5 2.1 %collective-permute-done.18 = bf16[2,2,2,256,128]{4,3,2,1,0:T(8,128)(2,1)S(1)} collective-permute-done((bf16[2,2,2,256,128]{4,3,2,1,0:T(8,128)(2,1)}, bf16[2,2,2,256,128]{4,3,2,1,0:T(8,128)(2,1)S(1)}, u32[]{:S(2)}, u32[]{:S(2)}) %collective-permute-start.18) | collective-permute-done | bytes 524320 | tf_op jit(solution)/shard_map/ppermute | solution.py:40
  63.6 1.2 %fusion.14 = (bf16[1,2,2,256,128]{4,3,2,1,0:T(8,128)(2,1)S(1)}, bf16[1,2,2,256,128]{4,3,2,1,0:T(8,128)(2,1)S(1)}) fusion(bf16[2,2,256,128]{3,2,1,0:T(8,128)(2,1)} %get-tuple-element.147, bf16[2,2,2,256,128]{4,3,2,1,0:T(8,128)(2,1)S(1)} %collective-permute-done.18, bf16[2,2,256,128]{3,2,1,0:T(8,128)(2,1)} %get-tuple-element.149), kind=kLoop, calls=%fused_computation.42 | loop fusion | flops 1048576 | bytes 1572864 | tf_op jit(solution)/shard_map/stack | solution.py:251
  64.9 0.8 collective-permute-start.20
  66.0 1.6 %collective-permute-start.21 = (bf16[4,2,256,128]{3,2,1,0:T(8,128)(2,1)S(1)}, bf16[4,2,256,128]{3,2,1,0:T(8,128)(2,1)S(1)}, u32[]{:S(2)}, u32[]{:S(2)}) collective-permute-start(bf16[4,2,256,128]{3,2,1,0:T(8,128)(2,1)S(1)} %pad_maximum_fusion.8), channel_id=1, source_target_pairs={{0,4},{4,0},{8,12},{12,8},{1,5},{5,1},{9,13},{13,9},{2,6},{6,2},{1... | collective-permute-start | bytes 1572872 | tf_op jit(solution)/shard_map/ppermute | solution.py:27
  67.6 6.0 %attention.5 = (bf16[1,2,256,128]{3,2,1,0:T(8,128)(2,1)}, bf16[1,2,256,128]{3,2,1,0:T(8,128)(2,1)}, bf16[1,2,256,128]{3,2,1,0:T(8,128)(2,1)}, bf16[1,2,256,128]{...) custom-call(f32[2,3,8,256]{3,2,1,0:T(8,128)S(1)} %fusion.22.bias_ref, ...), custom_call_target="tpu_custom_call" | custom-call | flops 1207959552 | bytes 1835008 | tf_op jit(solution)/shard_map/attention/pallas_call | solution.py:153
  73.6 0.6 collective-permute-start.19
  74.1 4.8 %collective-permute-done.20 = bf16[2,2,2,256,128]{4,3,2,1,0:T(8,128)(2,1)S(1)} collective-permute-done((bf16[2,2,2,256,128]{4,3,2,1,0:T(8,128)(2,1)S(1)}, bf16[2,2,2,256,128]{4,3,2,1,0:T(8,128)(2,1)S(1)}, u32[]{:S(2)}, u32[]{:S(2)}) %collective-permute-start.20) | collective-permute-done | bytes 524320 | tf_op jit(solution)/shard_map/ppermute | solution.py:36
  79.0 1.0 collective-permute-done.21
  79.9 1.1 %fusion.18 = (bf16[1,2,256,128]{3,2,1,0:T(8,128)(2,1)S(1)}, bf16[1,2,256,128]{3,2,1,0:T(8,128)(2,1)S(1)}) fusion(bf16[1,2,256,128]{3,2,1,0:T(8,128)(2,1)} %get-tuple-element.168, bf16[2,1,2,256,128]{4,3,2,1,0:T(8,128)(2,1)S(1)} %collective-permute-done.19, bf16[1,2,256,128]{3,2,1,0:T(8,128)(2,1)} %get-tuple-element.159), kind=kLoop, calls=%fused_computation.52 | loop fusion | flops 524288 | bytes 786432 | tf_op jit(solution)/shard_map/convert_element_type | solution.py:243
  81.0 1.2 %collective-permute-start.23 = (bf16[1,2,256,128]{3,2,1,0:T(8,128)(2,1)S(1)}, bf16[1,2,256,128]{3,2,1,0:T(8,128)(2,1)S(1)}, u32[]{:S(2)}, u32[]{:S(2)}) collective-permute-start(bf16[1,2,256,128]{3,2,1,0:T(8,128)(2,1)S(1)} %get-tuple-element.213), channel_id=1, source_target_pairs={{0,8},{4,12},{8,0},{12,4},{1,9},{5,13},{9,1},{13,5},{2,10},{6,14},... | collective-permute-start | bytes 393224 | tf_op jit(solution)/shard_map/ppermute | solution.py:36
  82.2 0.2 fusion.1
  82.5 1.2 %collective-permute-start.27 = (bf16[3,2,256,128]{3,2,1,0:T(8,128)(2,1)S(1)}, bf16[3,2,256,128]{3,2,1,0:T(8,128)(2,1)S(1)}, u32[]{:S(2)}, u32[]{:S(2)}) collective-permute-start(bf16[3,2,256,128]{3,2,1,0:T(8,128)(2,1)S(1)} %pad_maximum_fusion.9), channel_id=1, source_target_pairs={{0,4},{4,0},{8,12},{12,8},{1,5},{5,1},{9,13},{13,9},{2,6},{6,2},{1... | collective-permute-start | bytes 1179656 | tf_op jit(solution)/shard_map/ppermute | solution.py:27
  83.8 2.3 %collective-permute-done.23 = bf16[1,2,256,128]{3,2,1,0:T(8,128)(2,1)S(1)} collective-permute-done((bf16[1,2,256,128]{3,2,1,0:T(8,128)(2,1)S(1)}, bf16[1,2,256,128]{3,2,1,0:T(8,128)(2,1)S(1)}, u32[]{:S(2)}, u32[]{:S(2)}) %collective-permute-start.23) | collective-permute-done | bytes 131104 | tf_op jit(solution)/shard_map/ppermute | solution.py:36
  86.0 1.1 %collective-permute-start.26 = (bf16[1,2,256,128]{3,2,1,0:T(8,128)(2,1)S(1)}, bf16[1,2,256,128]{3,2,1,0:T(8,128)(2,1)S(1)}, u32[]{:S(2)}, u32[]{:S(2)}) collective-permute-start(bf16[1,2,256,128]{3,2,1,0:T(8,128)(2,1)S(1)} %get-tuple-element.169), channel_id=1, source_target_pairs={{0,8},{4,12},{8,0},{12,4},{1,9},{5,13},{9,1},{13,5},{2,10},{6,14},... | collective-permute-start | bytes 393224 | tf_op jit(solution)/shard_map/ppermute | solution.py:36
  87.2 1.2 %collective-permute-start.25 = (bf16[1,2,256,128]{3,2,1,0:T(8,128)(2,1)S(1)}, bf16[1,2,256,128]{3,2,1,0:T(8,128)(2,1)S(1)}, u32[]{:S(2)}, u32[]{:S(2)}) collective-permute-start(bf16[1,2,256,128]{3,2,1,0:T(8,128)(2,1)S(1)} %fusion.20), channel_id=1, source_target_pairs={{0,4},{4,0},{8,12},{12,8},{1,5},{5,1},{9,13},{13,9},{2,6},{6,2},{1... | collective-permute-start | bytes 393224 | tf_op jit(solution)/shard_map/ppermute | solution.py:27
  88.4 6.1 %collective-permute-done.27 = bf16[3,2,256,128]{3,2,1,0:T(8,128)(2,1)S(1)} collective-permute-done((bf16[3,2,256,128]{3,2,1,0:T(8,128)(2,1)S(1)}, bf16[3,2,256,128]{3,2,1,0:T(8,128)(2,1)S(1)}, u32[]{:S(2)}, u32[]{:S(2)}) %collective-permute-start.27) | collective-permute-done | bytes 393248 | tf_op jit(solution)/shard_map/ppermute | solution.py:27
  95.0 1.2 %copy_bitcast_fusion.2 = (bf16[4,8,8,1280]{3,2,1,0:T(8,128)(2,1)}, bf16[4,8,8,1280]{3,2,1,0:T(8,128)(2,1)}) fusion(bf16[1,4,8,8,10,128]{5,3,2,1,0,4:T(8,128)(2,1)S(1)} %get-tuple-element.194, bf16[1,4,8,8,10,128]{5,3,2,1,0,4:T(8,128)(2,1)S(1)} %get-tuple-element.195), kind=kLoop, calls=%fused_computation.10 | loop fusion | bytes 2621440 | tf_op jit(solution)/shard_map/squeeze | solution.py:296
  96.2 0.7 collective-permute-done.25
  97.4 0.9 copy.26
  98.4 0.9 copy.27
  (113 shorter events, 3.4 us)
Async XLA Ops:
  2.4 3.2 %copy-start.20 = (s32[1,2,2]{2,1,0:T(2,128)S(1)}, s32[1,2,2]{2,1,0:T(2,128)}, u32[]{:S(2)}) copy-start(s32[1,2,2]{2,1,0:T(2,128)} %param.10) | copy-start | bytes 52
  2.4 7.6 %copy-start.1 = (bf16[4,8,8,1280]{3,2,1,0:T(8,128)(2,1)S(1)}, bf16[4,8,8,1280]{3,2,1,0:T(8,128)(2,1)}, u32[]{:S(2)}) copy-start(bf16[4,8,8,1280]{3,2,1,0:T(8,128)(2,1)} %param.9) | copy-start | bytes 1966084
  2.5 7.6 %copy-start.2 = (bf16[4,8,8,1280]{3,2,1,0:T(8,128)(2,1)S(1)}, bf16[4,8,8,1280]{3,2,1,0:T(8,128)(2,1)}, u32[]{:S(2)}) copy-start(bf16[4,8,8,1280]{3,2,1,0:T(8,128)(2,1)} %param.6) | copy-start | bytes 1966084
  2.5 7.6 %copy-start = (bf16[5,2,256,128]{3,2,1,0:T(8,128)(2,1)}, bf16[5,2,256,128]{3,2,1,0:T(8,128)(2,1)S(1)}, u32[]{:S(2)}) copy-start(bf16[5,2,256,128]{3,2,1,0:T(8,128)(2,1)S(1)} %constant_dynamic-slice_fusion.3.own_a) | copy-start | bytes 1966084
  2.5 26.8 %collective-permute-start.6 = (bf16[5,2,256,128]{3,2,1,0:T(8,128)(2,1)S(1)}, bf16[5,2,256,128]{3,2,1,0:T(8,128)(2,1)}, u32[]{:S(2)}, u32[]{:S(2)}) collective-permute-start(bf16[5,2,256,128]{3,2,1,0:T(8,128)(2,1)S(1)} %constant_dynamic-slice_fusion.3.own_a), channel_id=1, source_target_pairs={{0,16},{16,0},{1,17},{17,1},{2,18},{18,2},{3,19},{19,3},{4,20},{20... | collective-permute-start | bytes 1966088 | tf_op jit(solution)/shard_map/ppermute | solution.py:40
  3.1 26.3 %collective-permute-start.3 = (bf16[5,2,256,128]{3,2,1,0:T(8,128)(2,1)S(1)}, bf16[5,2,256,128]{3,2,1,0:T(8,128)(2,1)}, u32[]{:S(2)}, u32[]{:S(2)}) collective-permute-start(bf16[5,2,256,128]{3,2,1,0:T(8,128)(2,1)S(1)} %constant_dynamic-slice_fusion.3.own_a), channel_id=1, source_target_pairs={{0,8},{4,12},{8,0},{12,4},{1,9},{5,13},{9,1},{13,5},{2,10},{6,14},... | collective-permute-start | bytes 1966088 | tf_op jit(solution)/shard_map/ppermute | solution.py:36
  5.7 11.4 %collective-permute-start.5 = (s32[2,2]{1,0:T(2,128)S(1)}, s32[2,2]{1,0:T(2,128)S(1)}, u32[]{:S(2)}, u32[]{:S(2)}) collective-permute-start(s32[2,2]{1,0:T(2,128)S(1)} %bitcast.120), channel_id=1, source_target_pairs={{0,4},{4,0},{8,12},{12,8},{1,5},{5,1},{9,13},{13,9},{2,6},{6,2},{1... | collective-permute-start | bytes 56 | tf_op jit(solution)/shard_map/ppermute | solution.py:27
  7.2 9.4 %collective-permute-start = (bf16[2,2,256,128]{3,2,1,0:T(8,128)(2,1)S(1)}, bf16[2,2,256,128]{3,2,1,0:T(8,128)(2,1)}, u32[]{:S(2)}, u32[]{:S(2)}) collective-permute-start(bf16[2,2,256,128]{3,2,1,0:T(8,128)(2,1)S(1)} %constant_dynamic-slice_fusion), channel_id=1, source_target_pairs={{0,4},{4,0},{8,12},{12,8},{1,5},{5,1},{9,13},{13,9},{2,6},{6,2},{1... | collective-permute-start | bytes 786440 | tf_op jit(solution)/shard_map/ppermute | solution.py:27
  8.5 16.3 %collective-permute-start.4 = (bf16[3,2,256,128]{3,2,1,0:T(8,128)(2,1)}, bf16[3,2,256,128]{3,2,1,0:T(8,128)(2,1)S(1)}, u32[]{:S(2)}, u32[]{:S(2)}) collective-permute-start(bf16[3,2,256,128]{3,2,1,0:T(8,128)(2,1)} %constant_dynamic-slice_fusion.5), channel_id=1, source_target_pairs={{0,4},{4,0},{8,12},{12,8},{1,5},{5,1},{9,13},{13,9},{2,6},{6,2},{1... | collective-permute-start | bytes 1179656 | tf_op jit(solution)/shard_map/ppermute | solution.py:27
  10.6 7.0 %copy-start.19 = (s32[2,3]{1,0:T(2,128)S(1)}, s32[2,3]{1,0:T(2,128)}, u32[]{:S(2)}) copy-start(s32[2,3]{1,0:T(2,128)} %constant.49.clone) | copy-start | bytes 76
  16.5 12.8 %collective-permute-start.2 = (bf16[2,2,256,128]{3,2,1,0:T(8,128)(2,1)S(1)}, bf16[2,2,256,128]{3,2,1,0:T(8,128)(2,1)S(1)}, u32[]{:S(2)}, u32[]{:S(2)}) collective-permute-start(bf16[2,2,256,128]{3,2,1,0:T(8,128)(2,1)S(1)} %constant_dynamic-slice_fusion.1), channel_id=1, source_target_pairs={{0,4},{4,0},{8,12},{12,8},{1,5},{5,1},{9,13},{13,9},{2,6},{6,2},{1... | collective-permute-start | bytes 786440 | tf_op jit(solution)/shard_map/ppermute | solution.py:27
  17.1 12.3 %collective-permute-start.1 = (bf16[2,2,256,128]{3,2,1,0:T(8,128)(2,1)}, bf16[2,2,256,128]{3,2,1,0:T(8,128)(2,1)S(1)}, u32[]{:S(2)}, u32[]{:S(2)}) collective-permute-start(bf16[2,2,256,128]{3,2,1,0:T(8,128)(2,1)} %collective-permute-done.par_a), channel_id=1, source_target_pairs={{0,8},{4,12},{8,0},{12,4},{1,9},{5,13},{9,1},{13,5},{2,10},{6,14},... | collective-permute-start | bytes 786440 | tf_op jit(solution)/shard_map/ppermute | solution.py:36
  24.9 18.5 %copy-start.4 = (bf16[3,2,256,128]{3,2,1,0:T(8,128)(2,1)}, bf16[3,2,256,128]{3,2,1,0:T(8,128)(2,1)S(1)}, u32[]{:S(2)}) copy-start(bf16[3,2,256,128]{3,2,1,0:T(8,128)(2,1)S(1)} %collective-permute-done.4.par_a) | copy-start | bytes 1179652
  29.4 3.5 %copy-start.22 = (bf16[2,2,256,128]{3,2,1,0:T(8,128)(2,1)}, bf16[2,2,256,128]{3,2,1,0:T(8,128)(2,1)S(1)}, u32[]{:S(2)}) copy-start(bf16[2,2,256,128]{3,2,1,0:T(8,128)(2,1)S(1)} %collective-permute-done.2.par_q) | copy-start | bytes 786436
  29.4 3.5 %copy-start.23 = (bf16[2,2,256,128]{3,2,1,0:T(8,128)(2,1)}, bf16[2,2,256,128]{3,2,1,0:T(8,128)(2,1)S(1)}, u32[]{:S(2)}) copy-start(bf16[2,2,256,128]{3,2,1,0:T(8,128)(2,1)S(1)} %collective-permute-done.1.rel_a) | copy-start | bytes 786436
  29.4 3.1 %collective-permute-start.9 = (bf16[5,2,256,128]{3,2,1,0:T(8,128)(2,1)}, bf16[5,2,256,128]{3,2,1,0:T(8,128)(2,1)S(1)}, u32[]{:S(2)}, u32[]{:S(2)}) collective-permute-start(bf16[5,2,256,128]{3,2,1,0:T(8,128)(2,1)} %collective-permute-done.3.yown_a), channel_id=1, source_target_pairs={{0,16},{16,0},{1,17},{17,1},{2,18},{18,2},{3,19},{19,3},{4,20},{20... | collective-permute-start | bytes 1966088 | tf_op jit(solution)/shard_map/ppermute | solution.py:40
  29.6 3.0 %collective-permute-start.8 = (bf16[2,2,256,128]{3,2,1,0:T(8,128)(2,1)}, bf16[2,2,256,128]{3,2,1,0:T(8,128)(2,1)S(1)}, u32[]{:S(2)}, u32[]{:S(2)}) collective-permute-start(bf16[2,2,256,128]{3,2,1,0:T(8,128)(2,1)} %collective-permute-done.par_a), channel_id=1, source_target_pairs={{0,16},{16,0},{1,17},{17,1},{2,18},{18,2},{3,19},{19,3},{4,20},{20... | collective-permute-start | bytes 786440 | tf_op jit(solution)/shard_map/ppermute | solution.py:40
  30.1 2.5 %collective-permute-start.7 = (bf16[2,2,256,128]{3,2,1,0:T(8,128)(2,1)S(1)}, bf16[2,2,256,128]{3,2,1,0:T(8,128)(2,1)S(1)}, u32[]{:S(2)}, u32[]{:S(2)}) collective-permute-start(bf16[2,2,256,128]{3,2,1,0:T(8,128)(2,1)S(1)} %collective-permute-done.1.rel_a), channel_id=1, source_target_pairs={{0,16},{16,0},{1,17},{17,1},{2,18},{18,2},{3,19},{19,3},{4,20},{20... | collective-permute-start | bytes 786440 | tf_op jit(solution)/shard_map/ppermute | solution.py:40
  30.7 12.7 %collective-permute-start.11 = (bf16[3,2,256,128]{3,2,1,0:T(8,128)(2,1)S(1)}, bf16[3,2,256,128]{3,2,1,0:T(8,128)(2,1)S(1)}, u32[]{:S(2)}, u32[]{:S(2)}) collective-permute-start(bf16[3,2,256,128]{3,2,1,0:T(8,128)(2,1)S(1)} %constant_dynamic-slice_fusion.4), channel_id=1, source_target_pairs={{0,4},{4,0},{8,12},{12,8},{1,5},{5,1},{9,13},{13,9},{2,6},{6,2},{1... | collective-permute-start | bytes 1179656 | tf_op jit(solution)/shard_map/ppermute | solution.py:27
  31.3 12.1 %collective-permute-start.10 = (bf16[3,2,256,128]{3,2,1,0:T(8,128)(2,1)S(1)}, bf16[3,2,256,128]{3,2,1,0:T(8,128)(2,1)S(1)}, u32[]{:S(2)}, u32[]{:S(2)}) collective-permute-start(bf16[3,2,256,128]{3,2,1,0:T(8,128)(2,1)S(1)} %collective-permute-done.4.par_a), channel_id=1, source_target_pairs={{0,8},{4,12},{8,0},{12,4},{1,9},{5,13},{9,1},{13,5},{2,10},{6,14},... | collective-permute-start | bytes 1179656 | tf_op jit(solution)/shard_map/ppermute | solution.py:36
  32.5 10.9 %collective-permute-start.12 = (bf16[3,2,256,128]{3,2,1,0:T(8,128)(2,1)S(1)}, bf16[3,2,256,128]{3,2,1,0:T(8,128)(2,1)S(1)}, u32[]{:S(2)}, u32[]{:S(2)}) collective-permute-start(bf16[3,2,256,128]{3,2,1,0:T(8,128)(2,1)S(1)} %collective-permute-done.4.par_a), channel_id=1, source_target_pairs={{0,16},{16,0},{1,17},{17,1},{2,18},{18,2},{3,19},{19,3},{4,20},{20... | collective-permute-start | bytes 1179656 | tf_op jit(solution)/shard_map/ppermute | solution.py:40
  43.4 3.9 %copy-start.5 = (bf16[3,2,256,128]{3,2,1,0:T(8,128)(2,1)}, bf16[3,2,256,128]{3,2,1,0:T(8,128)(2,1)S(1)}, u32[]{:S(2)}) copy-start(bf16[3,2,256,128]{3,2,1,0:T(8,128)(2,1)S(1)} %collective-permute-done.11.par_q) | copy-start | bytes 1179652
  43.4 3.9 %copy-start.6 = (bf16[3,2,256,128]{3,2,1,0:T(8,128)(2,1)}, bf16[3,2,256,128]{3,2,1,0:T(8,128)(2,1)S(1)}, u32[]{:S(2)}) copy-start(bf16[3,2,256,128]{3,2,1,0:T(8,128)(2,1)S(1)} %collective-permute-done.10.rel_a) | copy-start | bytes 1179652
  43.4 3.9 %copy-start.7 = (bf16[3,2,256,128]{3,2,1,0:T(8,128)(2,1)}, bf16[3,2,256,128]{3,2,1,0:T(8,128)(2,1)S(1)}, u32[]{:S(2)}) copy-start(bf16[3,2,256,128]{3,2,1,0:T(8,128)(2,1)S(1)} %collective-permute-done.12.par_b) | copy-start | bytes 1179652
  43.4 2.5 %collective-permute-start.13 = (bf16[2,2,2,256,128]{4,3,2,1,0:T(8,128)(2,1)}, bf16[2,2,2,256,128]{4,3,2,1,0:T(8,128)(2,1)S(1)}, u32[]{:S(2)}, u32[]{:S(2)}) collective-permute-start(bf16[2,2,2,256,128]{4,3,2,1,0:T(8,128)(2,1)} %get-tuple-element.123), channel_id=1, source_target_pairs={{0,16},{16,0},{1,17},{17,1},{2,18},{18,2},{3,19},{19,3},{4,20},{20... | collective-permute-start | bytes 1572872 | tf_op jit(solution)/shard_map/ppermute | solution.py:40
  43.6 2.4 %collective-permute-start.14 = (bf16[3,2,256,128]{3,2,1,0:T(8,128)(2,1)S(1)}, bf16[3,2,256,128]{3,2,1,0:T(8,128)(2,1)S(1)}, u32[]{:S(2)}, u32[]{:S(2)}) collective-permute-start(bf16[3,2,256,128]{3,2,1,0:T(8,128)(2,1)S(1)} %collective-permute-done.10.rel_a), channel_id=1, source_target_pairs={{0,16},{16,0},{1,17},{17,1},{2,18},{18,2},{3,19},{19,3},{4,20},{20... | collective-permute-start | bytes 1179656 | tf_op jit(solution)/shard_map/ppermute | solution.py:40
  46.0 2.2 %copy-start.25 = (bf16[2,2,256,128]{3,2,1,0:T(8,128)(2,1)S(1)}, bf16[2,2,256,128]{3,2,1,0:T(8,128)(2,1)}, u32[]{:S(2)}) copy-start(bf16[2,2,256,128]{3,2,1,0:T(8,128)(2,1)} %get-tuple-element.136) | copy-start | bytes 786436
  47.3 14.0 %collective-permute-start.15 = (bf16[2,2,2,256,128]{4,3,2,1,0:T(8,128)(2,1)S(1)}, bf16[2,2,2,256,128]{4,3,2,1,0:T(8,128)(2,1)S(1)}, u32[]{:S(2)}, u32[]{:S(2)}) collective-permute-start(bf16[2,2,2,256,128]{4,3,2,1,0:T(8,128)(2,1)S(1)} %pad_maximum_fusion.6), channel_id=1, source_target_pairs={{0,8},{4,12},{8,0},{12,4},{1,9},{5,13},{9,1},{13,5},{2,10},{6,14},... | collective-permute-start | bytes 1572872 | tf_op jit(solution)/shard_map/ppermute | solution.py:36
  48.1 13.3 %collective-permute-start.17 = (bf16[2,2,2,256,128]{4,3,2,1,0:T(8,128)(2,1)S(1)}, bf16[2,2,2,256,128]{4,3,2,1,0:T(8,128)(2,1)S(1)}, u32[]{:S(2)}, u32[]{:S(2)}) collective-permute-start(bf16[2,2,2,256,128]{4,3,2,1,0:T(8,128)(2,1)S(1)} %copy-done.21), channel_id=1, source_target_pairs={{0,16},{16,0},{1,17},{17,1},{2,18},{18,2},{3,19},{19,3},{4,20},{20... | collective-permute-start | bytes 1572872 | tf_op jit(solution)/shard_map/ppermute | solution.py:40
  48.2 13.2 %collective-permute-start.16 = (bf16[2,2,256,128]{3,2,1,0:T(8,128)(2,1)S(1)}, bf16[2,2,256,128]{3,2,1,0:T(8,128)(2,1)S(1)}, u32[]{:S(2)}, u32[]{:S(2)}) collective-permute-start(bf16[2,2,256,128]{3,2,1,0:T(8,128)(2,1)S(1)} %copy-done.25), channel_id=1, source_target_pairs={{0,4},{4,0},{8,12},{12,8},{1,5},{5,1},{9,13},{13,9},{2,6},{6,2},{1... | collective-permute-start | bytes 786440 | tf_op jit(solution)/shard_map/ppermute | solution.py:27
  61.4 2.2 %collective-permute-start.18 = (bf16[2,2,2,256,128]{4,3,2,1,0:T(8,128)(2,1)}, bf16[2,2,2,256,128]{4,3,2,1,0:T(8,128)(2,1)S(1)}, u32[]{:S(2)}, u32[]{:S(2)}) collective-permute-start(bf16[2,2,2,256,128]{4,3,2,1,0:T(8,128)(2,1)} %get-tuple-element.141), channel_id=1, source_target_pairs={{0,16},{16,0},{1,17},{17,1},{2,18},{18,2},{3,19},{19,3},{4,20},{20... | collective-permute-start | bytes 1572872 | tf_op jit(solution)/shard_map/ppermute | solution.py:40
  64.9 14.0 %collective-permute-start.20 = (bf16[2,2,2,256,128]{4,3,2,1,0:T(8,128)(2,1)S(1)}, bf16[2,2,2,256,128]{4,3,2,1,0:T(8,128)(2,1)S(1)}, u32[]{:S(2)}, u32[]{:S(2)}) collective-permute-start(bf16[2,2,2,256,128]{4,3,2,1,0:T(8,128)(2,1)S(1)} %pad_maximum_fusion.7), channel_id=1, source_target_pairs={{0,8},{4,12},{8,0},{12,4},{1,9},{5,13},{9,1},{13,5},{2,10},{6,14},... | collective-permute-start | bytes 1572872 | tf_op jit(solution)/shard_map/ppermute | solution.py:36
  66.0 13.9 %collective-permute-start.21 = (bf16[4,2,256,128]{3,2,1,0:T(8,128)(2,1)S(1)}, bf16[4,2,256,128]{3,2,1,0:T(8,128)(2,1)S(1)}, u32[]{:S(2)}, u32[]{:S(2)}) collective-permute-start(bf16[4,2,256,128]{3,2,1,0:T(8,128)(2,1)S(1)} %pad_maximum_fusion.8), channel_id=1, source_target_pairs={{0,4},{4,0},{8,12},{12,8},{1,5},{5,1},{9,13},{13,9},{2,6},{6,2},{1... | collective-permute-start | bytes 1572872 | tf_op jit(solution)/shard_map/ppermute | solution.py:27
  67.6 12.4 %collective-permute-start.22 = (bf16[2,2,2,256,128]{4,3,2,1,0:T(8,128)(2,1)}, bf16[2,2,2,256,128]{4,3,2,1,0:T(8,128)(2,1)S(1)}, u32[]{:S(2)}, u32[]{:S(2)}) collective-permute-start(bf16[2,2,2,256,128]{4,3,2,1,0:T(8,128)(2,1)} %get-tuple-element.157), channel_id=1, source_target_pairs={{0,16},{16,0},{1,17},{17,1},{2,18},{18,2},{3,19},{19,3},{4,20},{20... | collective-permute-start | bytes 1572872 | tf_op jit(solution)/shard_map/ppermute | solution.py:40
  73.6 6.3 %collective-permute-start.19 = (bf16[2,1,2,256,128]{4,3,2,1,0:T(8,128)(2,1)}, bf16[2,1,2,256,128]{4,3,2,1,0:T(8,128)(2,1)S(1)}, u32[]{:S(2)}, u32[]{:S(2)}) collective-permute-start(bf16[2,1,2,256,128]{4,3,2,1,0:T(8,128)(2,1)} %get-tuple-element.146), channel_id=1, source_target_pairs={{0,16},{16,0},{1,17},{17,1},{2,18},{18,2},{3,19},{19,3},{4,20},{20... | collective-permute-start | bytes 786440 | tf_op jit(solution)/shard_map/ppermute | solution.py:40
  74.1 8.0 %copy-start.24 = (bf16[2,1,2,256,128]{4,3,2,1,0:T(8,128)(2,1)S(1)}, bf16[2,1,2,256,128]{4,3,2,1,0:T(8,128)(2,1)}, u32[]{:S(2)}) copy-start(bf16[2,1,2,256,128]{4,3,2,1,0:T(8,128)(2,1)} %get-tuple-element.162) | copy-start | bytes 786436
  74.1 8.1 %copy-start.11 = (bf16[2,2,256,128]{3,2,1,0:T(8,128)(2,1)S(1)}, bf16[2,2,256,128]{3,2,1,0:T(8,128)(2,1)}, u32[]{:S(2)}) copy-start(bf16[2,2,256,128]{3,2,1,0:T(8,128)(2,1)} %get-tuple-element.185) | copy-start | bytes 786436
  74.1 8.1 %copy-start.12 = (bf16[2,2,256,128]{3,2,1,0:T(8,128)(2,1)S(1)}, bf16[2,2,256,128]{3,2,1,0:T(8,128)(2,1)}, u32[]{:S(2)}) copy-start(bf16[2,2,256,128]{3,2,1,0:T(8,128)(2,1)} %get-tuple-element.175) | copy-start | bytes 786436
  79.9 2.5 %copy-start.18 = (bf16[1,2,256,128]{3,2,1,0:T(8,128)(2,1)S(1)}, bf16[1,2,256,128]{3,2,1,0:T(8,128)(2,1)}, u32[]{:S(2)}) copy-start(bf16[1,2,256,128]{3,2,1,0:T(8,128)(2,1)} %get-tuple-element.180) | copy-start | bytes 393220
  81.0 5.0 %collective-permute-start.23 = (bf16[1,2,256,128]{3,2,1,0:T(8,128)(2,1)S(1)}, bf16[1,2,256,128]{3,2,1,0:T(8,128)(2,1)S(1)}, u32[]{:S(2)}, u32[]{:S(2)}) collective-permute-start(bf16[1,2,256,128]{3,2,1,0:T(8,128)(2,1)S(1)} %get-tuple-element.213), channel_id=1, source_target_pairs={{0,8},{4,12},{8,0},{12,4},{1,9},{5,13},{9,1},{13,5},{2,10},{6,14},... | collective-permute-start | bytes 393224 | tf_op jit(solution)/shard_map/ppermute | solution.py:36
  82.2 3.9 %collective-permute-start.24 = (bf16[2,1,2,256,128]{4,3,2,1,0:T(8,128)(2,1)S(1)}, bf16[2,1,2,256,128]{4,3,2,1,0:T(8,128)(2,1)S(1)}, u32[]{:S(2)}, u32[]{:S(2)}) collective-permute-start(bf16[2,1,2,256,128]{4,3,2,1,0:T(8,128)(2,1)S(1)} %copy-done.24), channel_id=1, source_target_pairs={{0,16},{16,0},{1,17},{17,1},{2,18},{18,2},{3,19},{19,3},{4,20},{20... | collective-permute-start | bytes 786440 | tf_op jit(solution)/shard_map/ppermute | solution.py:40
  82.4 4.7 %copy-start.17 = (bf16[1,2,256,128]{3,2,1,0:T(8,128)(2,1)S(1)}, bf16[1,2,256,128]{3,2,1,0:T(8,128)(2,1)}, u32[]{:S(2)}) copy-start(bf16[1,2,256,128]{3,2,1,0:T(8,128)(2,1)} %get-tuple-element.164) | copy-start | bytes 393220
  82.4 12.1 %copy-start.9 = (bf16[2,2,256,128]{3,2,1,0:T(8,128)(2,1)S(1)}, bf16[2,2,256,128]{3,2,1,0:T(8,128)(2,1)}, u32[]{:S(2)}) copy-start(bf16[2,2,256,128]{3,2,1,0:T(8,128)(2,1)} %get-tuple-element.170) | copy-start | bytes 786436
  82.5 12.1 %copy-start.10 = (bf16[2,2,256,128]{3,2,1,0:T(8,128)(2,1)S(1)}, bf16[2,2,256,128]{3,2,1,0:T(8,128)(2,1)}, u32[]{:S(2)}) copy-start(bf16[2,2,256,128]{3,2,1,0:T(8,128)(2,1)} %get-tuple-element.171) | copy-start | bytes 786436
  82.5 12.1 %copy-start.15 = (bf16[1,2,256,128]{3,2,1,0:T(8,128)(2,1)S(1)}, bf16[1,2,256,128]{3,2,1,0:T(8,128)(2,1)}, u32[]{:S(2)}) copy-start(bf16[1,2,256,128]{3,2,1,0:T(8,128)(2,1)} %get-tuple-element.172) | copy-start | bytes 393220
  82.5 12.0 %collective-permute-start.27 = (bf16[3,2,256,128]{3,2,1,0:T(8,128)(2,1)S(1)}, bf16[3,2,256,128]{3,2,1,0:T(8,128)(2,1)S(1)}, u32[]{:S(2)}, u32[]{:S(2)}) collective-permute-start(bf16[3,2,256,128]{3,2,1,0:T(8,128)(2,1)S(1)} %pad_maximum_fusion.9), channel_id=1, source_target_pairs={{0,4},{4,0},{8,12},{12,8},{1,5},{5,1},{9,13},{13,9},{2,6},{6,2},{1... | collective-permute-start | bytes 1179656 | tf_op jit(solution)/shard_map/ppermute | solution.py:27
  86.0 10.2 %collective-permute-start.26 = (bf16[1,2,256,128]{3,2,1,0:T(8,128)(2,1)S(1)}, bf16[1,2,256,128]{3,2,1,0:T(8,128)(2,1)S(1)}, u32[]{:S(2)}, u32[]{:S(2)}) collective-permute-start(bf16[1,2,256,128]{3,2,1,0:T(8,128)(2,1)S(1)} %get-tuple-element.169), channel_id=1, source_target_pairs={{0,8},{4,12},{8,0},{12,4},{1,9},{5,13},{9,1},{13,5},{2,10},{6,14},... | collective-permute-start | bytes 393224 | tf_op jit(solution)/shard_map/ppermute | solution.py:36
  87.2 9.7 %collective-permute-start.25 = (bf16[1,2,256,128]{3,2,1,0:T(8,128)(2,1)S(1)}, bf16[1,2,256,128]{3,2,1,0:T(8,128)(2,1)S(1)}, u32[]{:S(2)}, u32[]{:S(2)}) collective-permute-start(bf16[1,2,256,128]{3,2,1,0:T(8,128)(2,1)S(1)} %fusion.20), channel_id=1, source_target_pairs={{0,4},{4,0},{8,12},{12,8},{1,5},{5,1},{9,13},{13,9},{2,6},{6,2},{1... | collective-permute-start | bytes 393224 | tf_op jit(solution)/shard_map/ppermute | solution.py:27
  (7 other events, 11.1 us)

commit v3 on v2

--- a/solution.py
+++ b/solution.py
@@ -72,8 +72,6 @@
     near_rel,
     twin_stay,
     twin_send,
-    key_ref,
-    value_ref,
     scores_ref,
     probs_ref,
     dprobs_ref,
@@ -84,54 +82,80 @@
     scale = 1.0 / math.sqrt(HD)
     factor = math.log2(math.e) * scale
     ring = (rel_a, rel_b, own_a, own_b, par_a, par_b, yown_a, yown_b)
-    for at, ref in enumerate(ring):
-        key_ref[at] = ref[0, 0]
-        value_ref[at] = ref[0, 1]
     span = 6
-    for which, (q_ref, out_ref) in enumerate(((own_q, own_out), (par_q, par_out))):
-        first = 2 * which
-        query = q_ref[0, 0]
-        grad = q_ref[0, 1]
-        peak = None
-        for at in range(span):
-            score = dot(key_ref[first + at], query, LAST)
-            score = score.reshape(rows // lon, lon, rows) + bias_ref[which, at // 2][None]
-            scores_ref[at] = score.reshape(rows, rows)
-            top = jnp.max(score, axis=0)
-            peak = top if peak is None else jnp.maximum(peak, top)
-        peak = jnp.max(peak, axis=0, keepdims=True)
-        total = jnp.zeros((lon, rows), jnp.float32)
-        attended = jnp.zeros((HD, rows), jnp.float32)
-        for at in range(span):
-            expo = jnp.exp2((scores_ref[at] - peak) * factor)
-            total += jnp.sum(expo.reshape(rows // lon, lon, rows), axis=0)
-            probs = expo.astype(jnp.bfloat16)
-            probs_ref[at] = probs
-            attended += dot(value_ref[first + at], probs, FIRST)
-            dprobs_ref[at] = dot(value_ref[first + at], grad, LAST)
-        inverse = 1.0 / jnp.sum(total, axis=0, keepdims=True)
+    sides = ((own_q, own_out), (par_q, par_out))
+    peaks, totals, outs, deltas, query_grads, parts = ([None, None] for _ in range(6))
+
+    def score_step(which, at):
+        score = dot(ring[2 * which + at][0, 0], sides[which][0][0, 0], LAST)
+        score = score.reshape(rows // lon, lon, rows) + bias_ref[which, at // 2][None]
+        scores_ref[which, at] = score.reshape(rows, rows)
+        top = jnp.max(score, axis=0)
+        peaks[which] = top if at == 0 else jnp.maximum(peaks[which], top)
+
+    def peak_done(which):
+        peaks[which] = jnp.max(peaks[which], axis=0, keepdims=True)
+        totals[which] = jnp.zeros((lon, rows), jnp.float32)
+        outs[which] = jnp.zeros((HD, rows), jnp.float32)
+
+    def probs_step(which, at):
+        expo = jnp.exp2((scores_ref[which, at] - peaks[which]) * factor)
+        totals[which] += jnp.sum(expo.reshape(rows // lon, lon, rows), axis=0)
+        probs = expo.astype(jnp.bfloat16)
+        probs_ref[which, at] = probs
+        value = ring[2 * which + at][0, 1]
+        outs[which] += dot(value, probs, FIRST)
+        dprobs_ref[which, at] = dot(value, sides[which][0][0, 1], LAST)
+
+    def probs_done(which):
+        query, grad = sides[which][0][0, 0], sides[which][0][0, 1]
+        inverse = 1.0 / jnp.sum(totals[which], axis=0, keepdims=True)
+        totals[which] = inverse
         column = jnp.broadcast_to(inverse, (HD, rows)).T
-        query_part = (query.astype(jnp.float32) * (column * scale)).astype(jnp.bfloat16)
-        grad_part = (grad.astype(jnp.float32) * column).astype(jnp.bfloat16)
-        attended = (attended * inverse).astype(jnp.bfloat16)
-        out_ref[0, 0] = attended.T
+        parts[which] = (
+            (query.astype(jnp.float32) * (column * scale)).astype(jnp.bfloat16),
+            (grad.astype(jnp.float32) * column).astype(jnp.bfloat16),
+        )
+        attended = (outs[which] * inverse).astype(jnp.bfloat16)
+        sides[which][1][0, 0] = attended.T
         product = grad.T.astype(jnp.float32) * attended.astype(jnp.float32)
-        delta = jnp.sum(product, axis=0, keepdims=True)
-        query_grad = jnp.zeros((HD, rows), jnp.float32)
-        for at in range(span):
-            probs = probs_ref[at]
-            dscores = probs.astype(jnp.float32) * (dprobs_ref[at] - delta)
-            dscores = dscores.astype(jnp.bfloat16)
-            query_grad += dot(key_ref[first + at], dscores, FIRST)
-            key_part = dot(dscores, query_part, PLAIN)
-            value_part = dot(probs, grad_part, PLAIN)
-            if which == 0 or at >= 4:
-                grad_ref[first + at, 0] = key_part
-                grad_ref[first + at, 1] = value_part
-            else:
-                grad_ref[first + at, 0] += key_part
-                grad_ref[first + at, 1] += value_part
-        out_ref[0, 1] = (query_grad * (inverse * scale)).T.astype(jnp.bfloat16)
+        deltas[which] = jnp.sum(product, axis=0, keepdims=True)
+        query_grads[which] = jnp.zeros((HD, rows), jnp.float32)
+
+    def grad_step(which, at):
+        place = 2 * which + at
+        probs = probs_ref[which, at]
+        dscores = probs.astype(jnp.float32) * (dprobs_ref[which, at] - deltas[which])
+        dscores = dscores.astype(jnp.bfloat16)
+        query_grads[which] += dot(ring[place][0, 0], dscores, FIRST)
+        key_part = dot(dscores, parts[which][0], PLAIN)
+        value_part = dot(probs, parts[which][1], PLAIN)
+        if which == 0 or at >= 4:
+            grad_ref[place, 0] = key_part
+            grad_ref[place, 1] = value_part
+        else:
+            grad_ref[place, 0] += key_part
+            grad_ref[place, 1] += value_part
+
+    def grad_done(which):
+        sides[which][1][0, 1] = (query_grads[which] * (totals[which] * scale)).T.astype(jnp.bfloat16)
+
+    for at in range(span):
+        score_step(0, at)
+    peak_done(0)
+    for at in range(span):
+        probs_step(0, at)
+        score_step(1, at)
+    probs_done(0)
+    peak_done(1)
+    for at in range(span):
+        grad_step(0, at)
+        probs_step(1, at)
+    grad_done(0)
+    probs_done(1)
+    for at in range(span):
+        grad_step(1, at)
+    grad_done(1)
     for b, (at, near_ref) in enumerate(((2, near_own), (4, near_par), (6, near_far), (0, near_rel))):
         near_ref[0] = grad_ref[at].astype(jnp.bfloat16)
         twin_ref = twin_stay if b < 2 else twin_send
@@ -159,14 +183,12 @@
             pltpu.HBM(shape, jnp.bfloat16) for shape in [pairs] * 6 + [spread] * 2
         ],
         scratch_shapes=[
-            pltpu.VMEM((8, rows, HD), jnp.bfloat16),
-            pltpu.VMEM((8, rows, HD), jnp.bfloat16),
-            pltpu.VMEM((6, rows, rows), jnp.float32),
-            pltpu.VMEM((6, rows, rows), jnp.bfloat16),
-            pltpu.VMEM((6, rows, rows), jnp.float32),
+            pltpu.VMEM((2, 6, rows, rows), jnp.float32),
+            pltpu.VMEM((2, 6, rows, rows), jnp.bfloat16),
+            pltpu.VMEM((2, 6, rows, rows), jnp.float32),
             pltpu.VMEM((8, 2, rows, HD), jnp.float32),
         ],
-        compiler_params=pltpu.CompilerParams(vmem_limit_bytes=18 * 1024 * 1024),
+        compiler_params=pltpu.CompilerParams(vmem_limit_bytes=26 * 1024 * 1024),
         cost_estimate=pl.CostEstimate(
             flops=heads * 2 * 6 * 6 * 2 * rows * rows * HD, bytes_accessed=heads * 28 * rows * HD * 2, transcendentals=0
         ),
@@ -245,12 +267,6 @@
     def theirs_total(near, twin, back):
         return (total(near, twin, 1) + back.astype(jnp.float32)).astype(jnp.bfloat16)
 
-    def send_back(near, twin):
-        relayed, ahead = rounded(near, twin, 3), rounded(near, twin, 2)
-        if lax.axis_size("lon") == 4:
-            return to_far(jnp.stack([relayed, ahead]), True)
-        return to_far(relayed, False), to_far(ahead, True)
-
     done_0, out_0, *near_0, stay_0, send_0 = compute(
         0, first, (partner_0, partner_0b), (relay_0, relay_0b), part_q0
     )
@@ -258,31 +274,35 @@
     send_0 = to_twin(order.gate(send_0))
     relay_1b = to_twin(order.gate(relay_1))
     send_0, relay_1b = order.passed(send_0, relay_1b)
-    back_0, ahead_0 = send_back(near_0, send_0)
+    back_0 = to_far(rounded(near_0, send_0, 3), False)
     back_out_0 = to_partner(order.gate(out_0))
     stay_0 = to_twin(order.gate(stay_0))
 
     rest = (partner_1, partner_1b), (relay_1, relay_1b), part_q1
     done_1, out_1, *near_1, stay_1, send_1 = compute(first, last, *rest)
-    send_1, back_0, ahead_0, back_out_0, stay_0 = order.passed(send_1, back_0, ahead_0, back_out_0, stay_0)
+    send_1, back_0, back_out_0, stay_0 = order.passed(send_1, back_0, back_out_0, stay_0)
     send_1 = to_twin(order.gate(send_1))
     theirs_0 = theirs_total(near_0, stay_0, order.gate(back_0))
     mixed_1 = to_partner(jnp.concatenate([theirs_0, order.gate(out_1)]))
     send_1 = order.passed(send_1)
-    back_1, ahead_1 = send_back(near_1, send_1)
+    back_1 = to_far(rounded(near_1, send_1, 3), False)
+    ahead_0 = to_far(order.gate(rounded(near_0, send_0, 2)), True)
     stay_1 = to_twin(order.gate(stay_1))
 
     done_2, out_2, *near_2, stay_2, send_2 = compute(last, half, *rest)
+    send_2, back_1, stay_1 = order.passed(send_2, back_1, stay_1)
+    send_2 = to_twin(order.gate(send_2))
+    theirs_1 = theirs_total(near_1, stay_1, order.gate(back_1))
+    payload = jnp.concatenate([theirs_1, order.gate(out_2)])
     send_2 = order.passed(send_2)
-    send_2 = to_twin(order.gate(send_2))
-    send_2, back_1, ahead_1, mixed_1, stay_1 = order.passed(send_2, back_1, ahead_1, mixed_1, stay_1)
-    back_2 = to_far(rounded(near_2, send_2, 3), False)
-    theirs_1 = theirs_total(near_1, stay_1, order.gate(back_1))
-    mixed_2 = to_partner(jnp.concatenate([theirs_1, order.gate(out_2)]))
+    outward = rounded(near_2, send_2, 3)
+    outward, payload, mixed_1, ahead_0 = order.passed(outward, payload, mixed_1, ahead_0)
+    back_2 = to_far(outward, False)
+    mixed_2 = to_partner(payload)
     stay_2 = to_twin(order.gate(stay_2))
     back_2, stay_2 = order.passed(back_2, stay_2)
     theirs_2 = to_partner(theirs_total(near_2, stay_2, order.gate(back_2)))
-    ahead_2 = to_far(order.gate(rounded(near_2, send_2, 2)), True)
+    ahead_12 = to_far(order.gate(jnp.concatenate([rounded(near_1, send_1, 2), rounded(near_2, send_2, 2)])), True)
 
     theirs_0, back_out_1 = mixed_1[:first], mixed_1[first:]
     theirs_1, back_out_2 = mixed_2[: last - first], mixed_2[last - first :]
@@ -296,7 +316,8 @@
         return shaped[0], shaped[1]
 
     attended, query_out = assembled((done_0, done_1, done_2), (back_out_0, back_out_1, back_out_2))
-    theirs_2, ahead_2, attended, query_out = order.passed(theirs_2, ahead_2, attended, query_out)
+    theirs_2, ahead_12, attended, query_out = order.passed(theirs_2, ahead_12, attended, query_out)
+    ahead_1, ahead_2 = ahead_12[: last - first], ahead_12[last - first :]
     mine = [
         (total(near, twin, 0) + ahead.astype(jnp.float32)).astype(jnp.bfloat16)
         for near, twin, ahead in ((near_0, stay_0, ahead_0), (near_1, stay_1, ahead_1), (near_2, stay_2, ahead_2))

time: 99.6 us -> 95.3 us (0.957)
  starting transfers between devices: 20.1 us -> 18.2 us
  Pallas kernels: 25.8 us -> 24.1 us
    ppermute x7 -> x8, waiting for transfers between devices: 8.79 us -> 4.06 us  [to_far(): return lax.ppermute(block, 'lon', route)]
    ppermute x9, waiting for transfers between devices: 24.6 us -> 28.2 us  [to_partner(): return lax.ppermute(block, 'lon', [(i, i ^ 1) for i in range(count)])]
    another operation x4 -> x0, other arithmetic: 2.57 us -> none  [send_back(): return to_far(jnp.stack([relayed, ahead]), True)]
    ppermute x9, starting transfers between devices: 10.3 us -> 8.05 us  [to_partner(): return lax.ppermute(block, 'lon', [(i, i ^ 1) for i in range(count)])]
    pallas_call x3, Pallas kernels: 25.8 us -> 24.1 us  [attention(): pl.pallas_call(attention_kernel, grid=(heads,), in_specs=[whole, here, th...]
    convert_element_type x1 -> x3, other arithmetic: 1.08 us -> 2.45 us  [rounded(): return total(near, twin, block).astype(jnp.bfloat16)]
    ppermute x7 -> x8, starting transfers between devices: 7.24 us -> 7.87 us  [to_far(): return lax.ppermute(block, 'lon', route)]
  transfers between devices with their start and end apart: 28 -> 29, of which waited for: 12 -> 12; matrix products, arithmetic and copies ran while one was open for 5% -> 9% of each run, Pallas kernels for 26% -> 25%
where the time goes in v3:
time: 95.3 us; the launch traced here: 95 us
  waiting for transfers between devices  38 us (40%)
  Pallas kernels  24.1 us (25%)
  starting transfers between devices  18.2 us (19%)
  local copies, waits for them, and re-layouts  7.18 us (8%)
  other arithmetic  6.37 us (7%)
  between operations  1.18 us (1%)
    ppermute x9, waiting for transfers between devices, to_partner(): return lax.ppermute(block, 'lon', [(i, i ^ 1) for i in range(count)])  28.2 us
    pallas_call x3, Pallas kernels, attention(): pl.pallas_call(attention_kernel, grid=(heads,), in_specs=[whole, here, th...  24.1 us
    ppermute x9, starting transfers between devices, to_partner(): return lax.ppermute(block, 'lon', [(i, i ^ 1) for i in range(count)])  8.05 us
    ppermute x8, starting transfers between devices, to_far(): return lax.ppermute(block, 'lon', route)  7.87 us
    ppermute x12, waiting for transfers between devices, to_twin(): return lax.ppermute(block, 'tm', [(0, 1), (1, 0)])  5.69 us
    ppermute x8, waiting for transfers between devices, to_far(): return lax.ppermute(block, 'lon', route)  4.06 us
    convert_element_type x3, other arithmetic, rounded(): return total(near, twin, block).astype(jnp.bfloat16)  2.45 us
    ppermute x12, starting transfers between devices, to_twin(): return lax.ppermute(block, 'tm', [(0, 1), (1, 0)])  2.29 us
  transfers between devices with their start and end apart: 29, of which 12 were waited for; matrix products, arithmetic and copies ran while one was open for 9% of the time, Pallas kernels for 25%

profile of v3, /device:TPU:0, one launch (start us, length us, event | category | flops | bytes accessed | tf_op | source)
XLA Modules:
  0.0 95.0 jit_solution(18237645005034366232)
XLA Ops:
  0.6 1.4 %pad_maximum_fusion = bf16[2,4,8,8,10,128]{5,3,4,2,1,0:T(8,128)(2,1)S(1)} fusion(bf16[1,4,8,8,10,128]{5,3,4,2,1,0:T(8,128)(2,1)} %bitcast.90, bf16[1,4,8,8,10,128]{5,3,4,2,1,0:T(8,128)(2,1)} %bitcast.91), kind=kLoop, calls=%fused_computation | loop fusion | flops 655360 | bytes 2621440 | tf_op jit(solution)/shard_map/stack | solution.py:223
  2.1 0.4 copy.20
  2.5 0.5 collective-permute-start.6
  3.1 2.6 %collective-permute-start.3 = (bf16[5,2,256,128]{3,2,1,0:T(8,128)(2,1)S(1)}, bf16[5,2,256,128]{3,2,1,0:T(8,128)(2,1)}, u32[]{:S(2)}, u32[]{:S(2)}) collective-permute-start(bf16[5,2,256,128]{3,2,1,0:T(8,128)(2,1)S(1)} %constant_dynamic-slice_fusion.3.own_a), channel_id=1, source_target_pairs={{0,8},{4,12},{8,0},{12,4},{1,9},{5,13},{9,1},{13,5},{2,10},{6,14},... | collective-permute-start | bytes 1966088 | tf_op jit(solution)/shard_map/ppermute | solution.py:36
  5.7 1.5 %collective-permute-start.5 = (s32[2,2]{1,0:T(2,128)S(1)}, s32[2,2]{1,0:T(2,128)S(1)}, u32[]{:S(2)}, u32[]{:S(2)}) collective-permute-start(s32[2,2]{1,0:T(2,128)S(1)} %bitcast.104), channel_id=1, source_target_pairs={{0,4},{4,0},{8,12},{12,8},{1,5},{5,1},{9,13},{13,9},{2,6},{6,2},{1... | collective-permute-start | bytes 56 | tf_op jit(solution)/shard_map/ppermute | solution.py:27
  7.2 0.6 collective-permute-start
  7.8 0.8 constant_dynamic-slice_fusion.5
  8.5 1.5 %collective-permute-start.4 = (bf16[3,2,256,128]{3,2,1,0:T(8,128)(2,1)}, bf16[3,2,256,128]{3,2,1,0:T(8,128)(2,1)S(1)}, u32[]{:S(2)}, u32[]{:S(2)}) collective-permute-start(bf16[3,2,256,128]{3,2,1,0:T(8,128)(2,1)} %constant_dynamic-slice_fusion.5), channel_id=1, source_target_pairs={{0,4},{4,0},{8,12},{12,8},{1,5},{5,1},{9,13},{13,9},{2,6},{6,2},{1... | collective-permute-start | bytes 1179656 | tf_op jit(solution)/shard_map/ppermute | solution.py:27
  10.2 0.4 copy.21
  10.6 0.9 constant_dynamic-slice_fusion.2.own_q
  11.5 5.0 %collective-permute-done.par_a = bf16[2,2,256,128]{3,2,1,0:T(8,128)(2,1)} collective-permute-done((bf16[2,2,256,128]{3,2,1,0:T(8,128)(2,1)S(1)}, bf16[2,2,256,128]{3,2,1,0:T(8,128)(2,1)}, u32[]{:S(2)}, u32[]{:S(2)}) %collective-permute-start) | collective-permute-done | bytes 262176 | tf_op jit(solution)/shard_map/ppermute | solution.py:27
  16.5 0.5 collective-permute-start.2
  17.1 0.5 collective-permute-start.1
  17.6 7.3 %collective-permute-done.4.par_a = bf16[3,2,256,128]{3,2,1,0:T(8,128)(2,1)S(1)} collective-permute-done((bf16[3,2,256,128]{3,2,1,0:T(8,128)(2,1)}, bf16[3,2,256,128]{3,2,1,0:T(8,128)(2,1)S(1)}, u32[]{:S(2)}, u32[]{:S(2)}) %collective-permute-start.4) | collective-permute-done | bytes 393248 | tf_op jit(solution)/shard_map/ppermute | solution.py:27
  24.9 4.5 %collective-permute-done.2.par_q = bf16[2,2,256,128]{3,2,1,0:T(8,128)(2,1)S(1)} collective-permute-done((bf16[2,2,256,128]{3,2,1,0:T(8,128)(2,1)S(1)}, bf16[2,2,256,128]{3,2,1,0:T(8,128)(2,1)S(1)}, u32[]{:S(2)}, u32[]{:S(2)}) %collective-permute-start.2) | collective-permute-done | bytes 262176 | tf_op jit(solution)/shard_map/ppermute | solution.py:27
  29.6 0.5 collective-permute-start.8
  30.7 0.6 collective-permute-start.11
  31.3 0.3 collective-permute-start.10
  31.5 1.0 %collective-permute-done.8.par_b = bf16[2,2,256,128]{3,2,1,0:T(8,128)(2,1)S(1)} collective-permute-done((bf16[2,2,256,128]{3,2,1,0:T(8,128)(2,1)}, bf16[2,2,256,128]{3,2,1,0:T(8,128)(2,1)S(1)}, u32[]{:S(2)}, u32[]{:S(2)}) %collective-permute-start.8) | collective-permute-done | bytes 262176 | tf_op jit(solution)/shard_map/ppermute | solution.py:40
  32.8 0.4 copy-done.26
  33.2 0.2 copy-done.4
  33.4 9.2 %attention.3 = (bf16[2,2,256,128]{3,2,1,0:T(8,128)(2,1)}, bf16[2,2,256,128]{3,2,1,0:T(8,128)(2,1)}, bf16[2,2,256,128]{3,2,1,0:T(8,128)(2,1)}, bf16[2,2,256,128]{...) custom-call(f32[2,3,8,256]{3,2,1,0:T(8,128)S(1)} %fusion.18.bias_ref, ...), custom_call_target="tpu_custom_call" | custom-call | flops 2415919104 | bytes 3670016 | tf_op jit(solution)/shard_map/attention/pallas_call | solution.py:177
  42.9 0.4 collective-permute-start.14
  43.3 2.0 %collective-permute-done.14.rel_b = bf16[3,2,256,128]{3,2,1,0:T(8,128)(2,1)S(1)} collective-permute-done((bf16[3,2,256,128]{3,2,1,0:T(8,128)(2,1)S(1)}, bf16[3,2,256,128]{3,2,1,0:T(8,128)(2,1)S(1)}, u32[]{:S(2)}, u32[]{:S(2)}) %collective-permute-start.14) | collective-permute-done | bytes 393248 | tf_op jit(solution)/shard_map/ppermute | solution.py:40
  45.4 1.4 %collective-permute-start.16 = (bf16[2,2,256,128]{3,2,1,0:T(8,128)(2,1)}, bf16[2,2,256,128]{3,2,1,0:T(8,128)(2,1)S(1)}, u32[]{:S(2)}, u32[]{:S(2)}) collective-permute-start(bf16[2,2,256,128]{3,2,1,0:T(8,128)(2,1)} %get-tuple-element.138), channel_id=1, source_target_pairs={{0,4},{4,0},{8,12},{12,8},{1,5},{5,1},{9,13},{13,9},{2,6},{6,2},{1... | collective-permute-start | bytes 786440 | tf_op jit(solution)/shard_map/ppermute | solution.py:27
  46.9 1.2 %fusion.5 = (bf16[2,2,256,128]{3,2,1,0:T(8,128)(2,1)S(1)}, bf16[2,2,256,128]{3,2,1,0:T(8,128)(2,1)S(1)}) fusion(bf16[2,2,256,128]{3,2,1,0:T(8,128)(2,1)} %get-tuple-element.169, bf16[2,2,2,256,128]{4,3,2,1,0:T(8,128)(2,1)S(1)} %collective-permute-done.13, bf16[2,2,256,128]{3,2,1,0:T(8,128)(2,1)} %get-tuple-element.135), kind=kLoop, calls=%fused_computation.26 | loop fusion | flops 1048576 | bytes 1572864 | tf_op jit(solution)/shard_map/convert_element_type | solution.py:265
  48.0 0.9 collective-permute-start.15
  48.9 9.2 %attention.4 = (bf16[2,2,256,128]{3,2,1,0:T(8,128)(2,1)}, bf16[2,2,256,128]{3,2,1,0:T(8,128)(2,1)}, bf16[2,2,256,128]{3,2,1,0:T(8,128)(2,1)}, bf16[2,2,256,128]{...) custom-call(f32[2,3,8,256]{3,2,1,0:T(8,128)S(1)} %fusion.18.bias_ref, ...), custom_call_target="tpu_custom_call" | custom-call | flops 2415919104 | bytes 3670016 | tf_op jit(solution)/shard_map/attention/pallas_call | solution.py:177
  58.3 2.1 %collective-permute-done.18 = bf16[2,2,2,256,128]{4,3,2,1,0:T(8,128)(2,1)S(1)} collective-permute-done((bf16[2,2,2,256,128]{4,3,2,1,0:T(8,128)(2,1)}, bf16[2,2,2,256,128]{4,3,2,1,0:T(8,128)(2,1)S(1)}, u32[]{:S(2)}, u32[]{:S(2)}) %collective-permute-start.18) | collective-permute-done | bytes 524320 | tf_op jit(solution)/shard_map/ppermute | solution.py:40
  60.6 1.2 %fusion.4 = (bf16[2,2,256,128]{3,2,1,0:T(8,128)(2,1)S(1)}, bf16[2,2,256,128]{3,2,1,0:T(8,128)(2,1)S(1)}) fusion(bf16[2,2,256,128]{3,2,1,0:T(8,128)(2,1)} %get-tuple-element.180, bf16[2,2,2,256,128]{4,3,2,1,0:T(8,128)(2,1)S(1)} %collective-permute-done.18, bf16[2,2,256,128]{3,2,1,0:T(8,128)(2,1)} %get-tuple-element.147), kind=kLoop, calls=%fused_computation.24 | loop fusion | flops 1048576 | bytes 1572864 | tf_op jit(solution)/shard_map/convert_element_type | solution.py:265
  61.8 1.3 %collective-permute-start.19 = (bf16[2,2,256,128]{3,2,1,0:T(8,128)(2,1)S(1)}, bf16[2,2,256,128]{3,2,1,0:T(8,128)(2,1)S(1)}, u32[]{:S(2)}, u32[]{:S(2)}) collective-permute-start(bf16[2,2,256,128]{3,2,1,0:T(8,128)(2,1)S(1)} %get-tuple-element.208), channel_id=1, source_target_pairs={{0,8},{4,12},{8,0},{12,4},{1,9},{5,13},{9,1},{13,5},{2,10},{6,14},... | collective-permute-start | bytes 786440 | tf_op jit(solution)/shard_map/ppermute | solution.py:36
  63.2 0.7 collective-permute-start.22
  63.9 0.8 collective-permute-start.23
  64.7 5.6 %attention.5 = (bf16[1,2,256,128]{3,2,1,0:T(8,128)(2,1)}, bf16[1,2,256,128]{3,2,1,0:T(8,128)(2,1)}, bf16[1,2,256,128]{3,2,1,0:T(8,128)(2,1)}, bf16[1,2,256,128]{...) custom-call(f32[2,3,8,256]{3,2,1,0:T(8,128)S(1)} %fusion.18.bias_ref, ...), custom_call_target="tpu_custom_call" | custom-call | flops 1207959552 | bytes 1835008 | tf_op jit(solution)/shard_map/attention/pallas_call | solution.py:177
  70.3 0.7 collective-permute-done.19
  71.1 1.0 %pad_maximum_fusion.7 = bf16[3,2,256,128]{3,2,1,0:T(8,128)(2,1)S(1)} fusion(bf16[1,2,256,128]{3,2,1,0:T(8,128)(2,1)} %get-tuple-element.162, bf16[2,2,256,128]{3,2,1,0:T(8,128)(2,1)S(1)} %fusion.9), kind=kLoop, calls=%fused_computation.37 | loop fusion | flops 196608 | bytes 786432 | tf_op jit(solution)/shard_map/concatenate | solution.py:296
  72.1 0.6 collective-permute-done.21
  72.8 4.4 %collective-permute-done.22 = bf16[4,2,256,128]{3,2,1,0:T(8,128)(2,1)S(1)} collective-permute-done((bf16[4,2,256,128]{3,2,1,0:T(8,128)(2,1)S(1)}, bf16[4,2,256,128]{3,2,1,0:T(8,128)(2,1)S(1)}, u32[]{:S(2)}, u32[]{:S(2)}) %collective-permute-start.22) | collective-permute-done | bytes 524320 | tf_op jit(solution)/shard_map/ppermute | solution.py:27
  77.2 0.8 collective-permute-start.24
  78.0 0.5 collective-permute-start.28
  78.8 3.3 %collective-permute-done.24 = bf16[1,2,256,128]{3,2,1,0:T(8,128)(2,1)S(1)} collective-permute-done((bf16[1,2,256,128]{3,2,1,0:T(8,128)(2,1)S(1)}, bf16[1,2,256,128]{3,2,1,0:T(8,128)(2,1)S(1)}, u32[]{:S(2)}, u32[]{:S(2)}) %collective-permute-start.24) | collective-permute-done | bytes 131104 | tf_op jit(solution)/shard_map/ppermute | solution.py:36
  82.2 0.7 collective-permute-start.26
  82.9 0.8 collective-permute-start.27
  83.7 6.3 %collective-permute-done.28 = bf16[3,2,256,128]{3,2,1,0:T(8,128)(2,1)S(1)} collective-permute-done((bf16[3,2,256,128]{3,2,1,0:T(8,128)(2,1)S(1)}, bf16[3,2,256,128]{3,2,1,0:T(8,128)(2,1)S(1)}, u32[]{:S(2)}, u32[]{:S(2)}) %collective-permute-start.28) | collective-permute-done | bytes 393248 | tf_op jit(solution)/shard_map/ppermute | solution.py:27
  90.4 1.2 %copy_bitcast_fusion.2 = (bf16[4,8,8,1280]{3,2,1,0:T(8,128)(2,1)}, bf16[4,8,8,1280]{3,2,1,0:T(8,128)(2,1)}) fusion(bf16[1,4,8,8,10,128]{5,3,2,1,0,4:T(8,128)(2,1)S(1)} %get-tuple-element.201, bf16[1,4,8,8,10,128]{5,3,2,1,0,4:T(8,128)(2,1)S(1)} %get-tuple-element.202), kind=kLoop, calls=%fused_computation.10 | loop fusion | bytes 2621440 | tf_op jit(solution)/shard_map/squeeze | solution.py:316
  91.6 0.7 collective-permute-done.26
  93.1 0.9 %copy.26 = bf16[1,4,8,8,10,128]{5,3,4,2,1,0:T(8,128)(2,1)} copy(bf16[1,4,8,8,10,128]{5,3,2,1,0,4:T(8,128)(2,1)S(1)} %get-tuple-element.197) | data formatting | bytes 1310720 | tf_op jit(solution)/shard_map/slice | solution.py:316
  94.0 0.9 copy.27
  (115 shorter events, 3.6 us)
Async XLA Ops:
  2.4 3.2 %copy-start.22 = (s32[1,2,2]{2,1,0:T(2,128)S(1)}, s32[1,2,2]{2,1,0:T(2,128)}, u32[]{:S(2)}) copy-start(s32[1,2,2]{2,1,0:T(2,128)} %param.10) | copy-start | bytes 52
  2.4 7.6 %copy-start.2 = (bf16[4,8,8,1280]{3,2,1,0:T(8,128)(2,1)S(1)}, bf16[4,8,8,1280]{3,2,1,0:T(8,128)(2,1)}, u32[]{:S(2)}) copy-start(bf16[4,8,8,1280]{3,2,1,0:T(8,128)(2,1)} %param.9) | copy-start | bytes 1966084
  2.5 7.6 %copy-start.3 = (bf16[4,8,8,1280]{3,2,1,0:T(8,128)(2,1)S(1)}, bf16[4,8,8,1280]{3,2,1,0:T(8,128)(2,1)}, u32[]{:S(2)}) copy-start(bf16[4,8,8,1280]{3,2,1,0:T(8,128)(2,1)} %param.6) | copy-start | bytes 1966084
  2.5 7.6 %copy-start = (bf16[5,2,256,128]{3,2,1,0:T(8,128)(2,1)}, bf16[5,2,256,128]{3,2,1,0:T(8,128)(2,1)S(1)}, u32[]{:S(2)}) copy-start(bf16[5,2,256,128]{3,2,1,0:T(8,128)(2,1)S(1)} %constant_dynamic-slice_fusion.3.own_a) | copy-start | bytes 1966084
  2.5 26.8 %collective-permute-start.6 = (bf16[5,2,256,128]{3,2,1,0:T(8,128)(2,1)S(1)}, bf16[5,2,256,128]{3,2,1,0:T(8,128)(2,1)}, u32[]{:S(2)}, u32[]{:S(2)}) collective-permute-start(bf16[5,2,256,128]{3,2,1,0:T(8,128)(2,1)S(1)} %constant_dynamic-slice_fusion.3.own_a), channel_id=1, source_target_pairs={{0,16},{16,0},{1,17},{17,1},{2,18},{18,2},{3,19},{19,3},{4,20},{20... | collective-permute-start | bytes 1966088 | tf_op jit(solution)/shard_map/ppermute | solution.py:40
  3.1 26.3 %collective-permute-start.3 = (bf16[5,2,256,128]{3,2,1,0:T(8,128)(2,1)S(1)}, bf16[5,2,256,128]{3,2,1,0:T(8,128)(2,1)}, u32[]{:S(2)}, u32[]{:S(2)}) collective-permute-start(bf16[5,2,256,128]{3,2,1,0:T(8,128)(2,1)S(1)} %constant_dynamic-slice_fusion.3.own_a), channel_id=1, source_target_pairs={{0,8},{4,12},{8,0},{12,4},{1,9},{5,13},{9,1},{13,5},{2,10},{6,14},... | collective-permute-start | bytes 1966088 | tf_op jit(solution)/shard_map/ppermute | solution.py:36
  5.7 11.4 %collective-permute-start.5 = (s32[2,2]{1,0:T(2,128)S(1)}, s32[2,2]{1,0:T(2,128)S(1)}, u32[]{:S(2)}, u32[]{:S(2)}) collective-permute-start(s32[2,2]{1,0:T(2,128)S(1)} %bitcast.104), channel_id=1, source_target_pairs={{0,4},{4,0},{8,12},{12,8},{1,5},{5,1},{9,13},{13,9},{2,6},{6,2},{1... | collective-permute-start | bytes 56 | tf_op jit(solution)/shard_map/ppermute | solution.py:27
  7.2 9.4 %collective-permute-start = (bf16[2,2,256,128]{3,2,1,0:T(8,128)(2,1)S(1)}, bf16[2,2,256,128]{3,2,1,0:T(8,128)(2,1)}, u32[]{:S(2)}, u32[]{:S(2)}) collective-permute-start(bf16[2,2,256,128]{3,2,1,0:T(8,128)(2,1)S(1)} %constant_dynamic-slice_fusion), channel_id=1, source_target_pairs={{0,4},{4,0},{8,12},{12,8},{1,5},{5,1},{9,13},{13,9},{2,6},{6,2},{1... | collective-permute-start | bytes 786440 | tf_op jit(solution)/shard_map/ppermute | solution.py:27
  8.5 16.3 %collective-permute-start.4 = (bf16[3,2,256,128]{3,2,1,0:T(8,128)(2,1)}, bf16[3,2,256,128]{3,2,1,0:T(8,128)(2,1)S(1)}, u32[]{:S(2)}, u32[]{:S(2)}) collective-permute-start(bf16[3,2,256,128]{3,2,1,0:T(8,128)(2,1)} %constant_dynamic-slice_fusion.5), channel_id=1, source_target_pairs={{0,4},{4,0},{8,12},{12,8},{1,5},{5,1},{9,13},{13,9},{2,6},{6,2},{1... | collective-permute-start | bytes 1179656 | tf_op jit(solution)/shard_map/ppermute | solution.py:27
  10.6 7.0 %copy-start.21 = (s32[2,3]{1,0:T(2,128)S(1)}, s32[2,3]{1,0:T(2,128)}, u32[]{:S(2)}) copy-start(s32[2,3]{1,0:T(2,128)} %constant.49.clone) | copy-start | bytes 76
  16.5 12.8 %collective-permute-start.2 = (bf16[2,2,256,128]{3,2,1,0:T(8,128)(2,1)S(1)}, bf16[2,2,256,128]{3,2,1,0:T(8,128)(2,1)S(1)}, u32[]{:S(2)}, u32[]{:S(2)}) collective-permute-start(bf16[2,2,256,128]{3,2,1,0:T(8,128)(2,1)S(1)} %constant_dynamic-slice_fusion.1), channel_id=1, source_target_pairs={{0,4},{4,0},{8,12},{12,8},{1,5},{5,1},{9,13},{13,9},{2,6},{6,2},{1... | collective-permute-start | bytes 786440 | tf_op jit(solution)/shard_map/ppermute | solution.py:27
  17.1 12.3 %collective-permute-start.1 = (bf16[2,2,256,128]{3,2,1,0:T(8,128)(2,1)}, bf16[2,2,256,128]{3,2,1,0:T(8,128)(2,1)S(1)}, u32[]{:S(2)}, u32[]{:S(2)}) collective-permute-start(bf16[2,2,256,128]{3,2,1,0:T(8,128)(2,1)} %collective-permute-done.par_a), channel_id=1, source_target_pairs={{0,8},{4,12},{8,0},{12,4},{1,9},{5,13},{9,1},{13,5},{2,10},{6,14},... | collective-permute-start | bytes 786440 | tf_op jit(solution)/shard_map/ppermute | solution.py:36
  24.9 4.7 %copy-start.5 = (bf16[3,2,256,128]{3,2,1,0:T(8,128)(2,1)}, bf16[3,2,256,128]{3,2,1,0:T(8,128)(2,1)S(1)}, u32[]{:S(2)}) copy-start(bf16[3,2,256,128]{3,2,1,0:T(8,128)(2,1)S(1)} %collective-permute-done.4.par_a) | copy-start | bytes 1179652
  29.4 3.5 %copy-start.23 = (bf16[2,2,256,128]{3,2,1,0:T(8,128)(2,1)}, bf16[2,2,256,128]{3,2,1,0:T(8,128)(2,1)S(1)}, u32[]{:S(2)}) copy-start(bf16[2,2,256,128]{3,2,1,0:T(8,128)(2,1)S(1)} %collective-permute-done.2.par_q) | copy-start | bytes 786436
  29.4 3.2 %copy-start.24 = (bf16[2,2,256,128]{3,2,1,0:T(8,128)(2,1)}, bf16[2,2,256,128]{3,2,1,0:T(8,128)(2,1)S(1)}, u32[]{:S(2)}) copy-start(bf16[2,2,256,128]{3,2,1,0:T(8,128)(2,1)S(1)} %collective-permute-done.1.rel_a) | copy-start | bytes 786436
  29.4 3.1 %collective-permute-start.9 = (bf16[5,2,256,128]{3,2,1,0:T(8,128)(2,1)}, bf16[5,2,256,128]{3,2,1,0:T(8,128)(2,1)S(1)}, u32[]{:S(2)}, u32[]{:S(2)}) collective-permute-start(bf16[5,2,256,128]{3,2,1,0:T(8,128)(2,1)} %collective-permute-done.3.yown_a), channel_id=1, source_target_pairs={{0,16},{16,0},{1,17},{17,1},{2,18},{18,2},{3,19},{19,3},{4,20},{20... | collective-permute-start | bytes 1966088 | tf_op jit(solution)/shard_map/ppermute | solution.py:40
  29.6 3.0 %collective-permute-start.8 = (bf16[2,2,256,128]{3,2,1,0:T(8,128)(2,1)}, bf16[2,2,256,128]{3,2,1,0:T(8,128)(2,1)S(1)}, u32[]{:S(2)}, u32[]{:S(2)}) collective-permute-start(bf16[2,2,256,128]{3,2,1,0:T(8,128)(2,1)} %collective-permute-done.par_a), channel_id=1, source_target_pairs={{0,16},{16,0},{1,17},{17,1},{2,18},{18,2},{3,19},{19,3},{4,20},{20... | collective-permute-start | bytes 786440 | tf_op jit(solution)/shard_map/ppermute | solution.py:40
  30.1 2.5 %collective-permute-start.7 = (bf16[2,2,256,128]{3,2,1,0:T(8,128)(2,1)S(1)}, bf16[2,2,256,128]{3,2,1,0:T(8,128)(2,1)S(1)}, u32[]{:S(2)}, u32[]{:S(2)}) collective-permute-start(bf16[2,2,256,128]{3,2,1,0:T(8,128)(2,1)S(1)} %collective-permute-done.1.rel_a), channel_id=1, source_target_pairs={{0,16},{16,0},{1,17},{17,1},{2,18},{18,2},{3,19},{19,3},{4,20},{20... | collective-permute-start | bytes 786440 | tf_op jit(solution)/shard_map/ppermute | solution.py:40
  30.7 12.0 %collective-permute-start.11 = (bf16[3,2,256,128]{3,2,1,0:T(8,128)(2,1)S(1)}, bf16[3,2,256,128]{3,2,1,0:T(8,128)(2,1)S(1)}, u32[]{:S(2)}, u32[]{:S(2)}) collective-permute-start(bf16[3,2,256,128]{3,2,1,0:T(8,128)(2,1)S(1)} %constant_dynamic-slice_fusion.4), channel_id=1, source_target_pairs={{0,4},{4,0},{8,12},{12,8},{1,5},{5,1},{9,13},{13,9},{2,6},{6,2},{1... | collective-permute-start | bytes 1179656 | tf_op jit(solution)/shard_map/ppermute | solution.py:27
  31.3 11.4 %collective-permute-start.10 = (bf16[3,2,256,128]{3,2,1,0:T(8,128)(2,1)}, bf16[3,2,256,128]{3,2,1,0:T(8,128)(2,1)S(1)}, u32[]{:S(2)}, u32[]{:S(2)}) collective-permute-start(bf16[3,2,256,128]{3,2,1,0:T(8,128)(2,1)} %copy-done.5), channel_id=1, source_target_pairs={{0,8},{4,12},{8,0},{12,4},{1,9},{5,13},{9,1},{13,5},{2,10},{6,14},... | collective-permute-start | bytes 1179656 | tf_op jit(solution)/shard_map/ppermute | solution.py:36
  32.6 10.2 %collective-permute-start.12 = (bf16[3,2,256,128]{3,2,1,0:T(8,128)(2,1)}, bf16[3,2,256,128]{3,2,1,0:T(8,128)(2,1)S(1)}, u32[]{:S(2)}, u32[]{:S(2)}) collective-permute-start(bf16[3,2,256,128]{3,2,1,0:T(8,128)(2,1)} %copy-done.5), channel_id=1, source_target_pairs={{0,16},{16,0},{1,17},{17,1},{2,18},{18,2},{3,19},{19,3},{4,20},{20... | collective-permute-start | bytes 1179656 | tf_op jit(solution)/shard_map/ppermute | solution.py:40
  42.7 6.3 %copy-start.6 = (bf16[3,2,256,128]{3,2,1,0:T(8,128)(2,1)}, bf16[3,2,256,128]{3,2,1,0:T(8,128)(2,1)S(1)}, u32[]{:S(2)}) copy-start(bf16[3,2,256,128]{3,2,1,0:T(8,128)(2,1)S(1)} %collective-permute-done.11.par_q) | copy-start | bytes 1179652
  42.7 6.2 %copy-start.7 = (bf16[3,2,256,128]{3,2,1,0:T(8,128)(2,1)}, bf16[3,2,256,128]{3,2,1,0:T(8,128)(2,1)S(1)}, u32[]{:S(2)}) copy-start(bf16[3,2,256,128]{3,2,1,0:T(8,128)(2,1)S(1)} %collective-permute-done.10.rel_a) | copy-start | bytes 1179652
  42.7 6.2 %copy-start.8 = (bf16[3,2,256,128]{3,2,1,0:T(8,128)(2,1)}, bf16[3,2,256,128]{3,2,1,0:T(8,128)(2,1)S(1)}, u32[]{:S(2)}) copy-start(bf16[3,2,256,128]{3,2,1,0:T(8,128)(2,1)S(1)} %collective-permute-done.12.par_b) | copy-start | bytes 1179652
  42.7 2.5 %collective-permute-start.13 = (bf16[2,2,2,256,128]{4,3,2,1,0:T(8,128)(2,1)}, bf16[2,2,2,256,128]{4,3,2,1,0:T(8,128)(2,1)S(1)}, u32[]{:S(2)}, u32[]{:S(2)}) collective-permute-start(bf16[2,2,2,256,128]{4,3,2,1,0:T(8,128)(2,1)} %get-tuple-element.126), channel_id=1, source_target_pairs={{0,16},{16,0},{1,17},{17,1},{2,18},{18,2},{3,19},{19,3},{4,20},{20... | collective-permute-start | bytes 1572872 | tf_op jit(solution)/shard_map/ppermute | solution.py:40
  42.9 2.3 %collective-permute-start.14 = (bf16[3,2,256,128]{3,2,1,0:T(8,128)(2,1)S(1)}, bf16[3,2,256,128]{3,2,1,0:T(8,128)(2,1)S(1)}, u32[]{:S(2)}, u32[]{:S(2)}) collective-permute-start(bf16[3,2,256,128]{3,2,1,0:T(8,128)(2,1)S(1)} %collective-permute-done.10.rel_a), channel_id=1, source_target_pairs={{0,16},{16,0},{1,17},{17,1},{2,18},{18,2},{3,19},{19,3},{4,20},{20... | collective-permute-start | bytes 1179656 | tf_op jit(solution)/shard_map/ppermute | solution.py:40
  45.3 12.9 %collective-permute-start.17 = (bf16[2,2,2,256,128]{4,3,2,1,0:T(8,128)(2,1)}, bf16[2,2,2,256,128]{4,3,2,1,0:T(8,128)(2,1)S(1)}, u32[]{:S(2)}, u32[]{:S(2)}) collective-permute-start(bf16[2,2,2,256,128]{4,3,2,1,0:T(8,128)(2,1)} %get-tuple-element.140), channel_id=1, source_target_pairs={{0,16},{16,0},{1,17},{17,1},{2,18},{18,2},{3,19},{19,3},{4,20},{20... | collective-permute-start | bytes 1572872 | tf_op jit(solution)/shard_map/ppermute | solution.py:40
  45.4 12.8 %collective-permute-start.16 = (bf16[2,2,256,128]{3,2,1,0:T(8,128)(2,1)}, bf16[2,2,256,128]{3,2,1,0:T(8,128)(2,1)S(1)}, u32[]{:S(2)}, u32[]{:S(2)}) collective-permute-start(bf16[2,2,256,128]{3,2,1,0:T(8,128)(2,1)} %get-tuple-element.138), channel_id=1, source_target_pairs={{0,4},{4,0},{8,12},{12,8},{1,5},{5,1},{9,13},{13,9},{2,6},{6,2},{1... | collective-permute-start | bytes 786440 | tf_op jit(solution)/shard_map/ppermute | solution.py:27
  48.0 10.2 %collective-permute-start.15 = (bf16[2,2,256,128]{3,2,1,0:T(8,128)(2,1)S(1)}, bf16[2,2,256,128]{3,2,1,0:T(8,128)(2,1)S(1)}, u32[]{:S(2)}, u32[]{:S(2)}) collective-permute-start(bf16[2,2,256,128]{3,2,1,0:T(8,128)(2,1)S(1)} %get-tuple-element.210), channel_id=1, source_target_pairs={{0,8},{4,12},{8,0},{12,4},{1,9},{5,13},{9,1},{13,5},{2,10},{6,14},... | collective-permute-start | bytes 786440 | tf_op jit(solution)/shard_map/ppermute | solution.py:36
  58.2 4.9 %copy-start.11 = (bf16[2,2,256,128]{3,2,1,0:T(8,128)(2,1)S(1)}, bf16[2,2,256,128]{3,2,1,0:T(8,128)(2,1)}, u32[]{:S(2)}) copy-start(bf16[2,2,256,128]{3,2,1,0:T(8,128)(2,1)} %get-tuple-element.163) | copy-start | bytes 786436
  58.2 2.2 %collective-permute-start.18 = (bf16[2,2,2,256,128]{4,3,2,1,0:T(8,128)(2,1)}, bf16[2,2,2,256,128]{4,3,2,1,0:T(8,128)(2,1)S(1)}, u32[]{:S(2)}, u32[]{:S(2)}) collective-permute-start(bf16[2,2,2,256,128]{4,3,2,1,0:T(8,128)(2,1)} %get-tuple-element.143), channel_id=1, source_target_pairs={{0,16},{16,0},{1,17},{17,1},{2,18},{18,2},{3,19},{19,3},{4,20},{20... | collective-permute-start | bytes 1572872 | tf_op jit(solution)/shard_map/ppermute | solution.py:40
  60.4 10.6 %collective-permute-start.20 = (bf16[2,2,2,256,128]{4,3,2,1,0:T(8,128)(2,1)}, bf16[2,2,2,256,128]{4,3,2,1,0:T(8,128)(2,1)S(1)}, u32[]{:S(2)}, u32[]{:S(2)}) collective-permute-start(bf16[2,2,2,256,128]{4,3,2,1,0:T(8,128)(2,1)} %get-tuple-element.150), channel_id=1, source_target_pairs={{0,16},{16,0},{1,17},{17,1},{2,18},{18,2},{3,19},{19,3},{4,20},{20... | collective-permute-start | bytes 1572872 | tf_op jit(solution)/shard_map/ppermute | solution.py:40
  61.8 9.2 %collective-permute-start.19 = (bf16[2,2,256,128]{3,2,1,0:T(8,128)(2,1)S(1)}, bf16[2,2,256,128]{3,2,1,0:T(8,128)(2,1)S(1)}, u32[]{:S(2)}, u32[]{:S(2)}) collective-permute-start(bf16[2,2,256,128]{3,2,1,0:T(8,128)(2,1)S(1)} %get-tuple-element.208), channel_id=1, source_target_pairs={{0,8},{4,12},{8,0},{12,4},{1,9},{5,13},{9,1},{13,5},{2,10},{6,14},... | collective-permute-start | bytes 786440 | tf_op jit(solution)/shard_map/ppermute | solution.py:36
  63.2 14.0 %collective-permute-start.22 = (bf16[4,2,256,128]{3,2,1,0:T(8,128)(2,1)S(1)}, bf16[4,2,256,128]{3,2,1,0:T(8,128)(2,1)S(1)}, u32[]{:S(2)}, u32[]{:S(2)}) collective-permute-start(bf16[4,2,256,128]{3,2,1,0:T(8,128)(2,1)S(1)} %pad_maximum_fusion.6), channel_id=1, source_target_pairs={{0,4},{4,0},{8,12},{12,8},{1,5},{5,1},{9,13},{13,9},{2,6},{6,2},{1... | collective-permute-start | bytes 1572872 | tf_op jit(solution)/shard_map/ppermute | solution.py:27
  63.9 7.1 %copy-start.12 = (bf16[2,2,256,128]{3,2,1,0:T(8,128)(2,1)S(1)}, bf16[2,2,256,128]{3,2,1,0:T(8,128)(2,1)}, u32[]{:S(2)}) copy-start(bf16[2,2,256,128]{3,2,1,0:T(8,128)(2,1)} %get-tuple-element.157) | copy-start | bytes 786436
  63.9 13.3 %collective-permute-start.23 = (bf16[2,2,256,128]{3,2,1,0:T(8,128)(2,1)S(1)}, bf16[2,2,256,128]{3,2,1,0:T(8,128)(2,1)S(1)}, u32[]{:S(2)}, u32[]{:S(2)}) collective-permute-start(bf16[2,2,256,128]{3,2,1,0:T(8,128)(2,1)S(1)} %get-tuple-element.170), channel_id=1, source_target_pairs={{0,8},{4,12},{8,0},{12,4},{1,9},{5,13},{9,1},{13,5},{2,10},{6,14},... | collective-permute-start | bytes 786440 | tf_op jit(solution)/shard_map/ppermute | solution.py:36
  71.0 1.7 %collective-permute-start.21 = (bf16[2,1,2,256,128]{4,3,2,1,0:T(8,128)(2,1)}, bf16[2,1,2,256,128]{4,3,2,1,0:T(8,128)(2,1)S(1)}, u32[]{:S(2)}, u32[]{:S(2)}) collective-permute-start(bf16[2,1,2,256,128]{4,3,2,1,0:T(8,128)(2,1)} %get-tuple-element.153), channel_id=1, source_target_pairs={{0,16},{16,0},{1,17},{17,1},{2,18},{18,2},{3,19},{19,3},{4,20},{20... | collective-permute-start | bytes 786440 | tf_op jit(solution)/shard_map/ppermute | solution.py:40
  71.0 7.0 %copy-start.25 = (bf16[2,1,2,256,128]{4,3,2,1,0:T(8,128)(2,1)S(1)}, bf16[2,1,2,256,128]{4,3,2,1,0:T(8,128)(2,1)}, u32[]{:S(2)}) copy-start(bf16[2,1,2,256,128]{4,3,2,1,0:T(8,128)(2,1)} %get-tuple-element.174) | copy-start | bytes 786436
  71.0 7.6 %copy-start.10 = (bf16[2,2,256,128]{3,2,1,0:T(8,128)(2,1)S(1)}, bf16[2,2,256,128]{3,2,1,0:T(8,128)(2,1)}, u32[]{:S(2)}) copy-start(bf16[2,2,256,128]{3,2,1,0:T(8,128)(2,1)} %get-tuple-element.191) | copy-start | bytes 786436
  77.2 5.0 %collective-permute-start.24 = (bf16[1,2,256,128]{3,2,1,0:T(8,128)(2,1)S(1)}, bf16[1,2,256,128]{3,2,1,0:T(8,128)(2,1)S(1)}, u32[]{:S(2)}, u32[]{:S(2)}) collective-permute-start(bf16[1,2,256,128]{3,2,1,0:T(8,128)(2,1)S(1)} %get-tuple-element.172), channel_id=1, source_target_pairs={{0,8},{4,12},{8,0},{12,4},{1,9},{5,13},{9,1},{13,5},{2,10},{6,14},... | collective-permute-start | bytes 393224 | tf_op jit(solution)/shard_map/ppermute | solution.py:36
  78.0 4.1 %collective-permute-start.25 = (bf16[2,1,2,256,128]{4,3,2,1,0:T(8,128)(2,1)S(1)}, bf16[2,1,2,256,128]{4,3,2,1,0:T(8,128)(2,1)S(1)}, u32[]{:S(2)}, u32[]{:S(2)}) collective-permute-start(bf16[2,1,2,256,128]{4,3,2,1,0:T(8,128)(2,1)S(1)} %copy-done.25), channel_id=1, source_target_pairs={{0,16},{16,0},{1,17},{17,1},{2,18},{18,2},{3,19},{19,3},{4,20},{20... | collective-permute-start | bytes 786440 | tf_op jit(solution)/shard_map/ppermute | solution.py:40
  78.0 11.9 %collective-permute-start.28 = (bf16[3,2,256,128]{3,2,1,0:T(8,128)(2,1)S(1)}, bf16[3,2,256,128]{3,2,1,0:T(8,128)(2,1)S(1)}, u32[]{:S(2)}, u32[]{:S(2)}) collective-permute-start(bf16[3,2,256,128]{3,2,1,0:T(8,128)(2,1)S(1)} %pad_maximum_fusion.7), channel_id=1, source_target_pairs={{0,4},{4,0},{8,12},{12,8},{1,5},{5,1},{9,13},{13,9},{2,6},{6,2},{1... | collective-permute-start | bytes 1179656 | tf_op jit(solution)/shard_map/ppermute | solution.py:27
  78.6 3.6 %copy-start.18 = (bf16[1,2,256,128]{3,2,1,0:T(8,128)(2,1)S(1)}, bf16[1,2,256,128]{3,2,1,0:T(8,128)(2,1)}, u32[]{:S(2)}) copy-start(bf16[1,2,256,128]{3,2,1,0:T(8,128)(2,1)} %get-tuple-element.176) | copy-start | bytes 393220
  78.7 11.3 %copy-start.14 = (bf16[2,2,256,128]{3,2,1,0:T(8,128)(2,1)S(1)}, bf16[2,2,256,128]{3,2,1,0:T(8,128)(2,1)}, u32[]{:S(2)}) copy-start(bf16[2,2,256,128]{3,2,1,0:T(8,128)(2,1)} %get-tuple-element.183) | copy-start | bytes 786436
  78.7 11.3 %copy-start.15 = (bf16[2,2,256,128]{3,2,1,0:T(8,128)(2,1)S(1)}, bf16[2,2,256,128]{3,2,1,0:T(8,128)(2,1)}, u32[]{:S(2)}) copy-start(bf16[2,2,256,128]{3,2,1,0:T(8,128)(2,1)} %get-tuple-element.184) | copy-start | bytes 786436
  78.7 11.3 %copy-start.16 = (bf16[1,2,256,128]{3,2,1,0:T(8,128)(2,1)S(1)}, bf16[1,2,256,128]{3,2,1,0:T(8,128)(2,1)}, u32[]{:S(2)}) copy-start(bf16[1,2,256,128]{3,2,1,0:T(8,128)(2,1)} %get-tuple-element.185) | copy-start | bytes 393220
  82.2 10.1 %collective-permute-start.26 = (bf16[1,2,256,128]{3,2,1,0:T(8,128)(2,1)S(1)}, bf16[1,2,256,128]{3,2,1,0:T(8,128)(2,1)S(1)}, u32[]{:S(2)}, u32[]{:S(2)}) collective-permute-start(bf16[1,2,256,128]{3,2,1,0:T(8,128)(2,1)S(1)} %fusion.16), channel_id=1, source_target_pairs={{0,4},{4,0},{8,12},{12,8},{1,5},{5,1},{9,13},{13,9},{2,6},{6,2},{1... | collective-permute-start | bytes 393224 | tf_op jit(solution)/shard_map/ppermute | solution.py:27
  82.9 9.5 %collective-permute-start.27 = (bf16[3,2,256,128]{3,2,1,0:T(8,128)(2,1)S(1)}, bf16[3,2,256,128]{3,2,1,0:T(8,128)(2,1)S(1)}, u32[]{:S(2)}, u32[]{:S(2)}) collective-permute-start(bf16[3,2,256,128]{3,2,1,0:T(8,128)(2,1)S(1)} %pad_maximum_fusion.8), channel_id=1, source_target_pairs={{0,8},{4,12},{8,0},{12,4},{1,9},{5,13},{9,1},{13,5},{2,10},{6,14},... | collective-permute-start | bytes 1179656 | tf_op jit(solution)/shard_map/ppermute | solution.py:36
  (9 other events, 14.7 us)

commit v4 on v3

--- a/solution.py
+++ b/solution.py
@@ -290,13 +290,13 @@
     stay_1 = to_twin(order.gate(stay_1))
 
     done_2, out_2, *near_2, stay_2, send_2 = compute(last, half, *rest)
-    send_2, back_1, stay_1 = order.passed(send_2, back_1, stay_1)
+    send_2, back_1, stay_1, mixed_1 = order.passed(send_2, back_1, stay_1, mixed_1)
     send_2 = to_twin(order.gate(send_2))
     theirs_1 = theirs_total(near_1, stay_1, order.gate(back_1))
     payload = jnp.concatenate([theirs_1, order.gate(out_2)])
     send_2 = order.passed(send_2)
     outward = rounded(near_2, send_2, 3)
-    outward, payload, mixed_1, ahead_0 = order.passed(outward, payload, mixed_1, ahead_0)
+    outward, payload, ahead_0 = order.passed(outward, payload, ahead_0)
     back_2 = to_far(outward, False)
     mixed_2 = to_partner(payload)
     stay_2 = to_twin(order.gate(stay_2))

time: 95.3 us -> 94.5 us (level)
  waiting for transfers between devices: 38 us -> 35.4 us
  starting transfers between devices: 18.2 us -> 19.4 us
    ppermute x12, waiting for transfers between devices: 5.69 us -> 3.85 us  [to_twin(): return lax.ppermute(block, 'tm', [(0, 1), (1, 0)])]
    convert_element_type x3, other arithmetic: 0.27 us -> 1.26 us  [theirs_total(): (total(near, twin, 1) + back.astype(jnp.float32)).astype(jnp.bfloat16)]
  transfers between devices with their start and end apart: 29 -> 29, of which waited for: 12 -> 13; matrix products, arithmetic and copies ran while one was open for 9% -> 10% of each run, Pallas kernels for 25% -> 26%
where the time goes in v4:
time: 94.5 us; the launch traced here: 94.3 us
  waiting for transfers between devices  35.4 us (37%)
  Pallas kernels  24.1 us (26%)
  starting transfers between devices  19.4 us (21%)
  local copies, waits for them, and re-layouts  7.09 us (8%)
  other arithmetic  7.03 us (7%)
  between operations  1.23 us (1%)
    ppermute x9, waiting for transfers between devices, to_partner(): return lax.ppermute(block, 'lon', [(i, i ^ 1) for i in range(count)])  28.1 us
    pallas_call x3, Pallas kernels, attention(): pl.pallas_call(attention_kernel, grid=(heads,), in_specs=[whole, here, th...  24.1 us
    ppermute x8, starting transfers between devices, to_far(): return lax.ppermute(block, 'lon', route)  8.61 us
    ppermute x9, starting transfers between devices, to_partner(): return lax.ppermute(block, 'lon', [(i, i ^ 1) for i in range(count)])  8.55 us
    ppermute x12, waiting for transfers between devices, to_twin(): return lax.ppermute(block, 'tm', [(0, 1), (1, 0)])  3.85 us
    ppermute x8, waiting for transfers between devices, to_far(): return lax.ppermute(block, 'lon', route)  3.52 us
    ppermute x12, starting transfers between devices, to_twin(): return lax.ppermute(block, 'tm', [(0, 1), (1, 0)])  2.28 us
    slice x4, local copies, waits for them, and re-layouts, assembled(): return (shaped[0], shaped[1])  2.16 us
  transfers between devices with their start and end apart: 29, of which 13 were waited for; matrix products, arithmetic and copies ran while one was open for 10% of the time, Pallas kernels for 26%

profile of v4, /device:TPU:0, one launch (start us, length us, event | category | flops | bytes accessed | tf_op | source)
XLA Modules:
  0.0 94.3 jit_solution(11182866461819185646)
XLA Ops:
  0.6 1.4 %pad_maximum_fusion = bf16[2,4,8,8,10,128]{5,3,4,2,1,0:T(8,128)(2,1)S(1)} fusion(bf16[1,4,8,8,10,128]{5,3,4,2,1,0:T(8,128)(2,1)} %bitcast.90, bf16[1,4,8,8,10,128]{5,3,4,2,1,0:T(8,128)(2,1)} %bitcast.91), kind=kLoop, calls=%fused_computation | loop fusion | flops 655360 | bytes 2621440 | tf_op jit(solution)/shard_map/stack | solution.py:223
  2.1 0.4 copy.20
  2.5 0.5 collective-permute-start.6
  3.1 2.6 %collective-permute-start.3 = (bf16[5,2,256,128]{3,2,1,0:T(8,128)(2,1)S(1)}, bf16[5,2,256,128]{3,2,1,0:T(8,128)(2,1)}, u32[]{:S(2)}, u32[]{:S(2)}) collective-permute-start(bf16[5,2,256,128]{3,2,1,0:T(8,128)(2,1)S(1)} %constant_dynamic-slice_fusion.3.own_a), channel_id=1, source_target_pairs={{0,8},{4,12},{8,0},{12,4},{1,9},{5,13},{9,1},{13,5},{2,10},{6,14},... | collective-permute-start | bytes 1966088 | tf_op jit(solution)/shard_map/ppermute | solution.py:36
  5.7 1.5 %collective-permute-start.5 = (s32[2,2]{1,0:T(2,128)S(1)}, s32[2,2]{1,0:T(2,128)S(1)}, u32[]{:S(2)}, u32[]{:S(2)}) collective-permute-start(s32[2,2]{1,0:T(2,128)S(1)} %bitcast.104), channel_id=1, source_target_pairs={{0,4},{4,0},{8,12},{12,8},{1,5},{5,1},{9,13},{13,9},{2,6},{6,2},{1... | collective-permute-start | bytes 56 | tf_op jit(solution)/shard_map/ppermute | solution.py:27
  7.2 0.6 collective-permute-start
  7.8 0.8 constant_dynamic-slice_fusion.5
  8.5 1.5 %collective-permute-start.4 = (bf16[3,2,256,128]{3,2,1,0:T(8,128)(2,1)}, bf16[3,2,256,128]{3,2,1,0:T(8,128)(2,1)}, u32[]{:S(2)}, u32[]{:S(2)}) collective-permute-start(bf16[3,2,256,128]{3,2,1,0:T(8,128)(2,1)} %constant_dynamic-slice_fusion.5), channel_id=1, source_target_pairs={{0,4},{4,0},{8,12},{12,8},{1,5},{5,1},{9,13},{13,9},{2,6},{6,2},{1... | collective-permute-start | bytes 1179656 | tf_op jit(solution)/shard_map/ppermute | solution.py:27
  10.2 0.4 copy.21
  10.6 0.9 constant_dynamic-slice_fusion.2.own_q
  11.5 5.0 %collective-permute-done.par_a = bf16[2,2,256,128]{3,2,1,0:T(8,128)(2,1)} collective-permute-done((bf16[2,2,256,128]{3,2,1,0:T(8,128)(2,1)S(1)}, bf16[2,2,256,128]{3,2,1,0:T(8,128)(2,1)}, u32[]{:S(2)}, u32[]{:S(2)}) %collective-permute-start) | collective-permute-done | bytes 262176 | tf_op jit(solution)/shard_map/ppermute | solution.py:27
  16.5 0.5 collective-permute-start.2
  17.1 0.5 collective-permute-start.1
  17.6 7.4 %collective-permute-done.4.par_a = bf16[3,2,256,128]{3,2,1,0:T(8,128)(2,1)} collective-permute-done((bf16[3,2,256,128]{3,2,1,0:T(8,128)(2,1)}, bf16[3,2,256,128]{3,2,1,0:T(8,128)(2,1)}, u32[]{:S(2)}, u32[]{:S(2)}) %collective-permute-start.4) | collective-permute-done | bytes 393248 | tf_op jit(solution)/shard_map/ppermute | solution.py:27
  25.0 4.4 %collective-permute-done.2.par_q = bf16[2,2,256,128]{3,2,1,0:T(8,128)(2,1)S(1)} collective-permute-done((bf16[2,2,256,128]{3,2,1,0:T(8,128)(2,1)S(1)}, bf16[2,2,256,128]{3,2,1,0:T(8,128)(2,1)S(1)}, u32[]{:S(2)}, u32[]{:S(2)}) %collective-permute-start.2) | collective-permute-done | bytes 262176 | tf_op jit(solution)/shard_map/ppermute | solution.py:27
  29.6 0.5 collective-permute-start.8
  30.7 0.6 collective-permute-start.11
  31.3 0.3 collective-permute-start.10
  31.5 1.0 %collective-permute-done.8.par_b = bf16[2,2,256,128]{3,2,1,0:T(8,128)(2,1)S(1)} collective-permute-done((bf16[2,2,256,128]{3,2,1,0:T(8,128)(2,1)}, bf16[2,2,256,128]{3,2,1,0:T(8,128)(2,1)S(1)}, u32[]{:S(2)}, u32[]{:S(2)}) %collective-permute-start.8) | collective-permute-done | bytes 262176 | tf_op jit(solution)/shard_map/ppermute | solution.py:40
  32.8 0.4 copy-done.29
  33.4 9.2 %attention.3 = (bf16[2,2,256,128]{3,2,1,0:T(8,128)(2,1)}, bf16[2,2,256,128]{3,2,1,0:T(8,128)(2,1)}, bf16[2,2,256,128]{3,2,1,0:T(8,128)(2,1)}, bf16[2,2,256,128]{...) custom-call(f32[2,3,8,256]{3,2,1,0:T(8,128)S(1)} %fusion.18.bias_ref, ...), custom_call_target="tpu_custom_call" | custom-call | flops 2415919104 | bytes 3670016 | tf_op jit(solution)/shard_map/attention/pallas_call | solution.py:177
  42.9 0.4 collective-permute-start.14
  43.3 2.0 %collective-permute-done.14.rel_b = bf16[3,2,256,128]{3,2,1,0:T(8,128)(2,1)S(1)} collective-permute-done((bf16[3,2,256,128]{3,2,1,0:T(8,128)(2,1)S(1)}, bf16[3,2,256,128]{3,2,1,0:T(8,128)(2,1)S(1)}, u32[]{:S(2)}, u32[]{:S(2)}) %collective-permute-start.14) | collective-permute-done | bytes 393248 | tf_op jit(solution)/shard_map/ppermute | solution.py:40
  45.4 1.4 %collective-permute-start.16 = (bf16[2,2,256,128]{3,2,1,0:T(8,128)(2,1)}, bf16[2,2,256,128]{3,2,1,0:T(8,128)(2,1)S(1)}, u32[]{:S(2)}, u32[]{:S(2)}) collective-permute-start(bf16[2,2,256,128]{3,2,1,0:T(8,128)(2,1)} %get-tuple-element.138), channel_id=1, source_target_pairs={{0,4},{4,0},{8,12},{12,8},{1,5},{5,1},{9,13},{13,9},{2,6},{6,2},{1... | collective-permute-start | bytes 786440 | tf_op jit(solution)/shard_map/ppermute | solution.py:27
  46.8 1.2 %fusion.5 = (bf16[2,2,256,128]{3,2,1,0:T(8,128)(2,1)S(1)}, bf16[2,2,256,128]{3,2,1,0:T(8,128)(2,1)S(1)}) fusion(bf16[2,2,256,128]{3,2,1,0:T(8,128)(2,1)} %get-tuple-element.169, bf16[2,2,2,256,128]{4,3,2,1,0:T(8,128)(2,1)S(1)} %collective-permute-done.13, bf16[2,2,256,128]{3,2,1,0:T(8,128)(2,1)} %get-tuple-element.135), kind=kLoop, calls=%fused_computation.26 | loop fusion | flops 1048576 | bytes 1572864 | tf_op jit(solution)/shard_map/convert_element_type | solution.py:265
  48.0 0.9 collective-permute-start.15
  48.9 9.3 %attention.4 = (bf16[2,2,256,128]{3,2,1,0:T(8,128)(2,1)}, bf16[2,2,256,128]{3,2,1,0:T(8,128)(2,1)}, bf16[2,2,256,128]{3,2,1,0:T(8,128)(2,1)}, bf16[2,2,256,128]{...) custom-call(f32[2,3,8,256]{3,2,1,0:T(8,128)S(1)} %fusion.18.bias_ref, ...), custom_call_target="tpu_custom_call" | custom-call | flops 2415919104 | bytes 3670016 | tf_op jit(solution)/shard_map/attention/pallas_call | solution.py:177
  58.5 1.0 %pad_maximum_fusion.6 = bf16[4,2,256,128]{3,2,1,0:T(8,128)(2,1)S(1)} fusion(bf16[2,2,256,128]{3,2,1,0:T(8,128)(2,1)} %get-tuple-element.156, bf16[2,2,256,128]{3,2,1,0:T(8,128)(2,1)S(1)} %fusion.9), kind=kLoop, calls=%fused_computation.16 | loop fusion | flops 262144 | bytes 1048576 | tf_op jit(solution)/shard_map/concatenate | solution.py:286
  59.5 0.6 collective-permute-start.21
  60.1 0.4 collective-permute-done.18
  60.6 0.8 fusion.4
  61.4 1.2 %collective-permute-start.19 = (bf16[2,2,256,128]{3,2,1,0:T(8,128)(2,1)}, bf16[2,2,256,128]{3,2,1,0:T(8,128)(2,1)}, u32[]{:S(2)}, u32[]{:S(2)}) collective-permute-start(bf16[2,2,256,128]{3,2,1,0:T(8,128)(2,1)} %get-tuple-element.208), channel_id=1, source_target_pairs={{0,8},{4,12},{8,0},{12,4},{1,9},{5,13},{9,1},{13,5},{2,10},{6,14},... | collective-permute-start | bytes 786440 | tf_op jit(solution)/shard_map/ppermute | solution.py:36
  62.6 0.9 collective-permute-start.23
  63.5 5.6 %attention.5 = (bf16[1,2,256,128]{3,2,1,0:T(8,128)(2,1)}, bf16[1,2,256,128]{3,2,1,0:T(8,128)(2,1)}, bf16[1,2,256,128]{3,2,1,0:T(8,128)(2,1)}, bf16[1,2,256,128]{...) custom-call(f32[2,3,8,256]{3,2,1,0:T(8,128)S(1)} %fusion.18.bias_ref, ...), custom_call_target="tpu_custom_call" | custom-call | flops 1207959552 | bytes 1835008 | tf_op jit(solution)/shard_map/attention/pallas_call | solution.py:177
  69.1 4.8 %collective-permute-done.21 = bf16[4,2,256,128]{3,2,1,0:T(8,128)(2,1)S(1)} collective-permute-done((bf16[4,2,256,128]{3,2,1,0:T(8,128)(2,1)S(1)}, bf16[4,2,256,128]{3,2,1,0:T(8,128)(2,1)S(1)}, u32[]{:S(2)}, u32[]{:S(2)}) %collective-permute-start.21) | collective-permute-done | bytes 524320 | tf_op jit(solution)/shard_map/ppermute | solution.py:27
  73.9 1.1 %fusion.7 = bf16[2,2,256,128]{3,2,1,0:T(8,128)(2,1)S(1)} fusion(bf16[2,2,256,128]{3,2,1,0:T(8,128)(2,1)} %collective-permute-done.19, bf16[2,2,256,128]{3,2,1,0:T(8,128)(2,1)S(1)} %copy-done.10, bf16[2,2,2,256,128]{4,3,2,1,0:T(8,128)(2,1)S(1)} %collective-permute-done.20), kind=kLoop, calls=%fused_computation.29 | loop fusion | flops 786432 | bytes 1048576 | tf_op jit(solution)/shard_map/convert_element_type | solution.py:268
  75.1 0.5 collective-permute-done.22
  75.9 1.2 %collective-permute-start.24 = (bf16[1,2,256,128]{3,2,1,0:T(8,128)(2,1)S(1)}, bf16[1,2,256,128]{3,2,1,0:T(8,128)(2,1)S(1)}, u32[]{:S(2)}, u32[]{:S(2)}) collective-permute-start(bf16[1,2,256,128]{3,2,1,0:T(8,128)(2,1)S(1)} %get-tuple-element.172), channel_id=1, source_target_pairs={{0,8},{4,12},{8,0},{12,4},{1,9},{5,13},{9,1},{13,5},{2,10},{6,14},... | collective-permute-start | bytes 393224 | tf_op jit(solution)/shard_map/ppermute | solution.py:36
  77.0 1.1 %collective-permute-start.28 = (bf16[3,2,256,128]{3,2,1,0:T(8,128)(2,1)S(1)}, bf16[3,2,256,128]{3,2,1,0:T(8,128)(2,1)S(1)}, u32[]{:S(2)}, u32[]{:S(2)}) collective-permute-start(bf16[3,2,256,128]{3,2,1,0:T(8,128)(2,1)S(1)} %pad_maximum_fusion.7), channel_id=1, source_target_pairs={{0,4},{4,0},{8,12},{12,8},{1,5},{5,1},{9,13},{13,9},{2,6},{6,2},{1... | collective-permute-start | bytes 1179656 | tf_op jit(solution)/shard_map/ppermute | solution.py:27
  78.3 3.0 %collective-permute-done.24 = bf16[1,2,256,128]{3,2,1,0:T(8,128)(2,1)S(1)} collective-permute-done((bf16[1,2,256,128]{3,2,1,0:T(8,128)(2,1)S(1)}, bf16[1,2,256,128]{3,2,1,0:T(8,128)(2,1)S(1)}, u32[]{:S(2)}, u32[]{:S(2)}) %collective-permute-start.24) | collective-permute-done | bytes 131104 | tf_op jit(solution)/shard_map/ppermute | solution.py:36
  81.4 0.7 collective-permute-start.26
  82.1 1.2 %collective-permute-start.27 = (bf16[3,2,256,128]{3,2,1,0:T(8,128)(2,1)S(1)}, bf16[3,2,256,128]{3,2,1,0:T(8,128)(2,1)S(1)}, u32[]{:S(2)}, u32[]{:S(2)}) collective-permute-start(bf16[3,2,256,128]{3,2,1,0:T(8,128)(2,1)S(1)} %pad_maximum_fusion.8), channel_id=1, source_target_pairs={{0,8},{4,12},{8,0},{12,4},{1,9},{5,13},{9,1},{13,5},{2,10},{6,14},... | collective-permute-start | bytes 1179656 | tf_op jit(solution)/shard_map/ppermute | solution.py:36
  83.2 5.7 %collective-permute-done.28 = bf16[3,2,256,128]{3,2,1,0:T(8,128)(2,1)S(1)} collective-permute-done((bf16[3,2,256,128]{3,2,1,0:T(8,128)(2,1)S(1)}, bf16[3,2,256,128]{3,2,1,0:T(8,128)(2,1)S(1)}, u32[]{:S(2)}, u32[]{:S(2)}) %collective-permute-start.28) | collective-permute-done | bytes 393248 | tf_op jit(solution)/shard_map/ppermute | solution.py:27
  89.4 1.2 %copy_bitcast_fusion.2 = (bf16[4,8,8,1280]{3,2,1,0:T(8,128)(2,1)}, bf16[4,8,8,1280]{3,2,1,0:T(8,128)(2,1)}) fusion(bf16[1,4,8,8,10,128]{5,3,2,1,0,4:T(8,128)(2,1)S(1)} %get-tuple-element.201, bf16[1,4,8,8,10,128]{5,3,2,1,0,4:T(8,128)(2,1)S(1)} %get-tuple-element.202), kind=kLoop, calls=%fused_computation.10 | loop fusion | bytes 2621440 | tf_op jit(solution)/shard_map/squeeze | solution.py:316
  90.6 0.7 collective-permute-done.26
  91.4 0.4 collective-permute-done.27
  92.4 0.9 %copy.26 = bf16[1,4,8,8,10,128]{5,3,4,2,1,0:T(8,128)(2,1)} copy(bf16[1,4,8,8,10,128]{5,3,2,1,0,4:T(8,128)(2,1)S(1)} %get-tuple-element.197) | data formatting | bytes 1310720 | tf_op jit(solution)/shard_map/slice | solution.py:316
  93.3 0.9 %copy.27 = bf16[1,4,8,8,10,128]{5,3,4,2,1,0:T(8,128)(2,1)} copy(bf16[1,4,8,8,10,128]{5,3,2,1,0,4:T(8,128)(2,1)S(1)} %get-tuple-element.198) | data formatting | bytes 1310720 | tf_op jit(solution)/shard_map/slice | solution.py:316
  (121 shorter events, 3.8 us)
Async XLA Ops:
  2.4 3.2 %copy-start.25 = (s32[1,2,2]{2,1,0:T(2,128)S(1)}, s32[1,2,2]{2,1,0:T(2,128)}, u32[]{:S(2)}) copy-start(s32[1,2,2]{2,1,0:T(2,128)} %param.10) | copy-start | bytes 52
  2.4 7.6 %copy-start.2 = (bf16[4,8,8,1280]{3,2,1,0:T(8,128)(2,1)S(1)}, bf16[4,8,8,1280]{3,2,1,0:T(8,128)(2,1)}, u32[]{:S(2)}) copy-start(bf16[4,8,8,1280]{3,2,1,0:T(8,128)(2,1)} %param.9) | copy-start | bytes 1966084
  2.5 7.6 %copy-start.3 = (bf16[4,8,8,1280]{3,2,1,0:T(8,128)(2,1)S(1)}, bf16[4,8,8,1280]{3,2,1,0:T(8,128)(2,1)}, u32[]{:S(2)}) copy-start(bf16[4,8,8,1280]{3,2,1,0:T(8,128)(2,1)} %param.6) | copy-start | bytes 1966084
  2.5 7.6 %copy-start = (bf16[5,2,256,128]{3,2,1,0:T(8,128)(2,1)}, bf16[5,2,256,128]{3,2,1,0:T(8,128)(2,1)S(1)}, u32[]{:S(2)}) copy-start(bf16[5,2,256,128]{3,2,1,0:T(8,128)(2,1)S(1)} %constant_dynamic-slice_fusion.3.own_a) | copy-start | bytes 1966084
  2.5 26.8 %collective-permute-start.6 = (bf16[5,2,256,128]{3,2,1,0:T(8,128)(2,1)S(1)}, bf16[5,2,256,128]{3,2,1,0:T(8,128)(2,1)}, u32[]{:S(2)}, u32[]{:S(2)}) collective-permute-start(bf16[5,2,256,128]{3,2,1,0:T(8,128)(2,1)S(1)} %constant_dynamic-slice_fusion.3.own_a), channel_id=1, source_target_pairs={{0,16},{16,0},{1,17},{17,1},{2,18},{18,2},{3,19},{19,3},{4,20},{20... | collective-permute-start | bytes 1966088 | tf_op jit(solution)/shard_map/ppermute | solution.py:40
  3.1 26.3 %collective-permute-start.3 = (bf16[5,2,256,128]{3,2,1,0:T(8,128)(2,1)S(1)}, bf16[5,2,256,128]{3,2,1,0:T(8,128)(2,1)}, u32[]{:S(2)}, u32[]{:S(2)}) collective-permute-start(bf16[5,2,256,128]{3,2,1,0:T(8,128)(2,1)S(1)} %constant_dynamic-slice_fusion.3.own_a), channel_id=1, source_target_pairs={{0,8},{4,12},{8,0},{12,4},{1,9},{5,13},{9,1},{13,5},{2,10},{6,14},... | collective-permute-start | bytes 1966088 | tf_op jit(solution)/shard_map/ppermute | solution.py:36
  5.7 11.4 %collective-permute-start.5 = (s32[2,2]{1,0:T(2,128)S(1)}, s32[2,2]{1,0:T(2,128)S(1)}, u32[]{:S(2)}, u32[]{:S(2)}) collective-permute-start(s32[2,2]{1,0:T(2,128)S(1)} %bitcast.104), channel_id=1, source_target_pairs={{0,4},{4,0},{8,12},{12,8},{1,5},{5,1},{9,13},{13,9},{2,6},{6,2},{1... | collective-permute-start | bytes 56 | tf_op jit(solution)/shard_map/ppermute | solution.py:27
  7.2 9.4 %collective-permute-start = (bf16[2,2,256,128]{3,2,1,0:T(8,128)(2,1)S(1)}, bf16[2,2,256,128]{3,2,1,0:T(8,128)(2,1)}, u32[]{:S(2)}, u32[]{:S(2)}) collective-permute-start(bf16[2,2,256,128]{3,2,1,0:T(8,128)(2,1)S(1)} %constant_dynamic-slice_fusion), channel_id=1, source_target_pairs={{0,4},{4,0},{8,12},{12,8},{1,5},{5,1},{9,13},{13,9},{2,6},{6,2},{1... | collective-permute-start | bytes 786440 | tf_op jit(solution)/shard_map/ppermute | solution.py:27
  8.5 16.4 %collective-permute-start.4 = (bf16[3,2,256,128]{3,2,1,0:T(8,128)(2,1)}, bf16[3,2,256,128]{3,2,1,0:T(8,128)(2,1)}, u32[]{:S(2)}, u32[]{:S(2)}) collective-permute-start(bf16[3,2,256,128]{3,2,1,0:T(8,128)(2,1)} %constant_dynamic-slice_fusion.5), channel_id=1, source_target_pairs={{0,4},{4,0},{8,12},{12,8},{1,5},{5,1},{9,13},{13,9},{2,6},{6,2},{1... | collective-permute-start | bytes 1179656 | tf_op jit(solution)/shard_map/ppermute | solution.py:27
  10.6 7.0 %copy-start.24 = (s32[2,3]{1,0:T(2,128)S(1)}, s32[2,3]{1,0:T(2,128)}, u32[]{:S(2)}) copy-start(s32[2,3]{1,0:T(2,128)} %constant.49.clone) | copy-start | bytes 76
  16.5 12.8 %collective-permute-start.2 = (bf16[2,2,256,128]{3,2,1,0:T(8,128)(2,1)S(1)}, bf16[2,2,256,128]{3,2,1,0:T(8,128)(2,1)S(1)}, u32[]{:S(2)}, u32[]{:S(2)}) collective-permute-start(bf16[2,2,256,128]{3,2,1,0:T(8,128)(2,1)S(1)} %constant_dynamic-slice_fusion.1), channel_id=1, source_target_pairs={{0,4},{4,0},{8,12},{12,8},{1,5},{5,1},{9,13},{13,9},{2,6},{6,2},{1... | collective-permute-start | bytes 786440 | tf_op jit(solution)/shard_map/ppermute | solution.py:27
  17.1 12.3 %collective-permute-start.1 = (bf16[2,2,256,128]{3,2,1,0:T(8,128)(2,1)}, bf16[2,2,256,128]{3,2,1,0:T(8,128)(2,1)S(1)}, u32[]{:S(2)}, u32[]{:S(2)}) collective-permute-start(bf16[2,2,256,128]{3,2,1,0:T(8,128)(2,1)} %collective-permute-done.par_a), channel_id=1, source_target_pairs={{0,8},{4,12},{8,0},{12,4},{1,9},{5,13},{9,1},{13,5},{2,10},{6,14},... | collective-permute-start | bytes 786440 | tf_op jit(solution)/shard_map/ppermute | solution.py:36
  29.4 3.5 %copy-start.26 = (bf16[2,2,256,128]{3,2,1,0:T(8,128)(2,1)}, bf16[2,2,256,128]{3,2,1,0:T(8,128)(2,1)S(1)}, u32[]{:S(2)}) copy-start(bf16[2,2,256,128]{3,2,1,0:T(8,128)(2,1)S(1)} %collective-permute-done.2.par_q) | copy-start | bytes 786436
  29.4 3.5 %copy-start.27 = (bf16[2,2,256,128]{3,2,1,0:T(8,128)(2,1)}, bf16[2,2,256,128]{3,2,1,0:T(8,128)(2,1)S(1)}, u32[]{:S(2)}) copy-start(bf16[2,2,256,128]{3,2,1,0:T(8,128)(2,1)S(1)} %collective-permute-done.1.rel_a) | copy-start | bytes 786436
  29.4 3.1 %collective-permute-start.9 = (bf16[5,2,256,128]{3,2,1,0:T(8,128)(2,1)}, bf16[5,2,256,128]{3,2,1,0:T(8,128)(2,1)S(1)}, u32[]{:S(2)}, u32[]{:S(2)}) collective-permute-start(bf16[5,2,256,128]{3,2,1,0:T(8,128)(2,1)} %collective-permute-done.3.yown_a), channel_id=1, source_target_pairs={{0,16},{16,0},{1,17},{17,1},{2,18},{18,2},{3,19},{19,3},{4,20},{20... | collective-permute-start | bytes 1966088 | tf_op jit(solution)/shard_map/ppermute | solution.py:40
  29.6 3.0 %collective-permute-start.8 = (bf16[2,2,256,128]{3,2,1,0:T(8,128)(2,1)}, bf16[2,2,256,128]{3,2,1,0:T(8,128)(2,1)S(1)}, u32[]{:S(2)}, u32[]{:S(2)}) collective-permute-start(bf16[2,2,256,128]{3,2,1,0:T(8,128)(2,1)} %collective-permute-done.par_a), channel_id=1, source_target_pairs={{0,16},{16,0},{1,17},{17,1},{2,18},{18,2},{3,19},{19,3},{4,20},{20... | collective-permute-start | bytes 786440 | tf_op jit(solution)/shard_map/ppermute | solution.py:40
  30.1 2.5 %collective-permute-start.7 = (bf16[2,2,256,128]{3,2,1,0:T(8,128)(2,1)S(1)}, bf16[2,2,256,128]{3,2,1,0:T(8,128)(2,1)S(1)}, u32[]{:S(2)}, u32[]{:S(2)}) collective-permute-start(bf16[2,2,256,128]{3,2,1,0:T(8,128)(2,1)S(1)} %collective-permute-done.1.rel_a), channel_id=1, source_target_pairs={{0,16},{16,0},{1,17},{17,1},{2,18},{18,2},{3,19},{19,3},{4,20},{20... | collective-permute-start | bytes 786440 | tf_op jit(solution)/shard_map/ppermute | solution.py:40
  30.7 12.0 %collective-permute-start.11 = (bf16[3,2,256,128]{3,2,1,0:T(8,128)(2,1)S(1)}, bf16[3,2,256,128]{3,2,1,0:T(8,128)(2,1)S(1)}, u32[]{:S(2)}, u32[]{:S(2)}) collective-permute-start(bf16[3,2,256,128]{3,2,1,0:T(8,128)(2,1)S(1)} %constant_dynamic-slice_fusion.4), channel_id=1, source_target_pairs={{0,4},{4,0},{8,12},{12,8},{1,5},{5,1},{9,13},{13,9},{2,6},{6,2},{1... | collective-permute-start | bytes 1179656 | tf_op jit(solution)/shard_map/ppermute | solution.py:27
  31.3 11.4 %collective-permute-start.10 = (bf16[3,2,256,128]{3,2,1,0:T(8,128)(2,1)}, bf16[3,2,256,128]{3,2,1,0:T(8,128)(2,1)S(1)}, u32[]{:S(2)}, u32[]{:S(2)}) collective-permute-start(bf16[3,2,256,128]{3,2,1,0:T(8,128)(2,1)} %collective-permute-done.4.par_a), channel_id=1, source_target_pairs={{0,8},{4,12},{8,0},{12,4},{1,9},{5,13},{9,1},{13,5},{2,10},{6,14},... | collective-permute-start | bytes 1179656 | tf_op jit(solution)/shard_map/ppermute | solution.py:36
  32.5 10.2 %collective-permute-start.12 = (bf16[3,2,256,128]{3,2,1,0:T(8,128)(2,1)}, bf16[3,2,256,128]{3,2,1,0:T(8,128)(2,1)S(1)}, u32[]{:S(2)}, u32[]{:S(2)}) collective-permute-start(bf16[3,2,256,128]{3,2,1,0:T(8,128)(2,1)} %collective-permute-done.4.par_a), channel_id=1, source_target_pairs={{0,16},{16,0},{1,17},{17,1},{2,18},{18,2},{3,19},{19,3},{4,20},{20... | collective-permute-start | bytes 1179656 | tf_op jit(solution)/shard_map/ppermute | solution.py:40
  42.7 6.2 %copy-start.5 = (bf16[3,2,256,128]{3,2,1,0:T(8,128)(2,1)}, bf16[3,2,256,128]{3,2,1,0:T(8,128)(2,1)S(1)}, u32[]{:S(2)}) copy-start(bf16[3,2,256,128]{3,2,1,0:T(8,128)(2,1)S(1)} %collective-permute-done.11.par_q) | copy-start | bytes 1179652
  42.7 6.2 %copy-start.6 = (bf16[3,2,256,128]{3,2,1,0:T(8,128)(2,1)}, bf16[3,2,256,128]{3,2,1,0:T(8,128)(2,1)S(1)}, u32[]{:S(2)}) copy-start(bf16[3,2,256,128]{3,2,1,0:T(8,128)(2,1)S(1)} %collective-permute-done.10.rel_a) | copy-start | bytes 1179652
  42.7 6.2 %copy-start.7 = (bf16[3,2,256,128]{3,2,1,0:T(8,128)(2,1)}, bf16[3,2,256,128]{3,2,1,0:T(8,128)(2,1)S(1)}, u32[]{:S(2)}) copy-start(bf16[3,2,256,128]{3,2,1,0:T(8,128)(2,1)S(1)} %collective-permute-done.12.par_b) | copy-start | bytes 1179652
  42.7 2.5 %collective-permute-start.13 = (bf16[2,2,2,256,128]{4,3,2,1,0:T(8,128)(2,1)}, bf16[2,2,2,256,128]{4,3,2,1,0:T(8,128)(2,1)S(1)}, u32[]{:S(2)}, u32[]{:S(2)}) collective-permute-start(bf16[2,2,2,256,128]{4,3,2,1,0:T(8,128)(2,1)} %get-tuple-element.126), channel_id=1, source_target_pairs={{0,16},{16,0},{1,17},{17,1},{2,18},{18,2},{3,19},{19,3},{4,20},{20... | collective-permute-start | bytes 1572872 | tf_op jit(solution)/shard_map/ppermute | solution.py:40
  42.9 2.3 %collective-permute-start.14 = (bf16[3,2,256,128]{3,2,1,0:T(8,128)(2,1)S(1)}, bf16[3,2,256,128]{3,2,1,0:T(8,128)(2,1)S(1)}, u32[]{:S(2)}, u32[]{:S(2)}) collective-permute-start(bf16[3,2,256,128]{3,2,1,0:T(8,128)(2,1)S(1)} %collective-permute-done.10.rel_a), channel_id=1, source_target_pairs={{0,16},{16,0},{1,17},{17,1},{2,18},{18,2},{3,19},{19,3},{4,20},{20... | collective-permute-start | bytes 1179656 | tf_op jit(solution)/shard_map/ppermute | solution.py:40
  45.3 13.0 %collective-permute-start.17 = (bf16[2,2,2,256,128]{4,3,2,1,0:T(8,128)(2,1)}, bf16[2,2,2,256,128]{4,3,2,1,0:T(8,128)(2,1)S(1)}, u32[]{:S(2)}, u32[]{:S(2)}) collective-permute-start(bf16[2,2,2,256,128]{4,3,2,1,0:T(8,128)(2,1)} %get-tuple-element.140), channel_id=1, source_target_pairs={{0,16},{16,0},{1,17},{17,1},{2,18},{18,2},{3,19},{19,3},{4,20},{20... | collective-permute-start | bytes 1572872 | tf_op jit(solution)/shard_map/ppermute | solution.py:40
  45.4 12.8 %collective-permute-start.16 = (bf16[2,2,256,128]{3,2,1,0:T(8,128)(2,1)}, bf16[2,2,256,128]{3,2,1,0:T(8,128)(2,1)S(1)}, u32[]{:S(2)}, u32[]{:S(2)}) collective-permute-start(bf16[2,2,256,128]{3,2,1,0:T(8,128)(2,1)} %get-tuple-element.138), channel_id=1, source_target_pairs={{0,4},{4,0},{8,12},{12,8},{1,5},{5,1},{9,13},{13,9},{2,6},{6,2},{1... | collective-permute-start | bytes 786440 | tf_op jit(solution)/shard_map/ppermute | solution.py:27
  48.0 10.3 %copy-start.11 = (bf16[2,2,256,128]{3,2,1,0:T(8,128)(2,1)S(1)}, bf16[2,2,256,128]{3,2,1,0:T(8,128)(2,1)}, u32[]{:S(2)}) copy-start(bf16[2,2,256,128]{3,2,1,0:T(8,128)(2,1)} %get-tuple-element.151) | copy-start | bytes 786436
  48.0 10.2 %collective-permute-start.15 = (bf16[2,2,256,128]{3,2,1,0:T(8,128)(2,1)S(1)}, bf16[2,2,256,128]{3,2,1,0:T(8,128)(2,1)S(1)}, u32[]{:S(2)}, u32[]{:S(2)}) collective-permute-start(bf16[2,2,256,128]{3,2,1,0:T(8,128)(2,1)S(1)} %get-tuple-element.210), channel_id=1, source_target_pairs={{0,8},{4,12},{8,0},{12,4},{1,9},{5,13},{9,1},{13,5},{2,10},{6,14},... | collective-permute-start | bytes 786440 | tf_op jit(solution)/shard_map/ppermute | solution.py:36
  58.2 3.2 %copy-start.15 = (bf16[2,2,256,128]{3,2,1,0:T(8,128)(2,1)}, bf16[2,2,256,128]{3,2,1,0:T(8,128)(2,1)S(1)}, u32[]{:S(2)}) copy-start(bf16[2,2,256,128]{3,2,1,0:T(8,128)(2,1)S(1)} %collective-permute-done.16) | copy-start | bytes 786436
  58.3 2.2 %collective-permute-start.18 = (bf16[2,2,2,256,128]{4,3,2,1,0:T(8,128)(2,1)}, bf16[2,2,2,256,128]{4,3,2,1,0:T(8,128)(2,1)S(1)}, u32[]{:S(2)}, u32[]{:S(2)}) collective-permute-start(bf16[2,2,2,256,128]{4,3,2,1,0:T(8,128)(2,1)} %get-tuple-element.143), channel_id=1, source_target_pairs={{0,16},{16,0},{1,17},{17,1},{2,18},{18,2},{3,19},{19,3},{4,20},{20... | collective-permute-start | bytes 1572872 | tf_op jit(solution)/shard_map/ppermute | solution.py:40
  59.5 14.4 %collective-permute-start.21 = (bf16[4,2,256,128]{3,2,1,0:T(8,128)(2,1)S(1)}, bf16[4,2,256,128]{3,2,1,0:T(8,128)(2,1)S(1)}, u32[]{:S(2)}, u32[]{:S(2)}) collective-permute-start(bf16[4,2,256,128]{3,2,1,0:T(8,128)(2,1)S(1)} %pad_maximum_fusion.6), channel_id=1, source_target_pairs={{0,4},{4,0},{8,12},{12,8},{1,5},{5,1},{9,13},{13,9},{2,6},{6,2},{1... | collective-permute-start | bytes 1572872 | tf_op jit(solution)/shard_map/ppermute | solution.py:27
  60.4 13.4 %collective-permute-start.20 = (bf16[2,2,2,256,128]{4,3,2,1,0:T(8,128)(2,1)}, bf16[2,2,2,256,128]{4,3,2,1,0:T(8,128)(2,1)S(1)}, u32[]{:S(2)}, u32[]{:S(2)}) collective-permute-start(bf16[2,2,2,256,128]{4,3,2,1,0:T(8,128)(2,1)} %get-tuple-element.150), channel_id=1, source_target_pairs={{0,16},{16,0},{1,17},{17,1},{2,18},{18,2},{3,19},{19,3},{4,20},{20... | collective-permute-start | bytes 1572872 | tf_op jit(solution)/shard_map/ppermute | solution.py:40
  61.4 12.4 %collective-permute-start.19 = (bf16[2,2,256,128]{3,2,1,0:T(8,128)(2,1)}, bf16[2,2,256,128]{3,2,1,0:T(8,128)(2,1)}, u32[]{:S(2)}, u32[]{:S(2)}) collective-permute-start(bf16[2,2,256,128]{3,2,1,0:T(8,128)(2,1)} %get-tuple-element.208), channel_id=1, source_target_pairs={{0,8},{4,12},{8,0},{12,4},{1,9},{5,13},{9,1},{13,5},{2,10},{6,14},... | collective-permute-start | bytes 786440 | tf_op jit(solution)/shard_map/ppermute | solution.py:36
  62.6 11.2 %copy-start.10 = (bf16[2,2,256,128]{3,2,1,0:T(8,128)(2,1)S(1)}, bf16[2,2,256,128]{3,2,1,0:T(8,128)(2,1)}, u32[]{:S(2)}) copy-start(bf16[2,2,256,128]{3,2,1,0:T(8,128)(2,1)} %get-tuple-element.163) | copy-start | bytes 786436
  62.6 13.2 %collective-permute-start.23 = (bf16[2,2,256,128]{3,2,1,0:T(8,128)(2,1)S(1)}, bf16[2,2,256,128]{3,2,1,0:T(8,128)(2,1)S(1)}, u32[]{:S(2)}, u32[]{:S(2)}) collective-permute-start(bf16[2,2,256,128]{3,2,1,0:T(8,128)(2,1)S(1)} %get-tuple-element.170), channel_id=1, source_target_pairs={{0,8},{4,12},{8,0},{12,4},{1,9},{5,13},{9,1},{13,5},{2,10},{6,14},... | collective-permute-start | bytes 786440 | tf_op jit(solution)/shard_map/ppermute | solution.py:36
  69.1 6.0 %copy-start.23 = (bf16[1,2,256,128]{3,2,1,0:T(8,128)(2,1)S(1)}, bf16[1,2,256,128]{3,2,1,0:T(8,128)(2,1)}, u32[]{:S(2)}) copy-start(bf16[1,2,256,128]{3,2,1,0:T(8,128)(2,1)} %get-tuple-element.168) | copy-start | bytes 393220
  73.8 1.7 %collective-permute-start.22 = (bf16[2,1,2,256,128]{4,3,2,1,0:T(8,128)(2,1)}, bf16[2,1,2,256,128]{4,3,2,1,0:T(8,128)(2,1)S(1)}, u32[]{:S(2)}, u32[]{:S(2)}) collective-permute-start(bf16[2,1,2,256,128]{4,3,2,1,0:T(8,128)(2,1)} %get-tuple-element.159), channel_id=1, source_target_pairs={{0,16},{16,0},{1,17},{17,1},{2,18},{18,2},{3,19},{19,3},{4,20},{20... | collective-permute-start | bytes 786440 | tf_op jit(solution)/shard_map/ppermute | solution.py:40
  75.6 5.7 %copy-start.20 = (bf16[1,2,256,128]{3,2,1,0:T(8,128)(2,1)S(1)}, bf16[1,2,256,128]{3,2,1,0:T(8,128)(2,1)}, u32[]{:S(2)}) copy-start(bf16[1,2,256,128]{3,2,1,0:T(8,128)(2,1)} %get-tuple-element.176) | copy-start | bytes 393220
  75.9 5.4 %collective-permute-start.24 = (bf16[1,2,256,128]{3,2,1,0:T(8,128)(2,1)S(1)}, bf16[1,2,256,128]{3,2,1,0:T(8,128)(2,1)S(1)}, u32[]{:S(2)}, u32[]{:S(2)}) collective-permute-start(bf16[1,2,256,128]{3,2,1,0:T(8,128)(2,1)S(1)} %get-tuple-element.172), channel_id=1, source_target_pairs={{0,8},{4,12},{8,0},{12,4},{1,9},{5,13},{9,1},{13,5},{2,10},{6,14},... | collective-permute-start | bytes 393224 | tf_op jit(solution)/shard_map/ppermute | solution.py:36
  77.0 4.3 %collective-permute-start.25 = (bf16[2,1,2,256,128]{4,3,2,1,0:T(8,128)(2,1)S(1)}, bf16[2,1,2,256,128]{4,3,2,1,0:T(8,128)(2,1)S(1)}, u32[]{:S(2)}, u32[]{:S(2)}) collective-permute-start(bf16[2,1,2,256,128]{4,3,2,1,0:T(8,128)(2,1)S(1)} %copy-done.28), channel_id=1, source_target_pairs={{0,16},{16,0},{1,17},{17,1},{2,18},{18,2},{3,19},{19,3},{4,20},{20... | collective-permute-start | bytes 786440 | tf_op jit(solution)/shard_map/ppermute | solution.py:40
  77.0 11.9 %collective-permute-start.28 = (bf16[3,2,256,128]{3,2,1,0:T(8,128)(2,1)S(1)}, bf16[3,2,256,128]{3,2,1,0:T(8,128)(2,1)S(1)}, u32[]{:S(2)}, u32[]{:S(2)}) collective-permute-start(bf16[3,2,256,128]{3,2,1,0:T(8,128)(2,1)S(1)} %pad_maximum_fusion.7), channel_id=1, source_target_pairs={{0,4},{4,0},{8,12},{12,8},{1,5},{5,1},{9,13},{13,9},{2,6},{6,2},{1... | collective-permute-start | bytes 1179656 | tf_op jit(solution)/shard_map/ppermute | solution.py:27
  78.1 10.8 %copy-start.14 = (bf16[2,2,256,128]{3,2,1,0:T(8,128)(2,1)S(1)}, bf16[2,2,256,128]{3,2,1,0:T(8,128)(2,1)}, u32[]{:S(2)}) copy-start(bf16[2,2,256,128]{3,2,1,0:T(8,128)(2,1)} %get-tuple-element.183) | copy-start | bytes 786436
  78.1 10.8 %copy-start.16 = (bf16[2,2,256,128]{3,2,1,0:T(8,128)(2,1)S(1)}, bf16[2,2,256,128]{3,2,1,0:T(8,128)(2,1)}, u32[]{:S(2)}) copy-start(bf16[2,2,256,128]{3,2,1,0:T(8,128)(2,1)} %copy-done.15) | copy-start | bytes 786436
  78.1 10.8 %copy-start.17 = (bf16[2,2,256,128]{3,2,1,0:T(8,128)(2,1)S(1)}, bf16[2,2,256,128]{3,2,1,0:T(8,128)(2,1)}, u32[]{:S(2)}) copy-start(bf16[2,2,256,128]{3,2,1,0:T(8,128)(2,1)} %get-tuple-element.184) | copy-start | bytes 786436
  78.2 10.8 %copy-start.18 = (bf16[1,2,256,128]{3,2,1,0:T(8,128)(2,1)S(1)}, bf16[1,2,256,128]{3,2,1,0:T(8,128)(2,1)}, u32[]{:S(2)}) copy-start(bf16[1,2,256,128]{3,2,1,0:T(8,128)(2,1)} %get-tuple-element.185) | copy-start | bytes 393220
  81.4 10.0 %collective-permute-start.26 = (bf16[1,2,256,128]{3,2,1,0:T(8,128)(2,1)S(1)}, bf16[1,2,256,128]{3,2,1,0:T(8,128)(2,1)S(1)}, u32[]{:S(2)}, u32[]{:S(2)}) collective-permute-start(bf16[1,2,256,128]{3,2,1,0:T(8,128)(2,1)S(1)} %fusion.16), channel_id=1, source_target_pairs={{0,4},{4,0},{8,12},{12,8},{1,5},{5,1},{9,13},{13,9},{2,6},{6,2},{1... | collective-permute-start | bytes 393224 | tf_op jit(solution)/shard_map/ppermute | solution.py:27
  82.1 9.7 %collective-permute-start.27 = (bf16[3,2,256,128]{3,2,1,0:T(8,128)(2,1)S(1)}, bf16[3,2,256,128]{3,2,1,0:T(8,128)(2,1)S(1)}, u32[]{:S(2)}, u32[]{:S(2)}) collective-permute-start(bf16[3,2,256,128]{3,2,1,0:T(8,128)(2,1)S(1)} %pad_maximum_fusion.8), channel_id=1, source_target_pairs={{0,8},{4,12},{8,0},{12,4},{1,9},{5,13},{9,1},{13,5},{2,10},{6,14},... | collective-permute-start | bytes 1179656 | tf_op jit(solution)/shard_map/ppermute | solution.py:36
  (12 other events, 21.5 us)

commit v5 on v4

--- a/solution.py
+++ b/solution.py
@@ -180,7 +180,7 @@
         in_specs=[whole, here, there, here, here, there, there, here, here, there, there],
         out_specs=[one] * 6 + [per_head] * 2,
         out_shape=[
-            pltpu.HBM(shape, jnp.bfloat16) for shape in [pairs] * 6 + [spread] * 2
+            jax.ShapeDtypeStruct(shape, jnp.bfloat16) for shape in [pairs] * 6 + [spread] * 2
         ],
         scratch_shapes=[
             pltpu.VMEM((2, 6, rows, rows), jnp.float32),

time: 94.5 us -> 93.5 us (0.989)
  Pallas kernels: 24.1 us -> 21.7 us
  starting transfers between devices: 19.4 us -> 20.7 us
    pallas_call x3, Pallas kernels: 24.1 us -> 21.7 us  [attention(): pl.pallas_call(attention_kernel, grid=(heads,), in_specs=[whole, here, th...]
    another operation x2, other arithmetic: 1.53 us -> 2.61 us  [by_head(): pair = jnp.stack(arrays).reshape(len(arrays), frames, lats, lons, heads, HD)]
    convert_element_type x3, other arithmetic: 2.09 us -> 1.05 us  [rounded(): return total(near, twin, block).astype(jnp.bfloat16)]
    convert_element_type x3, other arithmetic: 0.27 us -> 1.22 us  [on_device(): (total(near, twin, 0) + ahead.astype(jnp.float32)).astype(jnp.bfloat16)]
  transfers between devices with their start and end apart: 29 -> 29, of which waited for: 13 -> 15; matrix products, arithmetic and copies ran while one was open for 10% -> 9% of each run, Pallas kernels for 26% -> 23%
where the time goes in v5:
time: 93.5 us; the launch traced here: 93.2 us
  waiting for transfers between devices  35 us (37%)
  Pallas kernels  21.7 us (23%)
  starting transfers between devices  20.7 us (22%)
  other arithmetic  7.89 us (8%)
  local copies, waits for them, and re-layouts  6.77 us (7%)
  between operations  1.08 us (1%)
    ppermute x9, waiting for transfers between devices, to_partner(): return lax.ppermute(block, 'lon', [(i, i ^ 1) for i in range(count)])  28.5 us
    pallas_call x3, Pallas kernels, attention(): pl.pallas_call(attention_kernel, grid=(heads,), in_specs=[whole, here, th...  21.7 us
    ppermute x9, starting transfers between devices, to_partner(): return lax.ppermute(block, 'lon', [(i, i ^ 1) for i in range(count)])  9.35 us
    ppermute x8, starting transfers between devices, to_far(): return lax.ppermute(block, 'lon', route)  9.08 us
    ppermute x12, waiting for transfers between devices, to_twin(): return lax.ppermute(block, 'tm', [(0, 1), (1, 0)])  3.37 us
    ppermute x8, waiting for transfers between devices, to_far(): return lax.ppermute(block, 'lon', route)  3.17 us
    another operation x2, other arithmetic, by_head(): pair = jnp.stack(arrays).reshape(len(arrays), frames, lats, lons, heads, HD)  2.61 us
    ppermute x12, starting transfers between devices, to_twin(): return lax.ppermute(block, 'tm', [(0, 1), (1, 0)])  2.27 us
  transfers between devices with their start and end apart: 29, of which 15 were waited for; matrix products, arithmetic and copies ran while one was open for 9% of the time, Pallas kernels for 23%

profile of v5, /device:TPU:0, one launch (start us, length us, event | category | flops | bytes accessed | tf_op | source)
XLA Modules:
  0.0 93.2 jit_solution(4301803133307725697)
XLA Ops:
  0.6 1.4 %pad_maximum_fusion = bf16[2,4,8,8,10,128]{5,3,4,2,1,0:T(8,128)(2,1)S(1)} fusion(bf16[1,4,8,8,10,128]{5,3,4,2,1,0:T(8,128)(2,1)} %bitcast.93, bf16[1,4,8,8,10,128]{5,3,4,2,1,0:T(8,128)(2,1)} %bitcast.94), kind=kLoop, calls=%fused_computation | loop fusion | flops 655360 | bytes 2621440 | tf_op jit(solution)/shard_map/stack | solution.py:223
  2.1 0.4 copy.20
  2.5 0.5 collective-permute-start.6
  3.0 2.6 %collective-permute-start.3 = (bf16[5,2,256,128]{3,2,1,0:T(8,128)(2,1)S(1)}, bf16[5,2,256,128]{3,2,1,0:T(8,128)(2,1)}, u32[]{:S(2)}, u32[]{:S(2)}) collective-permute-start(bf16[5,2,256,128]{3,2,1,0:T(8,128)(2,1)S(1)} %constant_dynamic-slice_fusion.3.own_a), channel_id=1, source_target_pairs={{0,8},{4,12},{8,0},{12,4},{1,9},{5,13},{9,1},{13,5},{2,10},{6,14},... | collective-permute-start | bytes 1966088 | tf_op jit(solution)/shard_map/ppermute | solution.py:36
  5.6 1.5 %collective-permute-start.5 = (s32[2,2]{1,0:T(2,128)S(1)}, s32[2,2]{1,0:T(2,128)S(1)}, u32[]{:S(2)}, u32[]{:S(2)}) collective-permute-start(s32[2,2]{1,0:T(2,128)S(1)} %bitcast.104), channel_id=1, source_target_pairs={{0,4},{4,0},{8,12},{12,8},{1,5},{5,1},{9,13},{13,9},{2,6},{6,2},{1... | collective-permute-start | bytes 56 | tf_op jit(solution)/shard_map/ppermute | solution.py:27
  7.2 0.6 collective-permute-start
  7.8 1.6 %collective-permute-start.4 = (bf16[3,2,256,128]{3,2,1,0:T(8,128)(2,1)S(1)}, bf16[3,2,256,128]{3,2,1,0:T(8,128)(2,1)S(1)}, u32[]{:S(2)}, u32[]{:S(2)}) collective-permute-start(bf16[3,2,256,128]{3,2,1,0:T(8,128)(2,1)S(1)} %constant_dynamic-slice_fusion.5), channel_id=1, source_target_pairs={{0,4},{4,0},{8,12},{12,8},{1,5},{5,1},{9,13},{13,9},{2,6},{6,2},{1... | collective-permute-start | bytes 1179656 | tf_op jit(solution)/shard_map/ppermute | solution.py:27
  9.3 1.2 %pad_maximum_fusion.1 = bf16[2,4,8,8,10,128]{5,3,4,2,1,0:T(8,128)(2,1)S(1)} fusion(bf16[1,4,8,8,10,128]{5,3,4,2,1,0:T(8,128)(2,1)S(1)} %bitcast.95, bf16[1,4,8,8,10,128]{5,3,4,2,1,0:T(8,128)(2,1)} %bitcast.96), kind=kLoop, calls=%fused_computation.1 | loop fusion | flops 655360 | bytes 2621440 | tf_op jit(solution)/shard_map/stack | solution.py:223
  10.6 0.4 copy.21
  11.0 0.9 constant_dynamic-slice_fusion.2.own_q
  11.9 4.6 %collective-permute-done.par_a = bf16[2,2,256,128]{3,2,1,0:T(8,128)(2,1)} collective-permute-done((bf16[2,2,256,128]{3,2,1,0:T(8,128)(2,1)S(1)}, bf16[2,2,256,128]{3,2,1,0:T(8,128)(2,1)}, u32[]{:S(2)}, u32[]{:S(2)}) %collective-permute-start) | collective-permute-done | bytes 262176 | tf_op jit(solution)/shard_map/ppermute | solution.py:27
  16.5 0.5 collective-permute-start.2
  17.1 0.5 collective-permute-start.1
  17.6 7.3 %collective-permute-done.4.par_a = bf16[3,2,256,128]{3,2,1,0:T(8,128)(2,1)S(1)} collective-permute-done((bf16[3,2,256,128]{3,2,1,0:T(8,128)(2,1)S(1)}, bf16[3,2,256,128]{3,2,1,0:T(8,128)(2,1)S(1)}, u32[]{:S(2)}, u32[]{:S(2)}) %collective-permute-start.4) | collective-permute-done | bytes 393248 | tf_op jit(solution)/shard_map/ppermute | solution.py:27
  24.8 4.5 %collective-permute-done.2.par_q = bf16[2,2,256,128]{3,2,1,0:T(8,128)(2,1)S(1)} collective-permute-done((bf16[2,2,256,128]{3,2,1,0:T(8,128)(2,1)S(1)}, bf16[2,2,256,128]{3,2,1,0:T(8,128)(2,1)S(1)}, u32[]{:S(2)}, u32[]{:S(2)}) %collective-permute-start.2) | collective-permute-done | bytes 262176 | tf_op jit(solution)/shard_map/ppermute | solution.py:27
  29.6 0.5 collective-permute-start.8
  30.6 0.6 collective-permute-start.11
  31.5 1.0 %collective-permute-done.8.par_b = bf16[2,2,256,128]{3,2,1,0:T(8,128)(2,1)S(1)} collective-permute-done((bf16[2,2,256,128]{3,2,1,0:T(8,128)(2,1)}, bf16[2,2,256,128]{3,2,1,0:T(8,128)(2,1)S(1)}, u32[]{:S(2)}, u32[]{:S(2)}) %collective-permute-start.8) | collective-permute-done | bytes 262176 | tf_op jit(solution)/shard_map/ppermute | solution.py:40
  32.8 0.4 copy-done.16
  33.4 8.4 %attention.3 = (bf16[2,2,256,128]{3,2,1,0:T(8,128)(2,1)S(1)}, bf16[2,2,256,128]{3,2,1,0:T(8,128)(2,1)S(1)}, bf16[2,2,256,128]{3,2,1,0:T(8,128)(2,1)S(1)}, bf16[2...) custom-call(f32[2,3,8,256]{3,2,1,0:T(8,128)S(1)} %fusion.18.bias_ref, ...), custom_call_target="tpu_custom_call" | custom-call | flops 2415919104 | bytes 3670016 | tf_op jit(solution)/shard_map/attention/pallas_call | solution.py:177
  41.8 0.3 collective-permute-done.11.par_q
  42.5 0.5 collective-permute-start.14
  43.0 2.0 %collective-permute-done.14.rel_b = bf16[3,2,256,128]{3,2,1,0:T(8,128)(2,1)S(1)} collective-permute-done((bf16[3,2,256,128]{3,2,1,0:T(8,128)(2,1)S(1)}, bf16[3,2,256,128]{3,2,1,0:T(8,128)(2,1)S(1)}, u32[]{:S(2)}, u32[]{:S(2)}) %collective-permute-start.14) | collective-permute-done | bytes 393248 | tf_op jit(solution)/shard_map/ppermute | solution.py:40
  45.1 1.5 %collective-permute-start.16 = (bf16[2,2,256,128]{3,2,1,0:T(8,128)(2,1)S(1)}, bf16[2,2,256,128]{3,2,1,0:T(8,128)(2,1)S(1)}, u32[]{:S(2)}, u32[]{:S(2)}) collective-permute-start(bf16[2,2,256,128]{3,2,1,0:T(8,128)(2,1)S(1)} %get-tuple-element.138), channel_id=1, source_target_pairs={{0,4},{4,0},{8,12},{12,8},{1,5},{5,1},{9,13},{13,9},{2,6},{6,2},{1... | collective-permute-start | bytes 786440 | tf_op jit(solution)/shard_map/ppermute | solution.py:27
  46.8 0.6 collective-permute-start.15
  47.3 8.6 %attention.4 = (bf16[2,2,256,128]{3,2,1,0:T(8,128)(2,1)S(1)}, bf16[2,2,256,128]{3,2,1,0:T(8,128)(2,1)S(1)}, bf16[2,2,256,128]{3,2,1,0:T(8,128)(2,1)S(1)}, bf16[2...) custom-call(f32[2,3,8,256]{3,2,1,0:T(8,128)S(1)} %fusion.18.bias_ref, ...), custom_call_target="tpu_custom_call" | custom-call | flops 2415919104 | bytes 3670016 | tf_op jit(solution)/shard_map/attention/pallas_call | solution.py:177
  56.2 0.5 copy-done.10
  56.6 0.8 pad_maximum_fusion.6
  57.5 0.4 collective-permute-start.21
  58.1 0.8 fusion.4
  58.9 1.5 %collective-permute-start.19 = (bf16[2,2,256,128]{3,2,1,0:T(8,128)(2,1)}, bf16[2,2,256,128]{3,2,1,0:T(8,128)(2,1)}, u32[]{:S(2)}, u32[]{:S(2)}) collective-permute-start(bf16[2,2,256,128]{3,2,1,0:T(8,128)(2,1)} %get-tuple-element.208), channel_id=1, source_target_pairs={{0,8},{4,12},{8,0},{12,4},{1,9},{5,13},{9,1},{13,5},{2,10},{6,14},... | collective-permute-start | bytes 786440 | tf_op jit(solution)/shard_map/ppermute | solution.py:36
  60.5 0.5 collective-permute-start.23
  61.0 4.8 %attention.5 = (bf16[1,2,256,128]{3,2,1,0:T(8,128)(2,1)S(1)}, bf16[1,2,256,128]{3,2,1,0:T(8,128)(2,1)S(1)}, bf16[1,2,256,128]{3,2,1,0:T(8,128)(2,1)S(1)}, bf16[1...) custom-call(f32[2,3,8,256]{3,2,1,0:T(8,128)S(1)} %fusion.18.bias_ref, ...), custom_call_target="tpu_custom_call" | custom-call | flops 1207959552 | bytes 1835008 | tf_op jit(solution)/shard_map/attention/pallas_call | solution.py:177
  65.8 5.8 %collective-permute-done.21 = bf16[4,2,256,128]{3,2,1,0:T(8,128)(2,1)S(1)} collective-permute-done((bf16[4,2,256,128]{3,2,1,0:T(8,128)(2,1)}, bf16[4,2,256,128]{3,2,1,0:T(8,128)(2,1)S(1)}, u32[]{:S(2)}, u32[]{:S(2)}) %collective-permute-start.21) | collective-permute-done | bytes 524320 | tf_op jit(solution)/shard_map/ppermute | solution.py:27
  71.6 1.1 %fusion.7 = bf16[2,2,256,128]{3,2,1,0:T(8,128)(2,1)S(1)} fusion(bf16[2,2,256,128]{3,2,1,0:T(8,128)(2,1)} %collective-permute-done.19, bf16[2,2,256,128]{3,2,1,0:T(8,128)(2,1)S(1)} %get-tuple-element.163, bf16[2,2,2,256,128]{4,3,2,1,0:T(8,128)(2,1)} %collective-permute-done.20), kind=kLoop, calls=%fused_computation.29 | loop fusion | flops 786432 | bytes 1048576 | tf_op jit(solution)/shard_map/convert_element_type | solution.py:268
  72.8 0.3 collective-permute-done.22
  73.4 1.6 %collective-permute-start.24 = (bf16[1,2,256,128]{3,2,1,0:T(8,128)(2,1)S(1)}, bf16[1,2,256,128]{3,2,1,0:T(8,128)(2,1)S(1)}, u32[]{:S(2)}, u32[]{:S(2)}) collective-permute-start(bf16[1,2,256,128]{3,2,1,0:T(8,128)(2,1)S(1)} %get-tuple-element.172), channel_id=1, source_target_pairs={{0,8},{4,12},{8,0},{12,4},{1,9},{5,13},{9,1},{13,5},{2,10},{6,14},... | collective-permute-start | bytes 393224 | tf_op jit(solution)/shard_map/ppermute | solution.py:36
  75.0 1.5 %collective-permute-start.28 = (bf16[3,2,256,128]{3,2,1,0:T(8,128)(2,1)S(1)}, bf16[3,2,256,128]{3,2,1,0:T(8,128)(2,1)S(1)}, u32[]{:S(2)}, u32[]{:S(2)}) collective-permute-start(bf16[3,2,256,128]{3,2,1,0:T(8,128)(2,1)S(1)} %pad_maximum_fusion.7), channel_id=1, source_target_pairs={{0,4},{4,0},{8,12},{12,8},{1,5},{5,1},{9,13},{13,9},{2,6},{6,2},{1... | collective-permute-start | bytes 1179656 | tf_op jit(solution)/shard_map/ppermute | solution.py:27
  76.6 2.3 %collective-permute-done.24 = bf16[1,2,256,128]{3,2,1,0:T(8,128)(2,1)S(1)} collective-permute-done((bf16[1,2,256,128]{3,2,1,0:T(8,128)(2,1)S(1)}, bf16[1,2,256,128]{3,2,1,0:T(8,128)(2,1)S(1)}, u32[]{:S(2)}, u32[]{:S(2)}) %collective-permute-start.24) | collective-permute-done | bytes 131104 | tf_op jit(solution)/shard_map/ppermute | solution.py:36
  78.9 1.2 %collective-permute-start.26 = (bf16[1,2,256,128]{3,2,1,0:T(8,128)(2,1)S(1)}, bf16[1,2,256,128]{3,2,1,0:T(8,128)(2,1)S(1)}, u32[]{:S(2)}, u32[]{:S(2)}) collective-permute-start(bf16[1,2,256,128]{3,2,1,0:T(8,128)(2,1)S(1)} %fusion.16), channel_id=1, source_target_pairs={{0,4},{4,0},{8,12},{12,8},{1,5},{5,1},{9,13},{13,9},{2,6},{6,2},{1... | collective-permute-start | bytes 393224 | tf_op jit(solution)/shard_map/ppermute | solution.py:27
  80.2 1.5 %collective-permute-start.27 = (bf16[3,2,256,128]{3,2,1,0:T(8,128)(2,1)S(1)}, bf16[3,2,256,128]{3,2,1,0:T(8,128)(2,1)S(1)}, u32[]{:S(2)}, u32[]{:S(2)}) collective-permute-start(bf16[3,2,256,128]{3,2,1,0:T(8,128)(2,1)S(1)} %pad_maximum_fusion.8), channel_id=1, source_target_pairs={{0,8},{4,12},{8,0},{12,4},{1,9},{5,13},{9,1},{13,5},{2,10},{6,14},... | collective-permute-start | bytes 1179656 | tf_op jit(solution)/shard_map/ppermute | solution.py:36
  81.7 5.2 %collective-permute-done.28 = bf16[3,2,256,128]{3,2,1,0:T(8,128)(2,1)S(1)} collective-permute-done((bf16[3,2,256,128]{3,2,1,0:T(8,128)(2,1)S(1)}, bf16[3,2,256,128]{3,2,1,0:T(8,128)(2,1)S(1)}, u32[]{:S(2)}, u32[]{:S(2)}) %collective-permute-start.28) | collective-permute-done | bytes 393248 | tf_op jit(solution)/shard_map/ppermute | solution.py:27
  87.3 1.2 %copy_bitcast_fusion.2 = (bf16[4,8,8,1280]{3,2,1,0:T(8,128)(2,1)}, bf16[4,8,8,1280]{3,2,1,0:T(8,128)(2,1)}) fusion(bf16[1,4,8,8,10,128]{5,3,2,1,0,4:T(8,128)(2,1)S(1)} %get-tuple-element.201, bf16[1,4,8,8,10,128]{5,3,2,1,0,4:T(8,128)(2,1)S(1)} %get-tuple-element.202), kind=kLoop, calls=%fused_computation.10 | loop fusion | bytes 2621440 | tf_op jit(solution)/shard_map/squeeze | solution.py:316
  88.5 0.8 collective-permute-done.26
  89.3 0.4 collective-permute-done.27
  89.7 1.1 %fusion.1 = bf16[2,2,256,128]{3,2,1,0:T(8,128)(2,1)S(1)} fusion(bf16[2,2,256,128]{3,2,1,0:T(8,128)(2,1)S(1)} %get-tuple-element.193, bf16[3,2,256,128]{3,2,1,0:T(8,128)(2,1)S(1)} %collective-permute-done.27, bf16[2,2,2,256,128]{4,3,2,1,0:T(8,128)(2,1)} %collective-permute-done.20), kind=kLoop, calls=%fused_computation.19 | loop fusion | flops 786432 | bytes 1048576 | tf_op jit(solution)/shard_map/convert_element_type | solution.py:322
  91.3 0.9 %copy.26 = bf16[1,4,8,8,10,128]{5,3,4,2,1,0:T(8,128)(2,1)} copy(bf16[1,4,8,8,10,128]{5,3,2,1,0,4:T(8,128)(2,1)S(1)} %get-tuple-element.197) | data formatting | bytes 1310720 | tf_op jit(solution)/shard_map/slice | solution.py:316
  92.3 0.9 %copy.27 = bf16[1,4,8,8,10,128]{5,3,4,2,1,0:T(8,128)(2,1)} copy(bf16[1,4,8,8,10,128]{5,3,2,1,0,4:T(8,128)(2,1)S(1)} %get-tuple-element.198) | data formatting | bytes 1310720 | tf_op jit(solution)/shard_map/slice | solution.py:316
  (95 shorter events, 4.2 us)
Async XLA Ops:
  2.4 3.2 %copy-start.13 = (s32[1,2,2]{2,1,0:T(2,128)S(1)}, s32[1,2,2]{2,1,0:T(2,128)}, u32[]{:S(2)}) copy-start(s32[1,2,2]{2,1,0:T(2,128)} %param.10) | copy-start | bytes 52
  2.4 6.9 %copy-start.2 = (bf16[4,8,8,1280]{3,2,1,0:T(8,128)(2,1)S(1)}, bf16[4,8,8,1280]{3,2,1,0:T(8,128)(2,1)}, u32[]{:S(2)}) copy-start(bf16[4,8,8,1280]{3,2,1,0:T(8,128)(2,1)} %param.9) | copy-start | bytes 1966084
  2.5 8.0 %copy-start = (bf16[5,2,256,128]{3,2,1,0:T(8,128)(2,1)}, bf16[5,2,256,128]{3,2,1,0:T(8,128)(2,1)S(1)}, u32[]{:S(2)}) copy-start(bf16[5,2,256,128]{3,2,1,0:T(8,128)(2,1)S(1)} %constant_dynamic-slice_fusion.3.own_a) | copy-start | bytes 1966084
  2.5 26.8 %collective-permute-start.6 = (bf16[5,2,256,128]{3,2,1,0:T(8,128)(2,1)S(1)}, bf16[5,2,256,128]{3,2,1,0:T(8,128)(2,1)}, u32[]{:S(2)}, u32[]{:S(2)}) collective-permute-start(bf16[5,2,256,128]{3,2,1,0:T(8,128)(2,1)S(1)} %constant_dynamic-slice_fusion.3.own_a), channel_id=1, source_target_pairs={{0,16},{16,0},{1,17},{17,1},{2,18},{18,2},{3,19},{19,3},{4,20},{20... | collective-permute-start | bytes 1966088 | tf_op jit(solution)/shard_map/ppermute | solution.py:40
  3.0 26.3 %collective-permute-start.3 = (bf16[5,2,256,128]{3,2,1,0:T(8,128)(2,1)S(1)}, bf16[5,2,256,128]{3,2,1,0:T(8,128)(2,1)}, u32[]{:S(2)}, u32[]{:S(2)}) collective-permute-start(bf16[5,2,256,128]{3,2,1,0:T(8,128)(2,1)S(1)} %constant_dynamic-slice_fusion.3.own_a), channel_id=1, source_target_pairs={{0,8},{4,12},{8,0},{12,4},{1,9},{5,13},{9,1},{13,5},{2,10},{6,14},... | collective-permute-start | bytes 1966088 | tf_op jit(solution)/shard_map/ppermute | solution.py:36
  5.6 11.4 %collective-permute-start.5 = (s32[2,2]{1,0:T(2,128)S(1)}, s32[2,2]{1,0:T(2,128)S(1)}, u32[]{:S(2)}, u32[]{:S(2)}) collective-permute-start(s32[2,2]{1,0:T(2,128)S(1)} %bitcast.104), channel_id=1, source_target_pairs={{0,4},{4,0},{8,12},{12,8},{1,5},{5,1},{9,13},{13,9},{2,6},{6,2},{1... | collective-permute-start | bytes 56 | tf_op jit(solution)/shard_map/ppermute | solution.py:27
  7.2 9.4 %collective-permute-start = (bf16[2,2,256,128]{3,2,1,0:T(8,128)(2,1)S(1)}, bf16[2,2,256,128]{3,2,1,0:T(8,128)(2,1)}, u32[]{:S(2)}, u32[]{:S(2)}) collective-permute-start(bf16[2,2,256,128]{3,2,1,0:T(8,128)(2,1)S(1)} %constant_dynamic-slice_fusion), channel_id=1, source_target_pairs={{0,4},{4,0},{8,12},{12,8},{1,5},{5,1},{9,13},{13,9},{2,6},{6,2},{1... | collective-permute-start | bytes 786440 | tf_op jit(solution)/shard_map/ppermute | solution.py:27
  7.8 17.0 %collective-permute-start.4 = (bf16[3,2,256,128]{3,2,1,0:T(8,128)(2,1)S(1)}, bf16[3,2,256,128]{3,2,1,0:T(8,128)(2,1)S(1)}, u32[]{:S(2)}, u32[]{:S(2)}) collective-permute-start(bf16[3,2,256,128]{3,2,1,0:T(8,128)(2,1)S(1)} %constant_dynamic-slice_fusion.5), channel_id=1, source_target_pairs={{0,4},{4,0},{8,12},{12,8},{1,5},{5,1},{9,13},{13,9},{2,6},{6,2},{1... | collective-permute-start | bytes 1179656 | tf_op jit(solution)/shard_map/ppermute | solution.py:27
  10.9 6.6 %copy-start.12 = (s32[2,3]{1,0:T(2,128)S(1)}, s32[2,3]{1,0:T(2,128)}, u32[]{:S(2)}) copy-start(s32[2,3]{1,0:T(2,128)} %constant.49.clone) | copy-start | bytes 76
  16.5 12.8 %collective-permute-start.2 = (bf16[2,2,256,128]{3,2,1,0:T(8,128)(2,1)S(1)}, bf16[2,2,256,128]{3,2,1,0:T(8,128)(2,1)S(1)}, u32[]{:S(2)}, u32[]{:S(2)}) collective-permute-start(bf16[2,2,256,128]{3,2,1,0:T(8,128)(2,1)S(1)} %constant_dynamic-slice_fusion.1), channel_id=1, source_target_pairs={{0,4},{4,0},{8,12},{12,8},{1,5},{5,1},{9,13},{13,9},{2,6},{6,2},{1... | collective-permute-start | bytes 786440 | tf_op jit(solution)/shard_map/ppermute | solution.py:27
  17.1 12.3 %collective-permute-start.1 = (bf16[2,2,256,128]{3,2,1,0:T(8,128)(2,1)}, bf16[2,2,256,128]{3,2,1,0:T(8,128)(2,1)S(1)}, u32[]{:S(2)}, u32[]{:S(2)}) collective-permute-start(bf16[2,2,256,128]{3,2,1,0:T(8,128)(2,1)} %collective-permute-done.par_a), channel_id=1, source_target_pairs={{0,8},{4,12},{8,0},{12,4},{1,9},{5,13},{9,1},{13,5},{2,10},{6,14},... | collective-permute-start | bytes 786440 | tf_op jit(solution)/shard_map/ppermute | solution.py:36
  24.8 17.0 %copy-start.6 = (bf16[3,2,256,128]{3,2,1,0:T(8,128)(2,1)}, bf16[3,2,256,128]{3,2,1,0:T(8,128)(2,1)S(1)}, u32[]{:S(2)}) copy-start(bf16[3,2,256,128]{3,2,1,0:T(8,128)(2,1)S(1)} %collective-permute-done.4.par_a) | copy-start | bytes 1179652
  29.4 3.5 %copy-start.14 = (bf16[2,2,256,128]{3,2,1,0:T(8,128)(2,1)}, bf16[2,2,256,128]{3,2,1,0:T(8,128)(2,1)S(1)}, u32[]{:S(2)}) copy-start(bf16[2,2,256,128]{3,2,1,0:T(8,128)(2,1)S(1)} %collective-permute-done.2.par_q) | copy-start | bytes 786436
  29.4 3.4 %copy-start.15 = (bf16[2,2,256,128]{3,2,1,0:T(8,128)(2,1)}, bf16[2,2,256,128]{3,2,1,0:T(8,128)(2,1)S(1)}, u32[]{:S(2)}) copy-start(bf16[2,2,256,128]{3,2,1,0:T(8,128)(2,1)S(1)} %collective-permute-done.1.rel_a) | copy-start | bytes 786436
  29.4 3.1 %collective-permute-start.9 = (bf16[5,2,256,128]{3,2,1,0:T(8,128)(2,1)}, bf16[5,2,256,128]{3,2,1,0:T(8,128)(2,1)S(1)}, u32[]{:S(2)}, u32[]{:S(2)}) collective-permute-start(bf16[5,2,256,128]{3,2,1,0:T(8,128)(2,1)} %collective-permute-done.3.yown_a), channel_id=1, source_target_pairs={{0,16},{16,0},{1,17},{17,1},{2,18},{18,2},{3,19},{19,3},{4,20},{20... | collective-permute-start | bytes 1966088 | tf_op jit(solution)/shard_map/ppermute | solution.py:40
  29.6 3.0 %collective-permute-start.8 = (bf16[2,2,256,128]{3,2,1,0:T(8,128)(2,1)}, bf16[2,2,256,128]{3,2,1,0:T(8,128)(2,1)S(1)}, u32[]{:S(2)}, u32[]{:S(2)}) collective-permute-start(bf16[2,2,256,128]{3,2,1,0:T(8,128)(2,1)} %collective-permute-done.par_a), channel_id=1, source_target_pairs={{0,16},{16,0},{1,17},{17,1},{2,18},{18,2},{3,19},{19,3},{4,20},{20... | collective-permute-start | bytes 786440 | tf_op jit(solution)/shard_map/ppermute | solution.py:40
  30.0 2.5 %collective-permute-start.7 = (bf16[2,2,256,128]{3,2,1,0:T(8,128)(2,1)S(1)}, bf16[2,2,256,128]{3,2,1,0:T(8,128)(2,1)S(1)}, u32[]{:S(2)}, u32[]{:S(2)}) collective-permute-start(bf16[2,2,256,128]{3,2,1,0:T(8,128)(2,1)S(1)} %collective-permute-done.1.rel_a), channel_id=1, source_target_pairs={{0,16},{16,0},{1,17},{17,1},{2,18},{18,2},{3,19},{19,3},{4,20},{20... | collective-permute-start | bytes 786440 | tf_op jit(solution)/shard_map/ppermute | solution.py:40
  30.6 11.5 %collective-permute-start.11 = (bf16[3,2,256,128]{3,2,1,0:T(8,128)(2,1)S(1)}, bf16[3,2,256,128]{3,2,1,0:T(8,128)(2,1)S(1)}, u32[]{:S(2)}, u32[]{:S(2)}) collective-permute-start(bf16[3,2,256,128]{3,2,1,0:T(8,128)(2,1)S(1)} %constant_dynamic-slice_fusion.4), channel_id=1, source_target_pairs={{0,4},{4,0},{8,12},{12,8},{1,5},{5,1},{9,13},{13,9},{2,6},{6,2},{1... | collective-permute-start | bytes 1179656 | tf_op jit(solution)/shard_map/ppermute | solution.py:27
  31.3 11.2 %collective-permute-start.10 = (bf16[3,2,256,128]{3,2,1,0:T(8,128)(2,1)S(1)}, bf16[3,2,256,128]{3,2,1,0:T(8,128)(2,1)S(1)}, u32[]{:S(2)}, u32[]{:S(2)}) collective-permute-start(bf16[3,2,256,128]{3,2,1,0:T(8,128)(2,1)S(1)} %collective-permute-done.4.par_a), channel_id=1, source_target_pairs={{0,8},{4,12},{8,0},{12,4},{1,9},{5,13},{9,1},{13,5},{2,10},{6,14},... | collective-permute-start | bytes 1179656 | tf_op jit(solution)/shard_map/ppermute | solution.py:36
  32.5 0.7 copy-start.16
  32.5 0.9 copy-start.3
  32.5 9.9 %collective-permute-start.12 = (bf16[3,2,256,128]{3,2,1,0:T(8,128)(2,1)S(1)}, bf16[3,2,256,128]{3,2,1,0:T(8,128)(2,1)S(1)}, u32[]{:S(2)}, u32[]{:S(2)}) collective-permute-start(bf16[3,2,256,128]{3,2,1,0:T(8,128)(2,1)S(1)} %collective-permute-done.4.par_a), channel_id=1, source_target_pairs={{0,16},{16,0},{1,17},{17,1},{2,18},{18,2},{3,19},{19,3},{4,20},{20... | collective-permute-start | bytes 1179656 | tf_op jit(solution)/shard_map/ppermute | solution.py:40
  42.2 5.2 %copy-start.7 = (bf16[3,2,256,128]{3,2,1,0:T(8,128)(2,1)}, bf16[3,2,256,128]{3,2,1,0:T(8,128)(2,1)S(1)}, u32[]{:S(2)}) copy-start(bf16[3,2,256,128]{3,2,1,0:T(8,128)(2,1)S(1)} %collective-permute-done.11.par_q) | copy-start | bytes 1179652
  42.4 4.9 %copy-start.8 = (bf16[3,2,256,128]{3,2,1,0:T(8,128)(2,1)}, bf16[3,2,256,128]{3,2,1,0:T(8,128)(2,1)S(1)}, u32[]{:S(2)}) copy-start(bf16[3,2,256,128]{3,2,1,0:T(8,128)(2,1)S(1)} %collective-permute-done.10.rel_a) | copy-start | bytes 1179652
  42.4 4.9 %copy-start.9 = (bf16[3,2,256,128]{3,2,1,0:T(8,128)(2,1)}, bf16[3,2,256,128]{3,2,1,0:T(8,128)(2,1)S(1)}, u32[]{:S(2)}) copy-start(bf16[3,2,256,128]{3,2,1,0:T(8,128)(2,1)S(1)} %collective-permute-done.12.par_b) | copy-start | bytes 1179652
  42.4 2.5 %collective-permute-start.13 = (bf16[2,2,2,256,128]{4,3,2,1,0:T(8,128)(2,1)S(1)}, bf16[2,2,2,256,128]{4,3,2,1,0:T(8,128)(2,1)S(1)}, u32[]{:S(2)}, u32[]{:S(2)}) collective-permute-start(bf16[2,2,2,256,128]{4,3,2,1,0:T(8,128)(2,1)S(1)} %get-tuple-element.126), channel_id=1, source_target_pairs={{0,16},{16,0},{1,17},{17,1},{2,18},{18,2},{3,19},{19,3},{4,20},{20... | collective-permute-start | bytes 1572872 | tf_op jit(solution)/shard_map/ppermute | solution.py:40
  42.5 2.5 %collective-permute-start.14 = (bf16[3,2,256,128]{3,2,1,0:T(8,128)(2,1)S(1)}, bf16[3,2,256,128]{3,2,1,0:T(8,128)(2,1)S(1)}, u32[]{:S(2)}, u32[]{:S(2)}) collective-permute-start(bf16[3,2,256,128]{3,2,1,0:T(8,128)(2,1)S(1)} %collective-permute-done.10.rel_a), channel_id=1, source_target_pairs={{0,16},{16,0},{1,17},{17,1},{2,18},{18,2},{3,19},{19,3},{4,20},{20... | collective-permute-start | bytes 1179656 | tf_op jit(solution)/shard_map/ppermute | solution.py:40
  45.0 11.0 %collective-permute-start.17 = (bf16[2,2,2,256,128]{4,3,2,1,0:T(8,128)(2,1)S(1)}, bf16[2,2,2,256,128]{4,3,2,1,0:T(8,128)(2,1)S(1)}, u32[]{:S(2)}, u32[]{:S(2)}) collective-permute-start(bf16[2,2,2,256,128]{4,3,2,1,0:T(8,128)(2,1)S(1)} %get-tuple-element.140), channel_id=1, source_target_pairs={{0,16},{16,0},{1,17},{17,1},{2,18},{18,2},{3,19},{19,3},{4,20},{20... | collective-permute-start | bytes 1572872 | tf_op jit(solution)/shard_map/ppermute | solution.py:40
  45.1 10.8 %collective-permute-start.16 = (bf16[2,2,256,128]{3,2,1,0:T(8,128)(2,1)S(1)}, bf16[2,2,256,128]{3,2,1,0:T(8,128)(2,1)S(1)}, u32[]{:S(2)}, u32[]{:S(2)}) collective-permute-start(bf16[2,2,256,128]{3,2,1,0:T(8,128)(2,1)S(1)} %get-tuple-element.138), channel_id=1, source_target_pairs={{0,4},{4,0},{8,12},{12,8},{1,5},{5,1},{9,13},{13,9},{2,6},{6,2},{1... | collective-permute-start | bytes 786440 | tf_op jit(solution)/shard_map/ppermute | solution.py:27
  46.8 9.2 %collective-permute-start.15 = (bf16[2,2,256,128]{3,2,1,0:T(8,128)(2,1)S(1)}, bf16[2,2,256,128]{3,2,1,0:T(8,128)(2,1)S(1)}, u32[]{:S(2)}, u32[]{:S(2)}) collective-permute-start(bf16[2,2,256,128]{3,2,1,0:T(8,128)(2,1)S(1)} %get-tuple-element.210), channel_id=1, source_target_pairs={{0,8},{4,12},{8,0},{12,4},{1,9},{5,13},{9,1},{13,5},{2,10},{6,14},... | collective-permute-start | bytes 786440 | tf_op jit(solution)/shard_map/ppermute | solution.py:36
  55.9 0.7 copy-start.10
  56.0 3.0 %copy-start.4 = (bf16[2,2,2,256,128]{4,3,2,1,0:T(8,128)(2,1)}, bf16[2,2,2,256,128]{4,3,2,1,0:T(8,128)(2,1)S(1)}, u32[]{:S(2)}) copy-start(bf16[2,2,2,256,128]{4,3,2,1,0:T(8,128)(2,1)S(1)} %collective-permute-done.17) | copy-start | bytes 1572868
  56.0 2.0 %collective-permute-start.18 = (bf16[2,2,2,256,128]{4,3,2,1,0:T(8,128)(2,1)S(1)}, bf16[2,2,2,256,128]{4,3,2,1,0:T(8,128)(2,1)S(1)}, u32[]{:S(2)}, u32[]{:S(2)}) collective-permute-start(bf16[2,2,2,256,128]{4,3,2,1,0:T(8,128)(2,1)S(1)} %get-tuple-element.143), channel_id=1, source_target_pairs={{0,16},{16,0},{1,17},{17,1},{2,18},{18,2},{3,19},{19,3},{4,20},{20... | collective-permute-start | bytes 1572872 | tf_op jit(solution)/shard_map/ppermute | solution.py:40
  57.5 14.1 %collective-permute-start.21 = (bf16[4,2,256,128]{3,2,1,0:T(8,128)(2,1)}, bf16[4,2,256,128]{3,2,1,0:T(8,128)(2,1)S(1)}, u32[]{:S(2)}, u32[]{:S(2)}) collective-permute-start(bf16[4,2,256,128]{3,2,1,0:T(8,128)(2,1)} %pad_maximum_fusion.6), channel_id=1, source_target_pairs={{0,4},{4,0},{8,12},{12,8},{1,5},{5,1},{9,13},{13,9},{2,6},{6,2},{1... | collective-permute-start | bytes 1572872 | tf_op jit(solution)/shard_map/ppermute | solution.py:27
  58.0 13.6 %collective-permute-start.20 = (bf16[2,2,2,256,128]{4,3,2,1,0:T(8,128)(2,1)S(1)}, bf16[2,2,2,256,128]{4,3,2,1,0:T(8,128)(2,1)}, u32[]{:S(2)}, u32[]{:S(2)}) collective-permute-start(bf16[2,2,2,256,128]{4,3,2,1,0:T(8,128)(2,1)S(1)} %get-tuple-element.150), channel_id=1, source_target_pairs={{0,16},{16,0},{1,17},{17,1},{2,18},{18,2},{3,19},{19,3},{4,20},{20... | collective-permute-start | bytes 1572872 | tf_op jit(solution)/shard_map/ppermute | solution.py:40
  58.9 12.6 %collective-permute-start.19 = (bf16[2,2,256,128]{3,2,1,0:T(8,128)(2,1)}, bf16[2,2,256,128]{3,2,1,0:T(8,128)(2,1)}, u32[]{:S(2)}, u32[]{:S(2)}) collective-permute-start(bf16[2,2,256,128]{3,2,1,0:T(8,128)(2,1)} %get-tuple-element.208), channel_id=1, source_target_pairs={{0,8},{4,12},{8,0},{12,4},{1,9},{5,13},{9,1},{13,5},{2,10},{6,14},... | collective-permute-start | bytes 786440 | tf_op jit(solution)/shard_map/ppermute | solution.py:36
  60.5 12.9 %collective-permute-start.23 = (bf16[2,2,256,128]{3,2,1,0:T(8,128)(2,1)S(1)}, bf16[2,2,256,128]{3,2,1,0:T(8,128)(2,1)S(1)}, u32[]{:S(2)}, u32[]{:S(2)}) collective-permute-start(bf16[2,2,256,128]{3,2,1,0:T(8,128)(2,1)S(1)} %get-tuple-element.170), channel_id=1, source_target_pairs={{0,8},{4,12},{8,0},{12,4},{1,9},{5,13},{9,1},{13,5},{2,10},{6,14},... | collective-permute-start | bytes 786440 | tf_op jit(solution)/shard_map/ppermute | solution.py:36
  71.6 1.5 %collective-permute-start.22 = (bf16[2,1,2,256,128]{4,3,2,1,0:T(8,128)(2,1)S(1)}, bf16[2,1,2,256,128]{4,3,2,1,0:T(8,128)(2,1)S(1)}, u32[]{:S(2)}, u32[]{:S(2)}) collective-permute-start(bf16[2,1,2,256,128]{4,3,2,1,0:T(8,128)(2,1)S(1)} %get-tuple-element.159), channel_id=1, source_target_pairs={{0,16},{16,0},{1,17},{17,1},{2,18},{18,2},{3,19},{19,3},{4,20},{20... | collective-permute-start | bytes 786440 | tf_op jit(solution)/shard_map/ppermute | solution.py:40
  72.7 3.7 %copy-start.5 = (bf16[2,2,2,256,128]{4,3,2,1,0:T(8,128)(2,1)S(1)}, bf16[2,2,2,256,128]{4,3,2,1,0:T(8,128)(2,1)}, u32[]{:S(2)}) copy-start(bf16[2,2,2,256,128]{4,3,2,1,0:T(8,128)(2,1)} %copy-done.4) | copy-start | bytes 1572868
  73.4 5.5 %collective-permute-start.24 = (bf16[1,2,256,128]{3,2,1,0:T(8,128)(2,1)S(1)}, bf16[1,2,256,128]{3,2,1,0:T(8,128)(2,1)S(1)}, u32[]{:S(2)}, u32[]{:S(2)}) collective-permute-start(bf16[1,2,256,128]{3,2,1,0:T(8,128)(2,1)S(1)} %get-tuple-element.172), channel_id=1, source_target_pairs={{0,8},{4,12},{8,0},{12,4},{1,9},{5,13},{9,1},{13,5},{2,10},{6,14},... | collective-permute-start | bytes 393224 | tf_op jit(solution)/shard_map/ppermute | solution.py:36
  75.0 3.9 %collective-permute-start.25 = (bf16[2,1,2,256,128]{4,3,2,1,0:T(8,128)(2,1)S(1)}, bf16[2,1,2,256,128]{4,3,2,1,0:T(8,128)(2,1)S(1)}, u32[]{:S(2)}, u32[]{:S(2)}) collective-permute-start(bf16[2,1,2,256,128]{4,3,2,1,0:T(8,128)(2,1)S(1)} %get-tuple-element.174), channel_id=1, source_target_pairs={{0,16},{16,0},{1,17},{17,1},{2,18},{18,2},{3,19},{19,3},{4,20},{20... | collective-permute-start | bytes 786440 | tf_op jit(solution)/shard_map/ppermute | solution.py:40
  75.0 11.9 %collective-permute-start.28 = (bf16[3,2,256,128]{3,2,1,0:T(8,128)(2,1)S(1)}, bf16[3,2,256,128]{3,2,1,0:T(8,128)(2,1)S(1)}, u32[]{:S(2)}, u32[]{:S(2)}) collective-permute-start(bf16[3,2,256,128]{3,2,1,0:T(8,128)(2,1)S(1)} %pad_maximum_fusion.7), channel_id=1, source_target_pairs={{0,4},{4,0},{8,12},{12,8},{1,5},{5,1},{9,13},{13,9},{2,6},{6,2},{1... | collective-permute-start | bytes 1179656 | tf_op jit(solution)/shard_map/ppermute | solution.py:27
  76.4 10.4 %copy-start.11 = (bf16[2,2,256,128]{3,2,1,0:T(8,128)(2,1)S(1)}, bf16[2,2,256,128]{3,2,1,0:T(8,128)(2,1)}, u32[]{:S(2)}) copy-start(bf16[2,2,256,128]{3,2,1,0:T(8,128)(2,1)} %copy-done.10) | copy-start | bytes 786436
  78.9 10.4 %collective-permute-start.26 = (bf16[1,2,256,128]{3,2,1,0:T(8,128)(2,1)S(1)}, bf16[1,2,256,128]{3,2,1,0:T(8,128)(2,1)S(1)}, u32[]{:S(2)}, u32[]{:S(2)}) collective-permute-start(bf16[1,2,256,128]{3,2,1,0:T(8,128)(2,1)S(1)} %fusion.16), channel_id=1, source_target_pairs={{0,4},{4,0},{8,12},{12,8},{1,5},{5,1},{9,13},{13,9},{2,6},{6,2},{1... | collective-permute-start | bytes 393224 | tf_op jit(solution)/shard_map/ppermute | solution.py:27
  80.2 9.6 %collective-permute-start.27 = (bf16[3,2,256,128]{3,2,1,0:T(8,128)(2,1)S(1)}, bf16[3,2,256,128]{3,2,1,0:T(8,128)(2,1)S(1)}, u32[]{:S(2)}, u32[]{:S(2)}) collective-permute-start(bf16[3,2,256,128]{3,2,1,0:T(8,128)(2,1)S(1)} %pad_maximum_fusion.8), channel_id=1, source_target_pairs={{0,8},{4,12},{8,0},{12,4},{1,9},{5,13},{9,1},{13,5},{2,10},{6,14},... | collective-permute-start | bytes 1179656 | tf_op jit(solution)/shard_map/ppermute | solution.py:36
  86.9 1.7 %copy-start.1 = (bf16[3,2,256,128]{3,2,1,0:T(8,128)(2,1)}, bf16[3,2,256,128]{3,2,1,0:T(8,128)(2,1)S(1)}, u32[]{:S(2)}) copy-start(bf16[3,2,256,128]{3,2,1,0:T(8,128)(2,1)S(1)} %collective-permute-done.28) | copy-start | bytes 1179652
  88.5 2.3 %slice-start = ((bf16[3,2,256,128]{3,2,1,0:T(8,128)(2,1)}), bf16[2,2,256,128]{3,2,1,0:T(8,128)(2,1)S(1)}, s32[]{:S(2)}) async-start(bf16[3,2,256,128]{3,2,1,0:T(8,128)(2,1)} %copy-done.1), calls=%async_computation | async-start | bytes 524288 | tf_op jit(solution)/shard_map/slice | solution.py:308

commit v6 on v5

--- a/solution.py
+++ b/solution.py
@@ -188,7 +188,7 @@
             pltpu.VMEM((2, 6, rows, rows), jnp.float32),
             pltpu.VMEM((8, 2, rows, HD), jnp.float32),
         ],
-        compiler_params=pltpu.CompilerParams(vmem_limit_bytes=26 * 1024 * 1024),
+        compiler_params=pltpu.CompilerParams(vmem_limit_bytes=20 * 1024 * 1024),
         cost_estimate=pl.CostEstimate(
             flops=heads * 2 * 6 * 6 * 2 * rows * rows * HD, bytes_accessed=heads * 28 * rows * HD * 2, transcendentals=0
         ),

time: 93.5 us -> 93.5 us (level)
  no operation moved by 1% of the time
where the time goes in v6:
time: 93.5 us; the launch traced here: 93.2 us
  waiting for transfers between devices  35 us (37%)
  Pallas kernels  21.7 us (23%)
  starting transfers between devices  20.7 us (22%)
  other arithmetic  7.89 us (8%)
  local copies, waits for them, and re-layouts  6.77 us (7%)
  between operations  1.08 us (1%)
    ppermute x9, waiting for transfers between devices, to_partner(): return lax.ppermute(block, 'lon', [(i, i ^ 1) for i in range(count)])  28.5 us
    pallas_call x3, Pallas kernels, attention(): pl.pallas_call(attention_kernel, grid=(heads,), in_specs=[whole, here, th...  21.7 us
    ppermute x9, starting transfers between devices, to_partner(): return lax.ppermute(block, 'lon', [(i, i ^ 1) for i in range(count)])  9.35 us
    ppermute x8, starting transfers between devices, to_far(): return lax.ppermute(block, 'lon', route)  9.08 us
    ppermute x12, waiting for transfers between devices, to_twin(): return lax.ppermute(block, 'tm', [(0, 1), (1, 0)])  3.37 us
    ppermute x8, waiting for transfers between devices, to_far(): return lax.ppermute(block, 'lon', route)  3.17 us
    another operation x2, other arithmetic, by_head(): pair = jnp.stack(arrays).reshape(len(arrays), frames, lats, lons, heads, HD)  2.61 us
    ppermute x12, starting transfers between devices, to_twin(): return lax.ppermute(block, 'tm', [(0, 1), (1, 0)])  2.27 us
  transfers between devices with their start and end apart: 29, of which 15 were waited for; matrix products, arithmetic and copies ran while one was open for 9% of the time, Pallas kernels for 23%

profile of v6, /device:TPU:0, one launch (start us, length us, event | category | flops | bytes accessed | tf_op | source)
XLA Modules:
  0.0 93.2 jit_solution(9701270986468736518)
XLA Ops:
  0.6 1.4 %pad_maximum_fusion = bf16[2,4,8,8,10,128]{5,3,4,2,1,0:T(8,128)(2,1)S(1)} fusion(bf16[1,4,8,8,10,128]{5,3,4,2,1,0:T(8,128)(2,1)} %bitcast.93, bf16[1,4,8,8,10,128]{5,3,4,2,1,0:T(8,128)(2,1)} %bitcast.94), kind=kLoop, calls=%fused_computation | loop fusion | flops 655360 | bytes 2621440 | tf_op jit(solution)/shard_map/stack | solution.py:223
  2.1 0.4 copy.20
  2.5 0.5 collective-permute-start.6
  3.0 2.6 %collective-permute-start.3 = (bf16[5,2,256,128]{3,2,1,0:T(8,128)(2,1)S(1)}, bf16[5,2,256,128]{3,2,1,0:T(8,128)(2,1)}, u32[]{:S(2)}, u32[]{:S(2)}) collective-permute-start(bf16[5,2,256,128]{3,2,1,0:T(8,128)(2,1)S(1)} %constant_dynamic-slice_fusion.3.own_a), channel_id=1, source_target_pairs={{0,8},{4,12},{8,0},{12,4},{1,9},{5,13},{9,1},{13,5},{2,10},{6,14},... | collective-permute-start | bytes 1966088 | tf_op jit(solution)/shard_map/ppermute | solution.py:36
  5.6 1.5 %collective-permute-start.5 = (s32[2,2]{1,0:T(2,128)S(1)}, s32[2,2]{1,0:T(2,128)S(1)}, u32[]{:S(2)}, u32[]{:S(2)}) collective-permute-start(s32[2,2]{1,0:T(2,128)S(1)} %bitcast.104), channel_id=1, source_target_pairs={{0,4},{4,0},{8,12},{12,8},{1,5},{5,1},{9,13},{13,9},{2,6},{6,2},{1... | collective-permute-start | bytes 56 | tf_op jit(solution)/shard_map/ppermute | solution.py:27
  7.2 0.6 collective-permute-start
  7.8 1.6 %collective-permute-start.4 = (bf16[3,2,256,128]{3,2,1,0:T(8,128)(2,1)S(1)}, bf16[3,2,256,128]{3,2,1,0:T(8,128)(2,1)S(1)}, u32[]{:S(2)}, u32[]{:S(2)}) collective-permute-start(bf16[3,2,256,128]{3,2,1,0:T(8,128)(2,1)S(1)} %constant_dynamic-slice_fusion.5), channel_id=1, source_target_pairs={{0,4},{4,0},{8,12},{12,8},{1,5},{5,1},{9,13},{13,9},{2,6},{6,2},{1... | collective-permute-start | bytes 1179656 | tf_op jit(solution)/shard_map/ppermute | solution.py:27
  9.3 1.2 %pad_maximum_fusion.1 = bf16[2,4,8,8,10,128]{5,3,4,2,1,0:T(8,128)(2,1)S(1)} fusion(bf16[1,4,8,8,10,128]{5,3,4,2,1,0:T(8,128)(2,1)S(1)} %bitcast.95, bf16[1,4,8,8,10,128]{5,3,4,2,1,0:T(8,128)(2,1)} %bitcast.96), kind=kLoop, calls=%fused_computation.1 | loop fusion | flops 655360 | bytes 2621440 | tf_op jit(solution)/shard_map/stack | solution.py:223
  10.6 0.4 copy.21
  11.0 0.9 constant_dynamic-slice_fusion.2.own_q
  11.9 4.6 %collective-permute-done.par_a = bf16[2,2,256,128]{3,2,1,0:T(8,128)(2,1)} collective-permute-done((bf16[2,2,256,128]{3,2,1,0:T(8,128)(2,1)S(1)}, bf16[2,2,256,128]{3,2,1,0:T(8,128)(2,1)}, u32[]{:S(2)}, u32[]{:S(2)}) %collective-permute-start) | collective-permute-done | bytes 262176 | tf_op jit(solution)/shard_map/ppermute | solution.py:27
  16.5 0.5 collective-permute-start.2
  17.1 0.5 collective-permute-start.1
  17.6 7.3 %collective-permute-done.4.par_a = bf16[3,2,256,128]{3,2,1,0:T(8,128)(2,1)S(1)} collective-permute-done((bf16[3,2,256,128]{3,2,1,0:T(8,128)(2,1)S(1)}, bf16[3,2,256,128]{3,2,1,0:T(8,128)(2,1)S(1)}, u32[]{:S(2)}, u32[]{:S(2)}) %collective-permute-start.4) | collective-permute-done | bytes 393248 | tf_op jit(solution)/shard_map/ppermute | solution.py:27
  24.8 4.5 %collective-permute-done.2.par_q = bf16[2,2,256,128]{3,2,1,0:T(8,128)(2,1)S(1)} collective-permute-done((bf16[2,2,256,128]{3,2,1,0:T(8,128)(2,1)S(1)}, bf16[2,2,256,128]{3,2,1,0:T(8,128)(2,1)S(1)}, u32[]{:S(2)}, u32[]{:S(2)}) %collective-permute-start.2) | collective-permute-done | bytes 262176 | tf_op jit(solution)/shard_map/ppermute | solution.py:27
  29.6 0.5 collective-permute-start.8
  30.6 0.6 collective-permute-start.11
  31.5 1.0 %collective-permute-done.8.par_b = bf16[2,2,256,128]{3,2,1,0:T(8,128)(2,1)S(1)} collective-permute-done((bf16[2,2,256,128]{3,2,1,0:T(8,128)(2,1)}, bf16[2,2,256,128]{3,2,1,0:T(8,128)(2,1)S(1)}, u32[]{:S(2)}, u32[]{:S(2)}) %collective-permute-start.8) | collective-permute-done | bytes 262176 | tf_op jit(solution)/shard_map/ppermute | solution.py:40
  32.8 0.4 copy-done.16
  33.4 8.4 %attention.3 = (bf16[2,2,256,128]{3,2,1,0:T(8,128)(2,1)S(1)}, bf16[2,2,256,128]{3,2,1,0:T(8,128)(2,1)S(1)}, bf16[2,2,256,128]{3,2,1,0:T(8,128)(2,1)S(1)}, bf16[2...) custom-call(f32[2,3,8,256]{3,2,1,0:T(8,128)S(1)} %fusion.18.bias_ref, ...), custom_call_target="tpu_custom_call" | custom-call | flops 2415919104 | bytes 3670016 | tf_op jit(solution)/shard_map/attention/pallas_call | solution.py:177
  41.8 0.3 collective-permute-done.11.par_q
  42.5 0.5 collective-permute-start.14
  43.0 2.0 %collective-permute-done.14.rel_b = bf16[3,2,256,128]{3,2,1,0:T(8,128)(2,1)S(1)} collective-permute-done((bf16[3,2,256,128]{3,2,1,0:T(8,128)(2,1)S(1)}, bf16[3,2,256,128]{3,2,1,0:T(8,128)(2,1)S(1)}, u32[]{:S(2)}, u32[]{:S(2)}) %collective-permute-start.14) | collective-permute-done | bytes 393248 | tf_op jit(solution)/shard_map/ppermute | solution.py:40
  45.1 1.5 %collective-permute-start.16 = (bf16[2,2,256,128]{3,2,1,0:T(8,128)(2,1)S(1)}, bf16[2,2,256,128]{3,2,1,0:T(8,128)(2,1)S(1)}, u32[]{:S(2)}, u32[]{:S(2)}) collective-permute-start(bf16[2,2,256,128]{3,2,1,0:T(8,128)(2,1)S(1)} %get-tuple-element.138), channel_id=1, source_target_pairs={{0,4},{4,0},{8,12},{12,8},{1,5},{5,1},{9,13},{13,9},{2,6},{6,2},{1... | collective-permute-start | bytes 786440 | tf_op jit(solution)/shard_map/ppermute | solution.py:27
  46.8 0.6 collective-permute-start.15
  47.3 8.6 %attention.4 = (bf16[2,2,256,128]{3,2,1,0:T(8,128)(2,1)S(1)}, bf16[2,2,256,128]{3,2,1,0:T(8,128)(2,1)S(1)}, bf16[2,2,256,128]{3,2,1,0:T(8,128)(2,1)S(1)}, bf16[2...) custom-call(f32[2,3,8,256]{3,2,1,0:T(8,128)S(1)} %fusion.18.bias_ref, ...), custom_call_target="tpu_custom_call" | custom-call | flops 2415919104 | bytes 3670016 | tf_op jit(solution)/shard_map/attention/pallas_call | solution.py:177
  56.2 0.5 copy-done.10
  56.6 0.8 pad_maximum_fusion.6
  57.5 0.4 collective-permute-start.21
  58.1 0.8 fusion.4
  58.9 1.5 %collective-permute-start.19 = (bf16[2,2,256,128]{3,2,1,0:T(8,128)(2,1)}, bf16[2,2,256,128]{3,2,1,0:T(8,128)(2,1)}, u32[]{:S(2)}, u32[]{:S(2)}) collective-permute-start(bf16[2,2,256,128]{3,2,1,0:T(8,128)(2,1)} %get-tuple-element.208), channel_id=1, source_target_pairs={{0,8},{4,12},{8,0},{12,4},{1,9},{5,13},{9,1},{13,5},{2,10},{6,14},... | collective-permute-start | bytes 786440 | tf_op jit(solution)/shard_map/ppermute | solution.py:36
  60.5 0.5 collective-permute-start.23
  61.0 4.8 %attention.5 = (bf16[1,2,256,128]{3,2,1,0:T(8,128)(2,1)S(1)}, bf16[1,2,256,128]{3,2,1,0:T(8,128)(2,1)S(1)}, bf16[1,2,256,128]{3,2,1,0:T(8,128)(2,1)S(1)}, bf16[1...) custom-call(f32[2,3,8,256]{3,2,1,0:T(8,128)S(1)} %fusion.18.bias_ref, ...), custom_call_target="tpu_custom_call" | custom-call | flops 1207959552 | bytes 1835008 | tf_op jit(solution)/shard_map/attention/pallas_call | solution.py:177
  65.8 5.8 %collective-permute-done.21 = bf16[4,2,256,128]{3,2,1,0:T(8,128)(2,1)S(1)} collective-permute-done((bf16[4,2,256,128]{3,2,1,0:T(8,128)(2,1)}, bf16[4,2,256,128]{3,2,1,0:T(8,128)(2,1)S(1)}, u32[]{:S(2)}, u32[]{:S(2)}) %collective-permute-start.21) | collective-permute-done | bytes 524320 | tf_op jit(solution)/shard_map/ppermute | solution.py:27
  71.6 1.1 %fusion.7 = bf16[2,2,256,128]{3,2,1,0:T(8,128)(2,1)S(1)} fusion(bf16[2,2,256,128]{3,2,1,0:T(8,128)(2,1)} %collective-permute-done.19, bf16[2,2,256,128]{3,2,1,0:T(8,128)(2,1)S(1)} %get-tuple-element.163, bf16[2,2,2,256,128]{4,3,2,1,0:T(8,128)(2,1)} %collective-permute-done.20), kind=kLoop, calls=%fused_computation.29 | loop fusion | flops 786432 | bytes 1048576 | tf_op jit(solution)/shard_map/convert_element_type | solution.py:268
  72.8 0.3 collective-permute-done.22
  73.4 1.6 %collective-permute-start.24 = (bf16[1,2,256,128]{3,2,1,0:T(8,128)(2,1)S(1)}, bf16[1,2,256,128]{3,2,1,0:T(8,128)(2,1)S(1)}, u32[]{:S(2)}, u32[]{:S(2)}) collective-permute-start(bf16[1,2,256,128]{3,2,1,0:T(8,128)(2,1)S(1)} %get-tuple-element.172), channel_id=1, source_target_pairs={{0,8},{4,12},{8,0},{12,4},{1,9},{5,13},{9,1},{13,5},{2,10},{6,14},... | collective-permute-start | bytes 393224 | tf_op jit(solution)/shard_map/ppermute | solution.py:36
  75.0 1.5 %collective-permute-start.28 = (bf16[3,2,256,128]{3,2,1,0:T(8,128)(2,1)S(1)}, bf16[3,2,256,128]{3,2,1,0:T(8,128)(2,1)S(1)}, u32[]{:S(2)}, u32[]{:S(2)}) collective-permute-start(bf16[3,2,256,128]{3,2,1,0:T(8,128)(2,1)S(1)} %pad_maximum_fusion.7), channel_id=1, source_target_pairs={{0,4},{4,0},{8,12},{12,8},{1,5},{5,1},{9,13},{13,9},{2,6},{6,2},{1... | collective-permute-start | bytes 1179656 | tf_op jit(solution)/shard_map/ppermute | solution.py:27
  76.6 2.3 %collective-permute-done.24 = bf16[1,2,256,128]{3,2,1,0:T(8,128)(2,1)S(1)} collective-permute-done((bf16[1,2,256,128]{3,2,1,0:T(8,128)(2,1)S(1)}, bf16[1,2,256,128]{3,2,1,0:T(8,128)(2,1)S(1)}, u32[]{:S(2)}, u32[]{:S(2)}) %collective-permute-start.24) | collective-permute-done | bytes 131104 | tf_op jit(solution)/shard_map/ppermute | solution.py:36
  78.9 1.2 %collective-permute-start.26 = (bf16[1,2,256,128]{3,2,1,0:T(8,128)(2,1)S(1)}, bf16[1,2,256,128]{3,2,1,0:T(8,128)(2,1)S(1)}, u32[]{:S(2)}, u32[]{:S(2)}) collective-permute-start(bf16[1,2,256,128]{3,2,1,0:T(8,128)(2,1)S(1)} %fusion.16), channel_id=1, source_target_pairs={{0,4},{4,0},{8,12},{12,8},{1,5},{5,1},{9,13},{13,9},{2,6},{6,2},{1... | collective-permute-start | bytes 393224 | tf_op jit(solution)/shard_map/ppermute | solution.py:27
  80.2 1.5 %collective-permute-start.27 = (bf16[3,2,256,128]{3,2,1,0:T(8,128)(2,1)S(1)}, bf16[3,2,256,128]{3,2,1,0:T(8,128)(2,1)S(1)}, u32[]{:S(2)}, u32[]{:S(2)}) collective-permute-start(bf16[3,2,256,128]{3,2,1,0:T(8,128)(2,1)S(1)} %pad_maximum_fusion.8), channel_id=1, source_target_pairs={{0,8},{4,12},{8,0},{12,4},{1,9},{5,13},{9,1},{13,5},{2,10},{6,14},... | collective-permute-start | bytes 1179656 | tf_op jit(solution)/shard_map/ppermute | solution.py:36
  81.7 5.2 %collective-permute-done.28 = bf16[3,2,256,128]{3,2,1,0:T(8,128)(2,1)S(1)} collective-permute-done((bf16[3,2,256,128]{3,2,1,0:T(8,128)(2,1)S(1)}, bf16[3,2,256,128]{3,2,1,0:T(8,128)(2,1)S(1)}, u32[]{:S(2)}, u32[]{:S(2)}) %collective-permute-start.28) | collective-permute-done | bytes 393248 | tf_op jit(solution)/shard_map/ppermute | solution.py:27
  87.3 1.2 %copy_bitcast_fusion.2 = (bf16[4,8,8,1280]{3,2,1,0:T(8,128)(2,1)}, bf16[4,8,8,1280]{3,2,1,0:T(8,128)(2,1)}) fusion(bf16[1,4,8,8,10,128]{5,3,2,1,0,4:T(8,128)(2,1)S(1)} %get-tuple-element.201, bf16[1,4,8,8,10,128]{5,3,2,1,0,4:T(8,128)(2,1)S(1)} %get-tuple-element.202), kind=kLoop, calls=%fused_computation.10 | loop fusion | bytes 2621440 | tf_op jit(solution)/shard_map/squeeze | solution.py:316
  88.5 0.8 collective-permute-done.26
  89.3 0.4 collective-permute-done.27
  89.7 1.1 %fusion.1 = bf16[2,2,256,128]{3,2,1,0:T(8,128)(2,1)S(1)} fusion(bf16[2,2,256,128]{3,2,1,0:T(8,128)(2,1)S(1)} %get-tuple-element.193, bf16[3,2,256,128]{3,2,1,0:T(8,128)(2,1)S(1)} %collective-permute-done.27, bf16[2,2,2,256,128]{4,3,2,1,0:T(8,128)(2,1)} %collective-permute-done.20), kind=kLoop, calls=%fused_computation.19 | loop fusion | flops 786432 | bytes 1048576 | tf_op jit(solution)/shard_map/convert_element_type | solution.py:322
  91.3 0.9 %copy.26 = bf16[1,4,8,8,10,128]{5,3,4,2,1,0:T(8,128)(2,1)} copy(bf16[1,4,8,8,10,128]{5,3,2,1,0,4:T(8,128)(2,1)S(1)} %get-tuple-element.197) | data formatting | bytes 1310720 | tf_op jit(solution)/shard_map/slice | solution.py:316
  92.3 0.9 %copy.27 = bf16[1,4,8,8,10,128]{5,3,4,2,1,0:T(8,128)(2,1)} copy(bf16[1,4,8,8,10,128]{5,3,2,1,0,4:T(8,128)(2,1)S(1)} %get-tuple-element.198) | data formatting | bytes 1310720 | tf_op jit(solution)/shard_map/slice | solution.py:316
  (95 shorter events, 4.2 us)
Async XLA Ops:
  2.4 3.2 %copy-start.13 = (s32[1,2,2]{2,1,0:T(2,128)S(1)}, s32[1,2,2]{2,1,0:T(2,128)}, u32[]{:S(2)}) copy-start(s32[1,2,2]{2,1,0:T(2,128)} %param.10) | copy-start | bytes 52
  2.4 6.9 %copy-start.2 = (bf16[4,8,8,1280]{3,2,1,0:T(8,128)(2,1)S(1)}, bf16[4,8,8,1280]{3,2,1,0:T(8,128)(2,1)}, u32[]{:S(2)}) copy-start(bf16[4,8,8,1280]{3,2,1,0:T(8,128)(2,1)} %param.9) | copy-start | bytes 1966084
  2.5 8.0 %copy-start = (bf16[5,2,256,128]{3,2,1,0:T(8,128)(2,1)}, bf16[5,2,256,128]{3,2,1,0:T(8,128)(2,1)S(1)}, u32[]{:S(2)}) copy-start(bf16[5,2,256,128]{3,2,1,0:T(8,128)(2,1)S(1)} %constant_dynamic-slice_fusion.3.own_a) | copy-start | bytes 1966084
  2.5 26.8 %collective-permute-start.6 = (bf16[5,2,256,128]{3,2,1,0:T(8,128)(2,1)S(1)}, bf16[5,2,256,128]{3,2,1,0:T(8,128)(2,1)}, u32[]{:S(2)}, u32[]{:S(2)}) collective-permute-start(bf16[5,2,256,128]{3,2,1,0:T(8,128)(2,1)S(1)} %constant_dynamic-slice_fusion.3.own_a), channel_id=1, source_target_pairs={{0,16},{16,0},{1,17},{17,1},{2,18},{18,2},{3,19},{19,3},{4,20},{20... | collective-permute-start | bytes 1966088 | tf_op jit(solution)/shard_map/ppermute | solution.py:40
  3.0 26.3 %collective-permute-start.3 = (bf16[5,2,256,128]{3,2,1,0:T(8,128)(2,1)S(1)}, bf16[5,2,256,128]{3,2,1,0:T(8,128)(2,1)}, u32[]{:S(2)}, u32[]{:S(2)}) collective-permute-start(bf16[5,2,256,128]{3,2,1,0:T(8,128)(2,1)S(1)} %constant_dynamic-slice_fusion.3.own_a), channel_id=1, source_target_pairs={{0,8},{4,12},{8,0},{12,4},{1,9},{5,13},{9,1},{13,5},{2,10},{6,14},... | collective-permute-start | bytes 1966088 | tf_op jit(solution)/shard_map/ppermute | solution.py:36
  5.6 11.4 %collective-permute-start.5 = (s32[2,2]{1,0:T(2,128)S(1)}, s32[2,2]{1,0:T(2,128)S(1)}, u32[]{:S(2)}, u32[]{:S(2)}) collective-permute-start(s32[2,2]{1,0:T(2,128)S(1)} %bitcast.104), channel_id=1, source_target_pairs={{0,4},{4,0},{8,12},{12,8},{1,5},{5,1},{9,13},{13,9},{2,6},{6,2},{1... | collective-permute-start | bytes 56 | tf_op jit(solution)/shard_map/ppermute | solution.py:27
  7.2 9.4 %collective-permute-start = (bf16[2,2,256,128]{3,2,1,0:T(8,128)(2,1)S(1)}, bf16[2,2,256,128]{3,2,1,0:T(8,128)(2,1)}, u32[]{:S(2)}, u32[]{:S(2)}) collective-permute-start(bf16[2,2,256,128]{3,2,1,0:T(8,128)(2,1)S(1)} %constant_dynamic-slice_fusion), channel_id=1, source_target_pairs={{0,4},{4,0},{8,12},{12,8},{1,5},{5,1},{9,13},{13,9},{2,6},{6,2},{1... | collective-permute-start | bytes 786440 | tf_op jit(solution)/shard_map/ppermute | solution.py:27
  7.8 17.0 %collective-permute-start.4 = (bf16[3,2,256,128]{3,2,1,0:T(8,128)(2,1)S(1)}, bf16[3,2,256,128]{3,2,1,0:T(8,128)(2,1)S(1)}, u32[]{:S(2)}, u32[]{:S(2)}) collective-permute-start(bf16[3,2,256,128]{3,2,1,0:T(8,128)(2,1)S(1)} %constant_dynamic-slice_fusion.5), channel_id=1, source_target_pairs={{0,4},{4,0},{8,12},{12,8},{1,5},{5,1},{9,13},{13,9},{2,6},{6,2},{1... | collective-permute-start | bytes 1179656 | tf_op jit(solution)/shard_map/ppermute | solution.py:27
  10.9 6.6 %copy-start.12 = (s32[2,3]{1,0:T(2,128)S(1)}, s32[2,3]{1,0:T(2,128)}, u32[]{:S(2)}) copy-start(s32[2,3]{1,0:T(2,128)} %constant.49.clone) | copy-start | bytes 76
  16.5 12.8 %collective-permute-start.2 = (bf16[2,2,256,128]{3,2,1,0:T(8,128)(2,1)S(1)}, bf16[2,2,256,128]{3,2,1,0:T(8,128)(2,1)S(1)}, u32[]{:S(2)}, u32[]{:S(2)}) collective-permute-start(bf16[2,2,256,128]{3,2,1,0:T(8,128)(2,1)S(1)} %constant_dynamic-slice_fusion.1), channel_id=1, source_target_pairs={{0,4},{4,0},{8,12},{12,8},{1,5},{5,1},{9,13},{13,9},{2,6},{6,2},{1... | collective-permute-start | bytes 786440 | tf_op jit(solution)/shard_map/ppermute | solution.py:27
  17.1 12.3 %collective-permute-start.1 = (bf16[2,2,256,128]{3,2,1,0:T(8,128)(2,1)}, bf16[2,2,256,128]{3,2,1,0:T(8,128)(2,1)S(1)}, u32[]{:S(2)}, u32[]{:S(2)}) collective-permute-start(bf16[2,2,256,128]{3,2,1,0:T(8,128)(2,1)} %collective-permute-done.par_a), channel_id=1, source_target_pairs={{0,8},{4,12},{8,0},{12,4},{1,9},{5,13},{9,1},{13,5},{2,10},{6,14},... | collective-permute-start | bytes 786440 | tf_op jit(solution)/shard_map/ppermute | solution.py:36
  24.8 17.0 %copy-start.6 = (bf16[3,2,256,128]{3,2,1,0:T(8,128)(2,1)}, bf16[3,2,256,128]{3,2,1,0:T(8,128)(2,1)S(1)}, u32[]{:S(2)}) copy-start(bf16[3,2,256,128]{3,2,1,0:T(8,128)(2,1)S(1)} %collective-permute-done.4.par_a) | copy-start | bytes 1179652
  29.4 3.5 %copy-start.14 = (bf16[2,2,256,128]{3,2,1,0:T(8,128)(2,1)}, bf16[2,2,256,128]{3,2,1,0:T(8,128)(2,1)S(1)}, u32[]{:S(2)}) copy-start(bf16[2,2,256,128]{3,2,1,0:T(8,128)(2,1)S(1)} %collective-permute-done.2.par_q) | copy-start | bytes 786436
  29.4 3.4 %copy-start.15 = (bf16[2,2,256,128]{3,2,1,0:T(8,128)(2,1)}, bf16[2,2,256,128]{3,2,1,0:T(8,128)(2,1)S(1)}, u32[]{:S(2)}) copy-start(bf16[2,2,256,128]{3,2,1,0:T(8,128)(2,1)S(1)} %collective-permute-done.1.rel_a) | copy-start | bytes 786436
  29.4 3.1 %collective-permute-start.9 = (bf16[5,2,256,128]{3,2,1,0:T(8,128)(2,1)}, bf16[5,2,256,128]{3,2,1,0:T(8,128)(2,1)S(1)}, u32[]{:S(2)}, u32[]{:S(2)}) collective-permute-start(bf16[5,2,256,128]{3,2,1,0:T(8,128)(2,1)} %collective-permute-done.3.yown_a), channel_id=1, source_target_pairs={{0,16},{16,0},{1,17},{17,1},{2,18},{18,2},{3,19},{19,3},{4,20},{20... | collective-permute-start | bytes 1966088 | tf_op jit(solution)/shard_map/ppermute | solution.py:40
  29.6 3.0 %collective-permute-start.8 = (bf16[2,2,256,128]{3,2,1,0:T(8,128)(2,1)}, bf16[2,2,256,128]{3,2,1,0:T(8,128)(2,1)S(1)}, u32[]{:S(2)}, u32[]{:S(2)}) collective-permute-start(bf16[2,2,256,128]{3,2,1,0:T(8,128)(2,1)} %collective-permute-done.par_a), channel_id=1, source_target_pairs={{0,16},{16,0},{1,17},{17,1},{2,18},{18,2},{3,19},{19,3},{4,20},{20... | collective-permute-start | bytes 786440 | tf_op jit(solution)/shard_map/ppermute | solution.py:40
  30.0 2.5 %collective-permute-start.7 = (bf16[2,2,256,128]{3,2,1,0:T(8,128)(2,1)S(1)}, bf16[2,2,256,128]{3,2,1,0:T(8,128)(2,1)S(1)}, u32[]{:S(2)}, u32[]{:S(2)}) collective-permute-start(bf16[2,2,256,128]{3,2,1,0:T(8,128)(2,1)S(1)} %collective-permute-done.1.rel_a), channel_id=1, source_target_pairs={{0,16},{16,0},{1,17},{17,1},{2,18},{18,2},{3,19},{19,3},{4,20},{20... | collective-permute-start | bytes 786440 | tf_op jit(solution)/shard_map/ppermute | solution.py:40
  30.6 11.5 %collective-permute-start.11 = (bf16[3,2,256,128]{3,2,1,0:T(8,128)(2,1)S(1)}, bf16[3,2,256,128]{3,2,1,0:T(8,128)(2,1)S(1)}, u32[]{:S(2)}, u32[]{:S(2)}) collective-permute-start(bf16[3,2,256,128]{3,2,1,0:T(8,128)(2,1)S(1)} %constant_dynamic-slice_fusion.4), channel_id=1, source_target_pairs={{0,4},{4,0},{8,12},{12,8},{1,5},{5,1},{9,13},{13,9},{2,6},{6,2},{1... | collective-permute-start | bytes 1179656 | tf_op jit(solution)/shard_map/ppermute | solution.py:27
  31.3 11.2 %collective-permute-start.10 = (bf16[3,2,256,128]{3,2,1,0:T(8,128)(2,1)S(1)}, bf16[3,2,256,128]{3,2,1,0:T(8,128)(2,1)S(1)}, u32[]{:S(2)}, u32[]{:S(2)}) collective-permute-start(bf16[3,2,256,128]{3,2,1,0:T(8,128)(2,1)S(1)} %collective-permute-done.4.par_a), channel_id=1, source_target_pairs={{0,8},{4,12},{8,0},{12,4},{1,9},{5,13},{9,1},{13,5},{2,10},{6,14},... | collective-permute-start | bytes 1179656 | tf_op jit(solution)/shard_map/ppermute | solution.py:36
  32.5 0.7 copy-start.16
  32.5 0.9 copy-start.3
  32.5 9.9 %collective-permute-start.12 = (bf16[3,2,256,128]{3,2,1,0:T(8,128)(2,1)S(1)}, bf16[3,2,256,128]{3,2,1,0:T(8,128)(2,1)S(1)}, u32[]{:S(2)}, u32[]{:S(2)}) collective-permute-start(bf16[3,2,256,128]{3,2,1,0:T(8,128)(2,1)S(1)} %collective-permute-done.4.par_a), channel_id=1, source_target_pairs={{0,16},{16,0},{1,17},{17,1},{2,18},{18,2},{3,19},{19,3},{4,20},{20... | collective-permute-start | bytes 1179656 | tf_op jit(solution)/shard_map/ppermute | solution.py:40
  42.2 5.2 %copy-start.7 = (bf16[3,2,256,128]{3,2,1,0:T(8,128)(2,1)}, bf16[3,2,256,128]{3,2,1,0:T(8,128)(2,1)S(1)}, u32[]{:S(2)}) copy-start(bf16[3,2,256,128]{3,2,1,0:T(8,128)(2,1)S(1)} %collective-permute-done.11.par_q) | copy-start | bytes 1179652
  42.4 4.9 %copy-start.8 = (bf16[3,2,256,128]{3,2,1,0:T(8,128)(2,1)}, bf16[3,2,256,128]{3,2,1,0:T(8,128)(2,1)S(1)}, u32[]{:S(2)}) copy-start(bf16[3,2,256,128]{3,2,1,0:T(8,128)(2,1)S(1)} %collective-permute-done.10.rel_a) | copy-start | bytes 1179652
  42.4 4.9 %copy-start.9 = (bf16[3,2,256,128]{3,2,1,0:T(8,128)(2,1)}, bf16[3,2,256,128]{3,2,1,0:T(8,128)(2,1)S(1)}, u32[]{:S(2)}) copy-start(bf16[3,2,256,128]{3,2,1,0:T(8,128)(2,1)S(1)} %collective-permute-done.12.par_b) | copy-start | bytes 1179652
  42.4 2.5 %collective-permute-start.13 = (bf16[2,2,2,256,128]{4,3,2,1,0:T(8,128)(2,1)S(1)}, bf16[2,2,2,256,128]{4,3,2,1,0:T(8,128)(2,1)S(1)}, u32[]{:S(2)}, u32[]{:S(2)}) collective-permute-start(bf16[2,2,2,256,128]{4,3,2,1,0:T(8,128)(2,1)S(1)} %get-tuple-element.126), channel_id=1, source_target_pairs={{0,16},{16,0},{1,17},{17,1},{2,18},{18,2},{3,19},{19,3},{4,20},{20... | collective-permute-start | bytes 1572872 | tf_op jit(solution)/shard_map/ppermute | solution.py:40
  42.5 2.5 %collective-permute-start.14 = (bf16[3,2,256,128]{3,2,1,0:T(8,128)(2,1)S(1)}, bf16[3,2,256,128]{3,2,1,0:T(8,128)(2,1)S(1)}, u32[]{:S(2)}, u32[]{:S(2)}) collective-permute-start(bf16[3,2,256,128]{3,2,1,0:T(8,128)(2,1)S(1)} %collective-permute-done.10.rel_a), channel_id=1, source_target_pairs={{0,16},{16,0},{1,17},{17,1},{2,18},{18,2},{3,19},{19,3},{4,20},{20... | collective-permute-start | bytes 1179656 | tf_op jit(solution)/shard_map/ppermute | solution.py:40
  45.0 11.0 %collective-permute-start.17 = (bf16[2,2,2,256,128]{4,3,2,1,0:T(8,128)(2,1)S(1)}, bf16[2,2,2,256,128]{4,3,2,1,0:T(8,128)(2,1)S(1)}, u32[]{:S(2)}, u32[]{:S(2)}) collective-permute-start(bf16[2,2,2,256,128]{4,3,2,1,0:T(8,128)(2,1)S(1)} %get-tuple-element.140), channel_id=1, source_target_pairs={{0,16},{16,0},{1,17},{17,1},{2,18},{18,2},{3,19},{19,3},{4,20},{20... | collective-permute-start | bytes 1572872 | tf_op jit(solution)/shard_map/ppermute | solution.py:40
  45.1 10.8 %collective-permute-start.16 = (bf16[2,2,256,128]{3,2,1,0:T(8,128)(2,1)S(1)}, bf16[2,2,256,128]{3,2,1,0:T(8,128)(2,1)S(1)}, u32[]{:S(2)}, u32[]{:S(2)}) collective-permute-start(bf16[2,2,256,128]{3,2,1,0:T(8,128)(2,1)S(1)} %get-tuple-element.138), channel_id=1, source_target_pairs={{0,4},{4,0},{8,12},{12,8},{1,5},{5,1},{9,13},{13,9},{2,6},{6,2},{1... | collective-permute-start | bytes 786440 | tf_op jit(solution)/shard_map/ppermute | solution.py:27
  46.8 9.2 %collective-permute-start.15 = (bf16[2,2,256,128]{3,2,1,0:T(8,128)(2,1)S(1)}, bf16[2,2,256,128]{3,2,1,0:T(8,128)(2,1)S(1)}, u32[]{:S(2)}, u32[]{:S(2)}) collective-permute-start(bf16[2,2,256,128]{3,2,1,0:T(8,128)(2,1)S(1)} %get-tuple-element.210), channel_id=1, source_target_pairs={{0,8},{4,12},{8,0},{12,4},{1,9},{5,13},{9,1},{13,5},{2,10},{6,14},... | collective-permute-start | bytes 786440 | tf_op jit(solution)/shard_map/ppermute | solution.py:36
  55.9 0.7 copy-start.10
  56.0 3.0 %copy-start.4 = (bf16[2,2,2,256,128]{4,3,2,1,0:T(8,128)(2,1)}, bf16[2,2,2,256,128]{4,3,2,1,0:T(8,128)(2,1)S(1)}, u32[]{:S(2)}) copy-start(bf16[2,2,2,256,128]{4,3,2,1,0:T(8,128)(2,1)S(1)} %collective-permute-done.17) | copy-start | bytes 1572868
  56.0 2.0 %collective-permute-start.18 = (bf16[2,2,2,256,128]{4,3,2,1,0:T(8,128)(2,1)S(1)}, bf16[2,2,2,256,128]{4,3,2,1,0:T(8,128)(2,1)S(1)}, u32[]{:S(2)}, u32[]{:S(2)}) collective-permute-start(bf16[2,2,2,256,128]{4,3,2,1,0:T(8,128)(2,1)S(1)} %get-tuple-element.143), channel_id=1, source_target_pairs={{0,16},{16,0},{1,17},{17,1},{2,18},{18,2},{3,19},{19,3},{4,20},{20... | collective-permute-start | bytes 1572872 | tf_op jit(solution)/shard_map/ppermute | solution.py:40
  57.5 14.1 %collective-permute-start.21 = (bf16[4,2,256,128]{3,2,1,0:T(8,128)(2,1)}, bf16[4,2,256,128]{3,2,1,0:T(8,128)(2,1)S(1)}, u32[]{:S(2)}, u32[]{:S(2)}) collective-permute-start(bf16[4,2,256,128]{3,2,1,0:T(8,128)(2,1)} %pad_maximum_fusion.6), channel_id=1, source_target_pairs={{0,4},{4,0},{8,12},{12,8},{1,5},{5,1},{9,13},{13,9},{2,6},{6,2},{1... | collective-permute-start | bytes 1572872 | tf_op jit(solution)/shard_map/ppermute | solution.py:27
  58.0 13.6 %collective-permute-start.20 = (bf16[2,2,2,256,128]{4,3,2,1,0:T(8,128)(2,1)S(1)}, bf16[2,2,2,256,128]{4,3,2,1,0:T(8,128)(2,1)}, u32[]{:S(2)}, u32[]{:S(2)}) collective-permute-start(bf16[2,2,2,256,128]{4,3,2,1,0:T(8,128)(2,1)S(1)} %get-tuple-element.150), channel_id=1, source_target_pairs={{0,16},{16,0},{1,17},{17,1},{2,18},{18,2},{3,19},{19,3},{4,20},{20... | collective-permute-start | bytes 1572872 | tf_op jit(solution)/shard_map/ppermute | solution.py:40
  58.9 12.6 %collective-permute-start.19 = (bf16[2,2,256,128]{3,2,1,0:T(8,128)(2,1)}, bf16[2,2,256,128]{3,2,1,0:T(8,128)(2,1)}, u32[]{:S(2)}, u32[]{:S(2)}) collective-permute-start(bf16[2,2,256,128]{3,2,1,0:T(8,128)(2,1)} %get-tuple-element.208), channel_id=1, source_target_pairs={{0,8},{4,12},{8,0},{12,4},{1,9},{5,13},{9,1},{13,5},{2,10},{6,14},... | collective-permute-start | bytes 786440 | tf_op jit(solution)/shard_map/ppermute | solution.py:36
  60.5 12.9 %collective-permute-start.23 = (bf16[2,2,256,128]{3,2,1,0:T(8,128)(2,1)S(1)}, bf16[2,2,256,128]{3,2,1,0:T(8,128)(2,1)S(1)}, u32[]{:S(2)}, u32[]{:S(2)}) collective-permute-start(bf16[2,2,256,128]{3,2,1,0:T(8,128)(2,1)S(1)} %get-tuple-element.170), channel_id=1, source_target_pairs={{0,8},{4,12},{8,0},{12,4},{1,9},{5,13},{9,1},{13,5},{2,10},{6,14},... | collective-permute-start | bytes 786440 | tf_op jit(solution)/shard_map/ppermute | solution.py:36
  71.6 1.5 %collective-permute-start.22 = (bf16[2,1,2,256,128]{4,3,2,1,0:T(8,128)(2,1)S(1)}, bf16[2,1,2,256,128]{4,3,2,1,0:T(8,128)(2,1)S(1)}, u32[]{:S(2)}, u32[]{:S(2)}) collective-permute-start(bf16[2,1,2,256,128]{4,3,2,1,0:T(8,128)(2,1)S(1)} %get-tuple-element.159), channel_id=1, source_target_pairs={{0,16},{16,0},{1,17},{17,1},{2,18},{18,2},{3,19},{19,3},{4,20},{20... | collective-permute-start | bytes 786440 | tf_op jit(solution)/shard_map/ppermute | solution.py:40
  72.7 3.7 %copy-start.5 = (bf16[2,2,2,256,128]{4,3,2,1,0:T(8,128)(2,1)S(1)}, bf16[2,2,2,256,128]{4,3,2,1,0:T(8,128)(2,1)}, u32[]{:S(2)}) copy-start(bf16[2,2,2,256,128]{4,3,2,1,0:T(8,128)(2,1)} %copy-done.4) | copy-start | bytes 1572868
  73.4 5.5 %collective-permute-start.24 = (bf16[1,2,256,128]{3,2,1,0:T(8,128)(2,1)S(1)}, bf16[1,2,256,128]{3,2,1,0:T(8,128)(2,1)S(1)}, u32[]{:S(2)}, u32[]{:S(2)}) collective-permute-start(bf16[1,2,256,128]{3,2,1,0:T(8,128)(2,1)S(1)} %get-tuple-element.172), channel_id=1, source_target_pairs={{0,8},{4,12},{8,0},{12,4},{1,9},{5,13},{9,1},{13,5},{2,10},{6,14},... | collective-permute-start | bytes 393224 | tf_op jit(solution)/shard_map/ppermute | solution.py:36
  75.0 3.9 %collective-permute-start.25 = (bf16[2,1,2,256,128]{4,3,2,1,0:T(8,128)(2,1)S(1)}, bf16[2,1,2,256,128]{4,3,2,1,0:T(8,128)(2,1)S(1)}, u32[]{:S(2)}, u32[]{:S(2)}) collective-permute-start(bf16[2,1,2,256,128]{4,3,2,1,0:T(8,128)(2,1)S(1)} %get-tuple-element.174), channel_id=1, source_target_pairs={{0,16},{16,0},{1,17},{17,1},{2,18},{18,2},{3,19},{19,3},{4,20},{20... | collective-permute-start | bytes 786440 | tf_op jit(solution)/shard_map/ppermute | solution.py:40
  75.0 11.9 %collective-permute-start.28 = (bf16[3,2,256,128]{3,2,1,0:T(8,128)(2,1)S(1)}, bf16[3,2,256,128]{3,2,1,0:T(8,128)(2,1)S(1)}, u32[]{:S(2)}, u32[]{:S(2)}) collective-permute-start(bf16[3,2,256,128]{3,2,1,0:T(8,128)(2,1)S(1)} %pad_maximum_fusion.7), channel_id=1, source_target_pairs={{0,4},{4,0},{8,12},{12,8},{1,5},{5,1},{9,13},{13,9},{2,6},{6,2},{1... | collective-permute-start | bytes 1179656 | tf_op jit(solution)/shard_map/ppermute | solution.py:27
  76.4 10.4 %copy-start.11 = (bf16[2,2,256,128]{3,2,1,0:T(8,128)(2,1)S(1)}, bf16[2,2,256,128]{3,2,1,0:T(8,128)(2,1)}, u32[]{:S(2)}) copy-start(bf16[2,2,256,128]{3,2,1,0:T(8,128)(2,1)} %copy-done.10) | copy-start | bytes 786436
  78.9 10.4 %collective-permute-start.26 = (bf16[1,2,256,128]{3,2,1,0:T(8,128)(2,1)S(1)}, bf16[1,2,256,128]{3,2,1,0:T(8,128)(2,1)S(1)}, u32[]{:S(2)}, u32[]{:S(2)}) collective-permute-start(bf16[1,2,256,128]{3,2,1,0:T(8,128)(2,1)S(1)} %fusion.16), channel_id=1, source_target_pairs={{0,4},{4,0},{8,12},{12,8},{1,5},{5,1},{9,13},{13,9},{2,6},{6,2},{1... | collective-permute-start | bytes 393224 | tf_op jit(solution)/shard_map/ppermute | solution.py:27
  80.2 9.6 %collective-permute-start.27 = (bf16[3,2,256,128]{3,2,1,0:T(8,128)(2,1)S(1)}, bf16[3,2,256,128]{3,2,1,0:T(8,128)(2,1)S(1)}, u32[]{:S(2)}, u32[]{:S(2)}) collective-permute-start(bf16[3,2,256,128]{3,2,1,0:T(8,128)(2,1)S(1)} %pad_maximum_fusion.8), channel_id=1, source_target_pairs={{0,8},{4,12},{8,0},{12,4},{1,9},{5,13},{9,1},{13,5},{2,10},{6,14},... | collective-permute-start | bytes 1179656 | tf_op jit(solution)/shard_map/ppermute | solution.py:36
  86.9 1.7 %copy-start.1 = (bf16[3,2,256,128]{3,2,1,0:T(8,128)(2,1)}, bf16[3,2,256,128]{3,2,1,0:T(8,128)(2,1)S(1)}, u32[]{:S(2)}) copy-start(bf16[3,2,256,128]{3,2,1,0:T(8,128)(2,1)S(1)} %collective-permute-done.28) | copy-start | bytes 1179652
  88.5 2.3 %slice-start = ((bf16[3,2,256,128]{3,2,1,0:T(8,128)(2,1)}), bf16[2,2,256,128]{3,2,1,0:T(8,128)(2,1)S(1)}, s32[]{:S(2)}) async-start(bf16[3,2,256,128]{3,2,1,0:T(8,128)(2,1)} %copy-done.1), calls=%async_computation | async-start | bytes 524288 | tf_op jit(solution)/shard_map/slice | solution.py:308
